TPU v7x, 32 devices: a whole 2x2x4 slice. The times are simulated.
32 devices in a mesh: seq: 16 (over z, y, x), mp: 2 (over core).
Axes of the slice: x: 2, y: 2, z: 4, core: 2. Of those that a mesh axis runs over, the one named last changes fastest.
Arguments:
- tokens: bfloat16 [2, 6144, 768], P(None, 'seq'), may hold values from -6 to 6
- out_grad: bfloat16 [2, 6144, 768], P(None, 'seq'), may hold values from -6 to 6
- gains: float32 [768, 2], replicated, may hold values from 0.5 to 1.5
- routers: float32 [768, 3], replicated, may hold values from -0.21875 to 0.21875
- light_query_key_value_weight: bfloat16 [768, 3, 768], P(None, None, 'mp'), may hold values from -0.21875 to 0.21875
- light_attention_output_weight: bfloat16 [768, 768], P(None, 'mp'), may hold values from -1.75 to 1.75
- heavy_qkv: bfloat16 [768, 3, 768], P(None, None, 'mp'), may hold values from -0.21875 to 0.21875
- heavy_out: bfloat16 [768, 768], P(None, 'mp'), may hold values from -6 to 6
- light_feedforward_input_weight: bfloat16 [768, 2, 1024], P(None, None, 'mp'), may hold values from -0.21875 to 0.21875
- light_feedforward_output_weight: bfloat16 [768, 1024], P(None, 'mp'), may hold values from -0.1875 to 0.1875
- heavy_mlp_in: bfloat16 [768, 2, 4096], P(None, None, 'mp'), may hold values from -0.21875 to 0.21875
- heavy_mlp_out: bfloat16 [768, 4096], P(None, 'mp'), may hold values from -0.09375 to 0.09375
- routed_queries: int32 [2, 1536], P(None, 'seq'), may hold values from 0 to 6143, as said below
- routed_keys: int32 [2, 1536], P(None, 'seq'), may hold values from 0 to 6143, as said below
- routed_mlp: int32 [2, 1536], P(None, 'seq'), may hold values from 0 to 6143, as said below
- block_counts: int32 [2, 16, 3], P(None, 'seq'), may hold values from 1 to 96, as said below
Outputs:
- mixed: bfloat16 [2, 6144, 768], P(None, 'seq')
- input_grad: float32 [2, 6144, 768], P(None, 'seq')
- light_qkv_grad: float32 [768, 3, 768], P(None, None, 'mp')
- light_out_grad: float32 [768, 768], P(None, 'mp')
- heavy_qkv_grad: float32 [768, 3, 768], P(None, None, 'mp')
- heavy_out_grad: float32 [768, 768], P(None, 'mp')
- light_mlp_in_grad: float32 [768, 2, 1024], P(None, None, 'mp')
- light_mlp_out_grad: float32 [768, 1024], P(None, 'mp')
- heavy_mlp_in_grad: float32 [768, 2, 4096], P(None, None, 'mp')
- heavy_mlp_out_grad: float32 [768, 4096], P(None, 'mp')
- gains_grad: float32 [768, 2], replicated
- routers_grad: float32 [768, 3], replicated
Inputs may be any that keep to these rules, and one draw needn't show every extreme that they name: block_counts[s,b,k] slots of block b of sequence s are used for kind k; in every draw some block of each kind uses all 96 slots and some uses one. `routed_queries`: slots c * 96 to c * 96 + 95 belong to block c, positions c * 384 to c * 384 + 383 of the sequence; used slots hold distinct positions in rising order, unused slots repeat the block's first slot. `routed_keys`: as for routed_queries, with kind 1 of block_counts. `routed_mlp`: as for routed_queries, with kind 2 of block_counts.
All inputs are finite; a program needn't handle non-finite values.
Results may differ from a plain program's by a relative error of at most 0.022.
Values may be sent and summed in bfloat16 or wider, within the bound.
No kernel may reach another device: no remote copies, remote signals or barrier semaphores. Data moves between devices by JAX's collectives and lax.ppermute only.
A program may use at most 512 MiB of HBM per device.

v0:
```python
import math

import jax
import jax.numpy as jnp
from jax import lax
from jax.experimental import pallas as pl
from jax.experimental.pallas import tpu as pltpu
from jax.sharding import PartitionSpec as P

LHD = 96
HHD = 64
WIN = 128
LANES = 128

EPSILON = 1e-06
MASKED = -1e30
MARK = 1e30
EXACT = lax.Precision.HIGHEST
LOW = jnp.bfloat16
WIDE = jnp.float32

ROW_QUERY, ROW_KEY, ROW_MLP, OK_QUERY, OK_KEY, OK_MLP = range(6)


def lanes_of(shape):
    return lax.broadcasted_iota(jnp.int32, shape, len(shape) - 1)


def dot(a, b):
    return jnp.dot(a, b, preferred_element_type=WIDE)


def rows_dot(a, b):
    return lax.dot_general(a, b, (((1,), (1,)), ((), ())), preferred_element_type=WIDE)


def cols_dot(a, b):
    return lax.dot_general(a, b, (((0,), (0,)), ((), ())), preferred_element_type=WIDE)


def rms_of(values):
    return lax.rsqrt(jnp.mean(values * values, axis=-1, keepdims=True) + EPSILON)


def column(values, index):
    return values[:, index : index + 1]


def columns(shape, *parts):
    lane = lanes_of(shape)
    out = jnp.zeros(shape, WIDE)
    for index, part in enumerate(parts):
        out = jnp.where(lane == index, part, out)
    return out


def hot_rows(slots, index, length):
    rows = column(slots, index)
    return (lanes_of((rows.shape[0], length)) == rows).astype(WIDE)


def place_rows(hot, values):
    high = values.astype(LOW)
    rest = (values - high.astype(WIDE)).astype(LOW)
    return cols_dot(hot, high) + cols_dot(hot, rest)


def exact_place(hot, values):
    return lax.dot_general(
        hot, values, (((0,), (0,)), ((), ())), precision=EXACT, preferred_element_type=WIDE
    )


def exact_pick(hot, values):
    return jnp.dot(hot, values, precision=EXACT, preferred_element_type=WIDE)


def row_dots(values, vector):
    return jnp.sum(values * vector, axis=-1, keepdims=True)


def norm_back(values, factor, weighted):
    inner = jnp.mean(weighted * values, axis=-1, keepdims=True)
    return factor * weighted - values * (factor * factor * factor) * inner


def gelu_parts(gate, up, hidden_grad):
    root = math.sqrt(2.0 / math.pi)
    cube = 0.044715 * root
    square = gate * gate
    bend = jnp.tanh(gate * (root + cube * square))
    half = 0.5 + 0.5 * bend
    value = gate * half
    slope = half + gate * (1.0 - bend * bend) * (0.5 * root + (1.5 * cube) * square)
    return value * up, slope * up * hidden_grad, value * hidden_grad


def merge_heads(ref, rows, heads):
    tiles = []
    for head in range(0, heads, 2):
        first = ref[head, :rows, :].astype(WIDE)
        second = ref[head + 1, :rows, :].astype(WIDE)
        lane = lanes_of(first.shape)
        tiles.append(jnp.where(lane < HHD, first, pltpu.roll(second, HHD, 1)))
    return jnp.concatenate(tiles, axis=1)


def merge_upper(ref, rows, heads):
    tiles = []
    for head in range(0, heads, 2):
        first = ref[head, :rows, :].astype(WIDE)
        second = ref[head + 1, :rows, :].astype(WIDE)
        lane = lanes_of(first.shape)
        tiles.append(jnp.where(lane < HHD, pltpu.roll(first, HHD, 1), second))
    return jnp.concatenate(tiles, axis=1)


def head_low(values, head):
    tile = values[:, head // 2 * LANES : (head // 2 + 1) * LANES]
    return tile if head % 2 == 0 else pltpu.roll(tile, HHD, 1)


def head_high(values, head):
    tile = values[:, head // 2 * LANES : (head // 2 + 1) * LANES]
    return tile if head % 2 == 1 else pltpu.roll(tile, HHD, 1)


def fold(values):
    half = values.shape[0] // 2
    lane = lanes_of((half, LANES))
    return jnp.where(lane < HHD, values[:half], pltpu.roll(values[half:], HHD, 1))


def unfold(folded):
    lane = lanes_of(folded.shape)
    return jnp.concatenate(
        [
            jnp.where(lane < HHD, folded, 0.0),
            jnp.where(lane < HHD, pltpu.roll(folded, HHD, 1), 0.0),
        ],
        axis=0,
    )


def merge_folded(ref, start, heads):
    tiles = []
    for head in range(0, heads, 2):
        first = ref[head, start:, :].astype(WIDE)
        second = ref[head + 1, start:, :].astype(WIDE)
        lane = lanes_of(first.shape)
        upper = jnp.where(lane < HHD, first, pltpu.roll(second, HHD, 1))
        lower = jnp.where(lane < HHD, pltpu.roll(first, HHD, 1), second)
        tiles.append(jnp.concatenate([upper, lower], axis=0))
    return jnp.concatenate(tiles, axis=1)


def spread_matrix(heads):
    row = lax.broadcasted_iota(jnp.int32, (heads * LHD, heads * LANES), 0)
    lane = lanes_of((heads * LHD, heads * LANES))
    inner = lane & (LANES - 1)
    hit = (row == (lane >> 7) * LHD + inner) & (inner < LHD)
    return hit.astype(WIDE).astype(LOW)


def params(mib=56):
    return pltpu.CompilerParams(vmem_limit_bytes=mib * 2**20)


def cost(microseconds):
    return pl.CostEstimate(
        flops=int(microseconds * 2e7), bytes_accessed=2**10, transcendentals=0
    )


def whole(array):
    zeros = (0,) * array.ndim
    return pl.BlockSpec(array.shape, lambda *_: zeros, pipeline_mode=pl.Buffered(1))


def each(array):
    rest = (0,) * (array.ndim - 1)
    return pl.BlockSpec((1,) + array.shape[1:], lambda s: (s,) + rest)


def like(shape, kind):
    return jax.ShapeDtypeStruct(shape, kind)


def front_kernel(
    tokens_ref, gains_ref, routers_ref, slots_ref, heavy_ref, low_ref, pair_ref, raw_ref, gate_ref,
):
    inputs = tokens_ref[0].astype(WIDE)
    length = inputs.shape[0]
    normed = inputs * rms_of(inputs) * gains_ref[0:1, :]
    low = normed.astype(LOW)
    low_ref[0] = low
    slots = slots_ref[0]
    hot_query = hot_rows(slots, ROW_QUERY, length)
    hot_key = hot_rows(slots, ROW_KEY, length)
    logits = columns(
        (length, LANES),
        row_dots(normed, routers_ref[0:1, :]),
        row_dots(normed, routers_ref[1:2, :]),
    )
    query_gate = jax.nn.sigmoid(column(exact_pick(hot_query, logits), 0))
    key_gate = jax.nn.sigmoid(column(exact_pick(hot_key, logits), 1))
    gate_ref[0] = columns((slots.shape[0], LANES), query_gate, key_gate)
    query_in = dot(hot_query.astype(LOW), low).astype(LOW)
    key_in = dot(hot_key.astype(LOW), low).astype(LOW)
    query = dot(query_in, heavy_ref[0]).astype(LOW).astype(WIDE)
    key = dot(key_in, heavy_ref[1]).astype(LOW).astype(WIDE)
    raw = dot(key_in, heavy_ref[2])
    raw_ref[0] = raw
    value = (key_gate * raw).astype(LOW).astype(WIDE)
    value = jnp.where(column(slots, OK_KEY) > 0, value, MARK)
    cap = slots.shape[0]
    lane = lanes_of((cap, LANES))
    for head in range(raw.shape[1] // HHD):
        both = jnp.where(lane < HHD, head_low(query, head), head_high(key, head))
        pair_ref[head, :cap, :] = both.astype(LOW)
        pair_ref[head, cap:, :] = fold(head_low(value, head)).astype(LOW)


def front(tokens, gains, routers, slots, heavy, seq_devices):
    seqs, length, width = tokens.shape
    cap = slots.shape[1]
    heavy_cols = heavy.shape[2]
    heads = heavy_cols // HHD
    shapes = [
        like(tokens.shape, LOW),
        like((seq_devices, 3 * cap // 2, LANES), LOW),
        like((seqs, cap, heavy_cols), WIDE),
        like((seqs, cap, LANES), WIDE),
    ]
    specs = [each(s) for s in shapes]
    specs[1] = pl.BlockSpec((heads, 3 * cap // 2, LANES), lambda s: (s, 0, 0))
    return pl.pallas_call(
        front_kernel,
        grid=(seqs,),
        in_specs=[each(tokens), whole(gains), whole(routers), each(slots), whole(heavy)],
        out_specs=specs,
        out_shape=shapes,
        compiler_params=params(),
        cost_estimate=cost(8),
        name="front",
    )(tokens, gains, routers, slots, heavy)


def window_bias(block, length, base, total):
    row = lax.broadcasted_iota(jnp.int32, (WIN, 3 * WIN), 0)
    col = lanes_of((WIN, 3 * WIN))
    place = base + (block - 1) * WIN + col
    near = jnp.abs(col - WIN - row) < WIN
    return jnp.where(near & (place >= 0) & (place < total), 0.0, MASKED)


def light_forward_kernel(
    scale, place_ref, low_ref, before_ref, after_ref, gains_ref, weight_ref, out_ref,
    mix_ref, attn_ref, lse_ref, query_ref, window_ref, wide_ref,
):
    length, heads = low_ref.shape[1], weight_ref.shape[2] // LHD
    spread = spread_matrix(heads)

    def heads_of(rows, kind):
        projected = dot(rows, weight_ref[kind]).astype(LOW)
        return dot(projected, spread).astype(LOW)

    query_ref[0] = heads_of(low_ref[0], 0)
    edges = ((before_ref, slice(0, WIN)), (after_ref, slice(WIN + length, 2 * WIN + length)))
    for ref, rows in edges:
        inputs = ref[0].astype(WIDE)
        low = (inputs * rms_of(inputs) * gains_ref[0:1, :]).astype(LOW)
        for kind in range(2):
            window_ref[0, kind, rows, :] = heads_of(low, 1 + kind)
    for kind in range(2):
        window_ref[0, kind, WIN : WIN + length, :] = heads_of(low_ref[0], 1 + kind)
    for block in range(length // WIN):
        rows = slice(block * WIN, (block + 1) * WIN)
        near = slice(block * WIN, (block + 3) * WIN)
        bias = window_bias(block, length, place_ref[0, 0], place_ref[0, 1])
        lanes = [slice(head * LANES, (head + 1) * LANES) for head in range(heads)]
        scores = jnp.concatenate(
            [
                rows_dot(query_ref[0, rows, at], window_ref[0, 0, near, at]) * scale + bias
                for at in lanes
            ],
            axis=0,
        )
        top = jnp.max(scores, axis=-1, keepdims=True)
        expo = jnp.exp(scores - top)
        total = jnp.sum(expo, axis=-1, keepdims=True)
        lse = top + jnp.log(total)
        share = 1.0 / total
        expo = expo.astype(LOW)
        kept = []
        for head, at in enumerate(lanes):
            mine = slice(head * WIN, (head + 1) * WIN)
            mixed = dot(expo[mine], window_ref[0, 1, near, at]) * share[mine]
            wide_ref[rows, at] = mixed.astype(LOW)
            kept.append(lse[mine])
        lse_ref[0, rows, :] = columns((WIN, LANES), *kept)
    mix = rows_dot(wide_ref[...], spread).astype(LOW)
    mix_ref[0] = mix
    attn_ref[0] = rows_dot(mix, out_ref[...])


def light_forward(place, low, before, after, gains, weight, weight_out):
    seqs, length, _ = low.shape
    light_cols = weight.shape[2]
    heads = light_cols // LHD
    shapes = [
        like((seqs, length, light_cols), LOW),
        like((seqs, length, weight_out.shape[0]), WIDE),
        like((seqs, length, LANES), WIDE),
        like((seqs, length, heads * LANES), LOW),
        like((seqs, 2, length + 2 * WIN, heads * LANES), LOW),
    ]
    return pl.pallas_call(
        lambda *refs: light_forward_kernel(1.0 / math.sqrt(LHD), *refs),
        grid=(seqs,),
        in_specs=[
            pl.BlockSpec(memory_space=pltpu.SMEM),
            each(low),
            each(before),
            each(after),
            whole(gains),
            whole(weight),
            whole(weight_out),
        ],
        out_specs=[each(s) for s in shapes],
        out_shape=shapes,
        scratch_shapes=[pltpu.VMEM((length, heads * LANES), LOW)],
        compiler_params=params(),
        cost_estimate=cost(15),
        name="light_forward",
    )(place, low, before, after, gains, weight, weight_out)


def light_backward_kernel(
    scale, place_ref, query_ref, window_ref, lse_ref, grad_ref, local_ref, early_ref, late_ref, *scratch
):
    wide_ref, dkey_ref, dvalue_ref = scratch
    length, light_cols = grad_ref.shape[1:]
    heads = light_cols // LHD
    spread = spread_matrix(heads)
    grad = dot(grad_ref[0], spread).astype(LOW)
    dkey_ref[...] = jnp.zeros_like(dkey_ref)
    dvalue_ref[...] = jnp.zeros_like(dvalue_ref)
    for block in range(length // WIN):
        rows = slice(block * WIN, (block + 1) * WIN)
        near = slice(block * WIN, (block + 3) * WIN)
        bias = window_bias(block, length, place_ref[0, 0], place_ref[0, 1])
        lse = lse_ref[0, rows, :]
        lanes = [slice(head * LANES, (head + 1) * LANES) for head in range(heads)]
        scores = jnp.concatenate(
            [
                rows_dot(query_ref[0, rows, at], window_ref[0, 0, near, at]) * scale
                + (bias - column(lse, head))
                for head, at in enumerate(lanes)
            ],
            axis=0,
        )
        prob_grad = jnp.concatenate(
            [rows_dot(grad[rows, at], window_ref[0, 1, near, at]) for at in lanes], axis=0
        )
        probs = jnp.exp(scores)
        delta = jnp.sum(probs * prob_grad, axis=-1, keepdims=True)
        score_grad = (probs * (prob_grad - delta)).astype(LOW)
        probs = probs.astype(LOW)
        for head, at in enumerate(lanes):
            mine = slice(head * WIN, (head + 1) * WIN)
            part = score_grad[mine]
            wide_ref[rows, at] = (dot(part, window_ref[0, 0, near, at]) * scale).astype(LOW)
            dkey_ref[near, at] += cols_dot(part, query_ref[0, rows, at]) * scale
            dvalue_ref[near, at] += cols_dot(probs[mine], grad[rows, at])
    local_ref[0, 0] = rows_dot(wide_ref[...], spread).astype(LOW)
    for kind, ref in ((1, dkey_ref), (2, dvalue_ref)):
        all_rows = rows_dot(ref[...].astype(LOW), spread).astype(LOW)
        early_ref[0, kind - 1] = all_rows[:WIN]
        local_ref[0, kind] = all_rows[WIN : WIN + length]
        late_ref[0, kind - 1] = all_rows[WIN + length :]


def light_backward(place, query, window, lse, grad):
    seqs, length, light_cols = grad.shape
    edge = like((seqs, 2, WIN, light_cols), LOW)
    shapes = [like((seqs, 3, length, light_cols), LOW), edge, edge]
    return pl.pallas_call(
        lambda *refs: light_backward_kernel(1.0 / math.sqrt(LHD), *refs),
        grid=(seqs,),
        in_specs=[
            pl.BlockSpec(memory_space=pltpu.SMEM),
            each(query),
            each(window),
            each(lse),
            each(grad),
        ],
        out_specs=[each(s) for s in shapes],
        out_shape=shapes,
        scratch_shapes=[
            pltpu.VMEM(query.shape[1:], LOW),
            pltpu.VMEM(window.shape[2:], WIDE),
            pltpu.VMEM(window.shape[2:], WIDE),
        ],
        compiler_params=params(),
        cost_estimate=cost(14),
        name="light_backward",
    )(place, query, window, lse, grad)


def heavy_forward_kernel(scale, pair_ref, query_ref, key_ref, value_ref, kept_ref, mix_ref):
    devices, rows, _ = pair_ref.shape
    cap = 2 * rows // 3
    tile = kept_ref.shape[0]

    @pl.when(pl.program_id(0) == 0)
    def _():
        def unpack(index, carry):
            lane = lanes_of((cap, LANES))
            at = pl.ds(pl.multiple_of(index * cap, 16), cap)
            both = pair_ref[index, :cap, :].astype(WIDE)
            value = unfold(pair_ref[index, cap:, :].astype(WIDE))
            unused = column(value, 0) > 0.5 * MARK
            bias = jnp.where(unused, MASKED, 0.0)
            query = jnp.where(lane < HHD, both * scale, jnp.where(lane == HHD, 1.0, 0.0))
            key = jnp.where(
                lane < HHD, pltpu.roll(both, HHD, 1), jnp.where(lane == HHD, bias, 0.0)
            )
            query_ref[at, :] = query.astype(LOW)
            key_ref[at, :] = key.astype(LOW)
            value_ref[at, :] = jnp.where(unused, 0.0, value).astype(LOW)
            return carry

        lax.fori_loop(0, devices, unpack, 0, unroll=devices <= 16)

    start = pl.multiple_of(pl.program_id(0) * tile, 16)
    scores = rows_dot(query_ref[pl.ds(start, tile), :], key_ref[...])
    top = jnp.max(scores, axis=-1, keepdims=True)
    expo = jnp.exp(scores - top)
    total = jnp.sum(expo, axis=-1, keepdims=True)
    mix = dot(expo.astype(LOW), value_ref[...]) / total
    lane = lanes_of(mix.shape)
    kept_ref[...] = jnp.where(lane < HHD, mix, top + jnp.log(total))
    for index in range(tile // cap):
        mix_ref[index] = fold(mix[index * cap : (index + 1) * cap]).astype(LOW)


def heavy_backward_kernel(
    scale, query_ref, key_ref, value_ref, kept_ref, grad_ref, triple_ref, dq_ref, dk_ref, dv_ref
):
    step = pl.program_id(0)
    devices, rows, _ = triple_ref.shape
    cap = 2 * rows // 3
    tile = kept_ref.shape[0]

    @pl.when(step == 0)
    def _():
        dk_ref[...] = jnp.zeros_like(dk_ref)
        dv_ref[...] = jnp.zeros_like(dv_ref)

    start = pl.multiple_of(step * tile, 16)
    query = query_ref[pl.ds(start, tile), :]
    grad = jnp.concatenate(
        [unfold(grad_ref[index].astype(WIDE)) for index in range(tile // cap)], axis=0
    )
    kept = kept_ref[...]
    lse = column(kept, HHD)
    delta = jnp.sum(kept * grad, axis=-1, keepdims=True)
    grad = grad.astype(LOW)
    probs = jnp.exp(rows_dot(query, key_ref[...]) - lse)
    prob_grad = rows_dot(grad, value_ref[...])
    score_grad = (probs * (prob_grad - delta)).astype(LOW)
    dq_ref[pl.ds(start, tile), :] = dot(score_grad, key_ref[...]) * scale
    dk_ref[...] += cols_dot(score_grad, query)
    dv_ref[...] += cols_dot(probs.astype(LOW), grad)

    @pl.when(step == pl.num_programs(0) - 1)
    def _():
        def pack(index, carry):
            lane = lanes_of((cap, LANES))
            at = pl.ds(pl.multiple_of(index * cap, 16), cap)
            moved = pltpu.roll(dk_ref[at, :], HHD, 1)
            triple_ref[index, :cap, :] = jnp.where(lane < HHD, dq_ref[at, :], moved).astype(LOW)
            triple_ref[index, cap:, :] = fold(dv_ref[at, :]).astype(LOW)
            return carry

        lax.fori_loop(0, devices, pack, 0, unroll=devices <= 16)


def query_tile(devices, cap):
    return 4 * cap if devices <= 32 else cap


def heavy_forward(pair):
    devices, rows, _ = pair.shape
    cap = 2 * rows // 3
    length, tile = devices * cap, query_tile(devices, cap)
    operand = like((length, LANES), LOW)
    shapes = [operand] * 3 + [
        like((length, LANES), WIDE),
        like((devices, cap // 2, LANES), LOW),
    ]
    return pl.pallas_call(
        lambda *refs: heavy_forward_kernel(1.0 / math.sqrt(HHD), *refs),
        grid=(length // tile,),
        in_specs=[whole(pair)],
        out_specs=[whole(operand)] * 3
        + [
            pl.BlockSpec((tile, LANES), lambda i: (i, 0)),
            pl.BlockSpec((tile // cap, cap // 2, LANES), lambda i: (i, 0, 0)),
        ],
        out_shape=shapes,
        compiler_params=params(60),
        cost_estimate=cost(7),
        name="heavy_forward",
    )(pair)


def heavy_backward(query, key, value, kept, grad):
    devices, half, _ = grad.shape
    cap = 2 * half
    length, tile = devices * cap, query_tile(devices, cap)
    triple = like((devices, cap + half, LANES), LOW)
    return pl.pallas_call(
        lambda *refs: heavy_backward_kernel(1.0 / math.sqrt(HHD), *refs),
        grid=(length // tile,),
        in_specs=[
            whole(query),
            whole(key),
            whole(value),
            pl.BlockSpec((tile, LANES), lambda i: (i, 0)),
            pl.BlockSpec((tile // cap, half, LANES), lambda i: (i, 0, 0)),
        ],
        out_specs=whole(triple),
        out_shape=triple,
        scratch_shapes=[pltpu.VMEM((length, LANES), WIDE)] * 3,
        compiler_params=params(60),
        cost_estimate=cost(10),
        name="heavy_backward",
    )(query, key, value, kept, grad)


def combine_kernel(pairs_ref, attn_ref, out_ref, slots_ref, gate_ref, part_ref, mix_ref):
    slots = slots_ref[0]
    mix = merge_folded(pairs_ref, 0, pairs_ref.shape[0]).astype(LOW)
    mix_ref[0] = mix
    rows = rows_dot(mix, out_ref[...])
    weight = jnp.where(column(slots, OK_QUERY) > 0, column(gate_ref[0], 0), 0.0)
    hot = hot_rows(slots, ROW_QUERY, attn_ref.shape[1]).astype(LOW)
    part_ref[0] = (attn_ref[0] + place_rows(hot, weight * rows)).astype(LOW)


def pair_spec(pairs, heads):
    return pl.BlockSpec((heads,) + pairs.shape[1:], lambda s: (s, 0, 0))


def combine(pairs, attn, weight_out, slots, gate):
    seqs, cap = slots.shape[:2]
    heavy_cols = weight_out.shape[1]
    shapes = [like(attn.shape, LOW), like((seqs, cap, heavy_cols), LOW)]
    return pl.pallas_call(
        combine_kernel,
        grid=(seqs,),
        in_specs=[
            pair_spec(pairs, heavy_cols // HHD),
            each(attn),
            whole(weight_out),
            each(slots),
            each(gate),
        ],
        out_specs=[each(s) for s in shapes],
        out_shape=shapes,
        compiler_params=params(),
        cost_estimate=cost(4),
        name="combine",
    )(pairs, attn, weight_out, slots, gate)


def slots_kernel(
    core_ref, tokens_ref, own_ref, other_ref, up_ref, gains_ref, routers_ref, slots_ref,
    low_ref, rows_ref, slot_ref, ship_ref, gate_ref,
):
    middle = tokens_ref[0].astype(WIDE) + own_ref[0].astype(WIDE) + other_ref[0].astype(WIDE)
    length = middle.shape[0]
    normed = middle * rms_of(middle) * gains_ref[1:2, :]
    low = normed.astype(LOW)
    low_ref[0] = low
    slots = slots_ref[0]
    hot = hot_rows(slots, ROW_MLP, length)
    logits = columns((length, LANES), row_dots(normed, routers_ref[2:3, :]))
    gate = jax.nn.sigmoid(column(exact_pick(hot, logits), 0))
    weight = jnp.where(column(slots, OK_MLP) > 0, gate, 0.0)
    hot = hot.astype(LOW)
    rows = dot(hot, low)
    slot = weight * dot(hot, up_ref[0])
    rows_ref[0] = rows.astype(LOW)
    slot_ref[0] = slot.astype(LOW)
    ship_ref[0] = jnp.where(core_ref[0, 0] == 0, rows, slot).astype(LOW)
    gate_ref[0] = columns((slots.shape[0], LANES), gate, weight)


def mlp_slots(core, tokens, own, other, up, gains, routers, slots):
    seqs, length, width = tokens.shape
    cap = slots.shape[1]
    shapes = [like(tokens.shape, LOW)]
    shapes += [like((seqs, cap, width), LOW)] * 3 + [like((seqs, cap, LANES), WIDE)]
    return pl.pallas_call(
        slots_kernel,
        grid=(seqs,),
        in_specs=[
            pl.BlockSpec(memory_space=pltpu.SMEM),
            each(tokens), each(own), each(other), each(up), whole(gains), whole(routers), each(slots),
        ],
        out_specs=[each(s) for s in shapes],
        out_shape=shapes,
        compiler_params=params(),
        cost_estimate=cost(5),
        name="mlp_slots",
    )(core, tokens, own, other, up, gains, routers, slots)


def pack_wide(ref, value):
    value = value.astype(LOW)
    rows, cols = value.shape[0], ref.shape[1]
    extra = value.shape[1] - cols
    group = rows * extra // cols
    ref[:rows, :] = value[:, :cols]
    for index in range(cols // extra):
        ref[rows:, index * extra : (index + 1) * extra] = value[
            index * group : (index + 1) * group, cols:
        ]


def unpack_wide(store, ref, start, rows, extra):
    cols = ref.shape[1]
    group = rows * extra // cols
    store(slice(0, rows), slice(0, cols), ref[start : start + rows, :])
    for index in range(cols // extra):
        store(
            slice(index * group, (index + 1) * group),
            slice(cols, cols + extra),
            ref[start + rows : start + rows + group, index * extra : (index + 1) * extra],
        )


def feed_kernel(
    low_ref, rows_ref, slot_ref, kept_ref, up_ref, slots_ref, in_ref, out_ref, heavy_in_ref,
    heavy_out_ref, part_ref, weights_ref, gate_ref, heavy_acc, back_acc, hidden_ref, dgate_ref, dup_ref,
):
    step = pl.program_id(0)
    seqs, length, width = up_ref.shape
    cap = slots_ref.shape[1]

    @pl.when(step == 0)
    def _():
        heavy_acc[...] = jnp.zeros_like(heavy_acc)
        back_acc[...] = jnp.zeros_like(back_acc)

    first, second, last = heavy_in_ref[0], heavy_in_ref[1], heavy_out_ref[...]
    rows = rows_ref[...]
    hidden, gate_grad, up_grad = gelu_parts(
        dot(rows, first), dot(rows, second), dot(slot_ref[...], last)
    )
    heavy_acc[...] += rows_dot(hidden.astype(LOW), last)
    back_acc[...] += rows_dot(gate_grad.astype(LOW), first) + rows_dot(up_grad.astype(LOW), second)

    @pl.when(step == pl.num_programs(0) - 1)
    def _():
        for s in range(seqs):
            here = slice(s * length, (s + 1) * length)
            mine = slice(s * cap, (s + 1) * cap)
            low = low_ref[s]
            hidden, gate_grad, up_grad = gelu_parts(
                dot(low, in_ref[0]), dot(low, in_ref[1]), dot(up_ref[s], out_ref[...])
            )
            hidden, gate_grad, up_grad = (
                hidden.astype(LOW),
                gate_grad.astype(LOW),
                up_grad.astype(LOW),
            )
            hidden_ref[here, :] = hidden
            dgate_ref[here, :] = gate_grad
            dup_ref[here, :] = up_grad
            hot = hot_rows(slots_ref[s], ROW_MLP, length).astype(LOW)
            kept = kept_ref[s]
            heavy_rows = heavy_acc[mine, :]
            part_ref[0, s] = (
                rows_dot(hidden, out_ref[...]) + place_rows(hot, column(kept, 1) * heavy_rows)
            ).astype(LOW)
            part_ref[1, s] = (
                rows_dot(gate_grad, in_ref[0])
                + rows_dot(up_grad, in_ref[1])
                + place_rows(hot, back_acc[mine, :])
            ).astype(LOW)
            gate_part = jnp.sum(dot(hot, up_ref[s]) * heavy_rows, axis=-1, keepdims=True)
            gate_ref[s] = columns((cap, LANES), column(kept, 0), gate_part)
        low = low_ref[...].reshape(seqs * length, width)
        up = up_ref[...].reshape(seqs * length, width)
        pack_wide(weights_ref.at[0], cols_dot(low, dgate_ref[...]))
        pack_wide(weights_ref.at[1], cols_dot(low, dup_ref[...]))
        pack_wide(weights_ref.at[2], cols_dot(up, hidden_ref[...]))


def feed(low, rows, slot, kept, up, slots, light_in, light_out, heavy_in, heavy_out, packed_cols):
    seqs, length, width = up.shape
    cap = slots.shape[1]
    hidden = light_out.shape[1]
    cols = 256
    rows, slot = rows.reshape(-1, width), slot.reshape(-1, width)
    shapes = [
        like((2, seqs, length, width), LOW),
        like((3, width * hidden // packed_cols, packed_cols), LOW),
        like((seqs, cap, LANES), WIDE),
    ]
    return pl.pallas_call(
        feed_kernel,
        grid=(heavy_out.shape[1] // cols,),
        in_specs=[
            whole(low),
            whole(rows),
            whole(slot),
            whole(kept),
            whole(up),
            whole(slots),
            whole(light_in),
            whole(light_out),
            pl.BlockSpec((2, width, cols), lambda i: (0, 0, i)),
            pl.BlockSpec((width, cols), lambda i: (0, i)),
        ],
        out_specs=[whole(s) for s in shapes],
        out_shape=shapes,
        scratch_shapes=[pltpu.VMEM((seqs * cap, width), WIDE)] * 2
        + [pltpu.VMEM((seqs * length, hidden), LOW)] * 3,
        compiler_params=params(),
        cost_estimate=cost(20),
        name="feed",
    )(low, rows, slot, kept, up, slots, light_in, light_out, heavy_in, heavy_out)


def middle_kernel(
    tokens_ref, own_ref, other_ref, part_ref, beyond_ref, up_ref, gains_ref, routers_ref, slots_ref,
    gate_ref, mlp_ref, mlp_other_ref, mix_ref, heavy_mix_ref, light_out_ref, heavy_out_ref, down_ref,
    mixed_ref, middle_ref, grad_ref, pair_ref, weights_ref, small_ref, logit_ref, weights_acc,
):
    step = pl.program_id(0)

    @pl.when(step == 0)
    def _():
        weights_acc[...] = jnp.zeros_like(weights_acc)
        small_ref[...] = jnp.zeros_like(small_ref)

    slots = slots_ref[0]
    cap = slots.shape[0]
    middle = tokens_ref[0].astype(WIDE) + own_ref[0].astype(WIDE) + other_ref[0].astype(WIDE)
    length = middle.shape[0]
    factor = rms_of(middle)
    scaled = middle * factor
    normed = scaled * gains_ref[1:2, :]
    mixed = middle + (part_ref[0, 0].astype(WIDE) + beyond_ref[0, 0].astype(WIDE))
    mixed_ref[0] = mixed.astype(LOW)
    gate = column(mlp_ref[0], 0)
    gate_grad = column(mlp_ref[0], 1) + column(mlp_other_ref[0], 1)
    logit_grad = jnp.where(column(slots, OK_MLP) > 0, gate_grad * gate * (1.0 - gate), 0.0)
    token_grad = column(
        exact_place(hot_rows(slots, ROW_MLP, length), columns((cap, LANES), logit_grad)), 0
    )
    normed_grad = (
        part_ref[1, 0].astype(WIDE) + beyond_ref[1, 0].astype(WIDE)
    ) + token_grad * routers_ref[2:3, :]
    small_ref[0:1, :] += jnp.sum(normed_grad * scaled, axis=0, keepdims=True)
    small_ref[1:2, :] += jnp.sum(token_grad * normed, axis=0, keepdims=True)
    middle_grad = up_ref[0].astype(WIDE) + norm_back(middle, factor, normed_grad * gains_ref[1:2, :])
    middle_ref[0] = middle_grad
    low = middle_grad.astype(LOW)
    hot = hot_rows(slots, ROW_QUERY, length).astype(LOW)
    up_rows = dot(hot, low)
    weight = jnp.where(column(slots, OK_QUERY) > 0, column(gate_ref[0], 0), 0.0)
    slot = (weight * up_rows).astype(LOW)
    heavy_rows = rows_dot(heavy_mix_ref[0], heavy_out_ref[...])
    logit_ref[0] = columns(
        (cap, LANES), jnp.sum(up_rows * heavy_rows, axis=-1, keepdims=True)
    )
    mix_grad = dot(slot, heavy_out_ref[...]).astype(LOW).astype(WIDE)
    for head in range(mix_grad.shape[1] // HHD):
        pair_ref[head] = fold(head_low(mix_grad, head)).astype(LOW)
    grad_ref[0] = dot(low, light_out_ref[...]).astype(LOW)
    weights_acc[0] += cols_dot(low, mix_ref[0])
    weights_acc[1] += cols_dot(slot, heavy_mix_ref[0])

    @pl.when(step == pl.num_programs(0) - 1)
    def _():
        start, rows = down_ref.shape[0], weights_acc.shape[1]
        weights_ref[:start, :] = down_ref[...]
        for kind in range(2):
            weights_ref[start + kind * rows : start + (kind + 1) * rows, :] = weights_acc[kind].astype(LOW)


def middle_back(
    tokens, own, other, part, beyond, up, gains, routers, slots, gate, mlp, mlp_other,
    mix, heavy_mix, light_out, heavy_out, down, seq_devices,
):
    seqs, length, width = tokens.shape
    cap = slots.shape[1]
    cols = light_out.shape[1]
    heads = heavy_out.shape[1] // HHD
    shapes = [
        like(tokens.shape, LOW),
        like(tokens.shape, WIDE),
        like((seqs, length, cols), LOW),
        like((seq_devices, cap // 2, LANES), LOW),
        like((down.shape[0] + 2 * width, cols), LOW),
        like((8, width), WIDE),
        like((seqs, cap, LANES), WIDE),
    ]
    specs = [
        each(shapes[0]), each(shapes[1]), each(shapes[2]), pair_spec(shapes[3], heads),
        whole(shapes[4]), whole(shapes[5]), each(shapes[6]),
    ]
    both = pl.BlockSpec((2, 1, length, width), lambda s: (0, s, 0, 0))
    return pl.pallas_call(
        middle_kernel,
        grid=(seqs,),
        in_specs=[
            each(tokens), each(own), each(other), both, both, each(up), whole(gains),
            whole(routers), each(slots), each(gate), each(mlp), each(mlp_other), each(mix),
            each(heavy_mix), whole(light_out), whole(heavy_out), whole(down),
        ],
        out_specs=specs,
        out_shape=shapes,
        scratch_shapes=[pltpu.VMEM((2, width, cols), WIDE)],
        compiler_params=params(),
        cost_estimate=cost(11),
        name="middle_back",
    )(
        tokens, own, other, part, beyond, up, gains, routers, slots, gate, mlp, mlp_other,
        mix, heavy_mix, light_out, heavy_out, down,
    )


def light_project_kernel(local_ref, low_ref, light_ref, grad_ref, part_ref):
    @pl.when(pl.program_id(0) == 0)
    def _():
        grad_ref[...] = jnp.zeros_like(grad_ref)

    low = low_ref[0]
    part = None
    for kind in range(3):
        rows = local_ref[0, kind]
        grad_ref[kind] += cols_dot(low, rows)
        more = rows_dot(rows, light_ref[kind])
        part = more if part is None else part + more
    part_ref[0] = part


def light_project(local, low, light):
    shapes = [like(light.shape, WIDE), like(low.shape, WIDE)]
    return pl.pallas_call(
        light_project_kernel,
        grid=(low.shape[0],),
        in_specs=[each(local), each(low), whole(light)],
        out_specs=[whole(shapes[0]), each(shapes[1])],
        out_shape=shapes,
        compiler_params=params(),
        cost_estimate=cost(9),
        name="light_project",
    )(local, low, light)


def heavy_project_kernel(
    light_part_ref, low_ref, pairs_ref, heavy_ref, slots_ref, gate_ref, raw_ref, logit_ref,
    lead_ref, tail_ref, light_ref, light_sum_ref,
    grad_ref, light_grad_ref, part_ref, both_logit_ref, grad_acc, light_acc,
):
    step = pl.program_id(0)

    @pl.when(step == 0)
    def _():
        grad_acc[...] = jnp.zeros_like(grad_acc)
        light_acc[...] = light_sum_ref[1:]

    low = low_ref[0]
    length = low.shape[0]
    slots = slots_ref[0]
    cap = slots.shape[0]
    heads = raw_ref.shape[2] // HHD
    key_gate = column(gate_ref[0], 1)
    query_grad = merge_heads(pairs_ref, cap, heads).astype(LOW)
    key_grad = merge_upper(pairs_ref, cap, heads).astype(LOW)
    value_grad = merge_folded(pairs_ref, cap, heads)
    raw_grad = (key_gate * value_grad).astype(LOW)
    key_logit = jnp.sum(value_grad * raw_ref[0], axis=-1, keepdims=True)
    both_logit_ref[0] = columns((cap, LANES), column(logit_ref[0], 0), key_logit)
    hot_query = hot_rows(slots, ROW_QUERY, length).astype(LOW)
    hot_key = hot_rows(slots, ROW_KEY, length).astype(LOW)
    query_in = dot(hot_query, low).astype(LOW)
    key_in = dot(hot_key, low).astype(LOW)
    grad_acc[0] += cols_dot(query_in, query_grad)
    grad_acc[1] += cols_dot(key_in, key_grad)
    grad_acc[2] += cols_dot(key_in, raw_grad)
    part = light_part_ref[0] + place_rows(hot_query, rows_dot(query_grad, heavy_ref[0]))
    part = part + place_rows(
        hot_key, rows_dot(key_grad, heavy_ref[1]) + rows_dot(raw_grad, heavy_ref[2])
    )
    edges = []
    for ref, rows in ((lead_ref, slice(0, WIN)), (tail_ref, slice(length - WIN, length))):
        for kind in range(2):
            light_acc[kind] += cols_dot(low[rows], ref[0, kind])
        edges.append(rows_dot(ref[0, 0], light_ref[1]) + rows_dot(ref[0, 1], light_ref[2]))
    part_ref[0, :WIN] = (part[:WIN] + edges[0]).astype(LOW)
    part_ref[0, WIN : length - WIN] = part[WIN : length - WIN].astype(LOW)
    part_ref[0, length - WIN :] = (part[length - WIN :] + edges[1]).astype(LOW)

    @pl.when(step == pl.num_programs(0) - 1)
    def _():
        grad_ref[...] = grad_acc[...].astype(LOW)
        light_grad_ref[0] = light_sum_ref[0].astype(LOW)
        light_grad_ref[1:] = light_acc[...].astype(LOW)


def heavy_project(
    light_part, low, pairs, heavy, slots, gate, raw, logit, lead, tail, light, light_sum
):
    heads = heavy.shape[2] // HHD
    shapes = [
        like(heavy.shape, LOW),
        like(light.shape, LOW),
        like(low.shape, LOW),
        like(logit.shape, WIDE),
    ]
    return pl.pallas_call(
        heavy_project_kernel,
        grid=(low.shape[0],),
        in_specs=[
            each(light_part), each(low), pair_spec(pairs, heads), whole(heavy), each(slots),
            each(gate), each(raw), each(logit), each(lead), each(tail), whole(light),
            whole(light_sum),
        ],
        out_specs=[whole(shapes[0]), whole(shapes[1]), each(shapes[2]), each(shapes[3])],
        out_shape=shapes,
        scratch_shapes=[
            pltpu.VMEM(heavy.shape, WIDE),
            pltpu.VMEM((2,) + light.shape[1:], WIDE),
        ],
        compiler_params=params(),
        cost_estimate=cost(11),
        name="heavy_project",
    )(light_part, low, pairs, heavy, slots, gate, raw, logit, lead, tail, light, light_sum)


def input_kernel(
    part_ref, other_ref, logit_ref, logit_other_ref, gate_ref, slots_ref, tokens_ref, gains_ref,
    routers_ref, middle_ref, small_in_ref, grad_ref, small_ref,
):
    @pl.when(pl.program_id(0) == 0)
    def _():
        small_ref[...] = small_in_ref[...]

    slots = slots_ref[0]
    cap = slots.shape[0]
    inputs = tokens_ref[0].astype(WIDE)
    length = inputs.shape[0]
    factor = rms_of(inputs)
    scaled = inputs * factor
    normed = scaled * gains_ref[0:1, :]
    gates = gate_ref[0]
    grads = (logit_ref[0] + logit_other_ref[0]) * gates * (1.0 - gates)
    query_logit = jnp.where(column(slots, OK_QUERY) > 0, column(grads, 0), 0.0)
    key_logit = jnp.where(column(slots, OK_KEY) > 0, column(grads, 1), 0.0)
    query_token = column(
        exact_place(hot_rows(slots, ROW_QUERY, length), columns((cap, LANES), query_logit)), 0
    )
    key_token = column(
        exact_place(hot_rows(slots, ROW_KEY, length), columns((cap, LANES), key_logit)), 0
    )
    normed_grad = (
        (part_ref[0].astype(WIDE) + other_ref[0].astype(WIDE))
        + query_token * routers_ref[0:1, :]
        + key_token * routers_ref[1:2, :]
    )
    small_ref[2:3, :] += jnp.sum(normed_grad * scaled, axis=0, keepdims=True)
    small_ref[3:4, :] += jnp.sum(query_token * normed, axis=0, keepdims=True)
    small_ref[4:5, :] += jnp.sum(key_token * normed, axis=0, keepdims=True)
    grad_ref[0] = middle_ref[0] + norm_back(inputs, factor, normed_grad * gains_ref[0:1, :])


def input_back(part, other, logit, logit_other, gate, slots, tokens, gains, routers, middle, small):
    shapes = [like(middle.shape, WIDE), like(small.shape, WIDE)]
    return pl.pallas_call(
        input_kernel,
        grid=(tokens.shape[0],),
        in_specs=[
            each(part), each(other), each(logit), each(logit_other), each(gate), each(slots),
            each(tokens), whole(gains), whole(routers), each(middle), whole(small),
        ],
        out_specs=[each(shapes[0]), whole(shapes[1])],
        out_shape=shapes,
        compiler_params=params(),
        cost_estimate=cost(6),
        name="input_back",
    )(part, other, logit, logit_other, gate, slots, tokens, gains, routers, middle, small)


def heavy_weights_kernel(tile, core_ref, here_ref, there_ref, in_ref, out_ref, *refs):
    din_ref, dout_ref, rows_ref, grad_ref, hidden_ref, gate_ref, up_ref, sems = refs[-8:]

    starts = range(0, rows_ref.shape[0], tile)
    first = pl.program_id(0) == 0

    def copies(rows_from, grad_from, index):
        part = pl.ds(index * tile, tile)
        return [
            pltpu.make_async_copy(rows_from.at[part, :], rows_ref.at[part, :], sems.at[0, index]),
            pltpu.make_async_copy(grad_from.at[part, :], grad_ref.at[part, :], sems.at[1, index]),
        ]

    def fetch(rows_from, grad_from):
        for index in range(len(starts)):
            for copy in copies(rows_from, grad_from, index):
                copy.start()

    @pl.when(first & (core_ref[0, 0] == 0))
    def _():
        fetch(here_ref, there_ref)

    @pl.when(first & (core_ref[0, 0] != 0))
    def _():
        fetch(there_ref, here_ref)

    def every_tile(waits):
        for index, start in enumerate(starts):
            if waits:
                for copy in copies(here_ref, there_ref, index):
                    copy.wait()
            part = pl.ds(start, tile)
            rows = rows_ref[part, :]
            hidden, gate_grad, up_grad = gelu_parts(
                dot(rows, in_ref[0]), dot(rows, in_ref[1]), dot(grad_ref[part, :], out_ref[...])
            )
            hidden_ref[part, :] = hidden.astype(LOW)
            gate_ref[part, :] = gate_grad.astype(LOW)
            up_ref[part, :] = up_grad.astype(LOW)

    pl.when(first)(lambda: every_tile(True))
    pl.when(jnp.logical_not(first))(lambda: every_tile(False))
    dout_ref[...] = cols_dot(grad_ref[...], hidden_ref[...])
    din_ref[:, 0, :] = cols_dot(rows_ref[...], gate_ref[...])
    din_ref[:, 1, :] = cols_dot(rows_ref[...], up_ref[...])


def heavy_weights(core, here, there, weight_in, weight_out, first_block, count_blocks, done):
    count, width = here.shape
    hidden = weight_out.shape[1]
    cols = 256
    tile = 512 if count % 512 == 0 else count
    out_block = pl.BlockSpec((width, cols), lambda i: (0, first_block + i))
    in_block = pl.BlockSpec((width, 2, cols), lambda i: (0, 0, first_block + i))
    return pl.pallas_call(
        lambda *refs: heavy_weights_kernel(tile, *refs),
        grid=(count_blocks,),
        in_specs=[
            pl.BlockSpec(memory_space=pltpu.SMEM),
            pl.BlockSpec(memory_space=pl.ANY),
            pl.BlockSpec(memory_space=pl.ANY),
            pl.BlockSpec((2, width, cols), lambda i: (0, 0, first_block + i)),
            out_block,
        ]
        + [pl.BlockSpec(memory_space=pl.ANY)] * len(done),
        out_specs=[in_block, out_block],
        out_shape=[like((width, 2, hidden), WIDE), like((width, hidden), WIDE)],
        scratch_shapes=[pltpu.VMEM((count, width), LOW)] * 2
        + [pltpu.VMEM((count, cols), LOW)] * 3
        + [pltpu.SemaphoreType.DMA((2, count // tile))],
        input_output_aliases={5 + i: i for i in range(len(done))},
        compiler_params=params(60),
        cost_estimate=cost(4 + 9 * count_blocks * count / 3072),
        name="heavy_weights",
    )(core, here, there, weight_in, weight_out, *done)


def bit_pairs(bit):
    return [(i, i ^ (1 << bit)) for i in range(lax.axis_size("seq"))]


def bit_here(bit):
    return (lax.axis_index("seq") >> bit) & 1


def after(value, *others):
    return lax.optimization_barrier((value,) + others)[0]


def scatter_start(value, bit):
    halves = value.reshape(2, value.shape[0] // 2, value.shape[1])
    mine = bit_here(bit)
    sent = lax.dynamic_index_in_dim(halves, 1 - mine, 0, keepdims=False)
    kept = lax.dynamic_index_in_dim(halves, mine, 0, keepdims=False)
    return kept, lax.ppermute(sent, "seq", bit_pairs(bit))


def scatter_end(started, *others):
    kept, got = started
    got = after(got, *others)
    return (kept.astype(WIDE) + got.astype(WIDE)).astype(LOW)


def gather_start(value, bit):
    return value, lax.ppermute(value, "seq", bit_pairs(bit)), bit_here(bit)


def gather_end(started, *others):
    value, got, mine = started
    got = after(got, *others)
    return jnp.where(
        mine == 0,
        jnp.concatenate([value, got], axis=0),
        jnp.concatenate([got, value], axis=0),
    )


def interleave(parts, blocks):
    cut = [p.reshape(blocks, -1, p.shape[1]) for p in parts]
    return jnp.concatenate(cut, axis=1).reshape(-1, parts[0].shape[1])


def apart(value, blocks, rows):
    cut = value.reshape(blocks, -1, value.shape[1])
    marks = [sum(rows[:i]) // blocks for i in range(len(rows) + 1)]
    return [
        cut[:, marks[i] : marks[i + 1]].reshape(-1, value.shape[1]) for i in range(len(rows))
    ]


def in_order(bit_ref, mine_ref, got_ref, body):
    pl.when(bit_ref[0, 0] == 0)(lambda: body(mine_ref, got_ref))
    pl.when(bit_ref[0, 0] != 0)(lambda: body(got_ref, mine_ref))


def finish_call(kernel, bit, mine, got, shapes, name):
    shapes = [like(shape, WIDE) for shape in shapes]
    return pl.pallas_call(
        kernel,
        in_specs=[
            pl.BlockSpec(memory_space=pltpu.SMEM),
            pl.BlockSpec(memory_space=pltpu.VMEM),
            pl.BlockSpec(memory_space=pltpu.VMEM),
        ],
        out_shape=shapes,
        compiler_params=params(),
        name=name,
    )(bit_here(bit).astype(jnp.int32).reshape(1, 1), mine, got)


def feed_in_kernel(bit_ref, mine_ref, got_ref, in_ref):
    width, _, hidden = in_ref.shape

    def body(*halves):
        for kind, ref in enumerate(halves):

            def store(rows, cols, value, kind=kind):
                in_ref[rows, kind, cols] = value.astype(WIDE)

            unpack_wide(store, ref, 0, width, hidden - ref.shape[1])

    in_order(bit_ref, mine_ref, got_ref, body)


def outs_kernel(bit_ref, mine_ref, got_ref, feed_ref, light_ref, heavy_ref):
    width, hidden = feed_ref.shape

    def body(first_ref, second_ref):
        half, cols = first_ref.shape

        def store(rows, lanes, value):
            feed_ref[rows, lanes] = value.astype(WIDE)

        unpack_wide(store, first_ref, 0, width, hidden - cols)
        start = width * hidden // cols
        light_ref[: half - start, :] = first_ref[start:, :].astype(WIDE)
        rest = width - (half - start)
        light_ref[half - start :, :] = second_ref[:rest, :].astype(WIDE)
        heavy_ref[...] = second_ref[rest:, :].astype(WIDE)

    in_order(bit_ref, mine_ref, got_ref, body)


def kinds_kernel(bit_ref, mine_ref, got_ref, wide_ref):
    def body(first_ref, second_ref):
        half = first_ref.shape[0]
        wide_ref[:half, :] = first_ref[...].astype(WIDE)
        wide_ref[half:, :] = second_ref[...].astype(WIDE)

    in_order(bit_ref, mine_ref, got_ref, body)


def other_core(value):
    return lax.ppermute(value, "mp", [(0, 1), (1, 0)])


def to_neighbours(first, last):
    peers = lax.axis_size("seq")
    up = [(i, i + 1) for i in range(peers - 1)]
    down = [(i + 1, i) for i in range(peers - 1)]
    return lax.ppermute(last, "seq", up), lax.ppermute(first, "seq", down)


def exchange(pairs):
    return lax.all_to_all(pairs, "seq", split_axis=0, concat_axis=0, tiled=True)


def by_kind(weights):
    return weights.transpose(1, 0, 2)


def shards(
    tokens,
    out_grad,
    gains,
    routers,
    light_query_key_value_weight,
    light_attention_output_weight,
    heavy_qkv,
    heavy_out,
    light_feedforward_input_weight,
    light_feedforward_output_weight,
    heavy_mlp_in,
    heavy_mlp_out,
    routed_queries,
    routed_keys,
    routed_mlp,
    block_counts,
):
    seq_count, local_len, width = tokens.shape
    seq_devices = lax.axis_size("seq")
    row_base = lax.axis_index("seq") * local_len
    capacity = routed_queries.shape[1]
    light_cols = light_query_key_value_weight.shape[2]
    gain_rows, router_rows = gains.T, routers.T
    slot_ids = jnp.arange(capacity, dtype=jnp.int32)[None, :, None]
    rows = jnp.stack([routed_queries, routed_keys, routed_mlp], axis=2) - row_base
    valid = (slot_ids < block_counts).astype(jnp.int32)
    slots = jnp.concatenate([rows, valid], axis=2)
    place = jnp.stack([row_base, jnp.int32(seq_devices * local_len)]).astype(jnp.int32)[None, :]
    core = lax.axis_index("mp").astype(jnp.int32).reshape(1, 1)
    light_weights = by_kind(light_query_key_value_weight)
    heavy_weights_qkv = by_kind(heavy_qkv)

    own_tokens = lax.dynamic_index_in_dim(tokens, lax.axis_index("mp"), 0, keepdims=False)
    edges = to_neighbours(own_tokens[:WIN], own_tokens[local_len - WIN :])
    low, pairs, raw, gate = front(
        tokens, gain_rows, router_rows, slots, heavy_weights_qkv, seq_devices
    )
    edges = [after(edge, low) for edge in edges]
    first_core = lax.axis_index("mp") == 0
    before, behind = [
        jnp.where(first_core, jnp.stack([mine, more]), jnp.stack([more, mine]))
        for mine, more in zip(edges, [other_core(edge) for edge in edges])
    ]
    pair = exchange(after(pairs, before, behind))
    mix, attn, lse, query, window = light_forward(
        place, low, before, behind, gain_rows, light_weights, light_attention_output_weight
    )
    pair_query, pair_key, pair_value, kept, pair_mix = heavy_forward(after(pair, attn))
    mix_pairs = exchange(pair_mix)
    light_in = by_kind(after(light_feedforward_input_weight, kept))
    heavy_in = by_kind(after(heavy_mlp_in, kept))
    own, heavy_mix = combine(after(mix_pairs, light_in, heavy_in), attn, heavy_out, slots, gate)
    other = other_core(own)
    low_two, rows, slot, ship, gate_two = mlp_slots(
        core, tokens, own, other, out_grad, gain_rows, router_rows, slots
    )
    all_slots = seq_count * capacity * seq_devices
    gather_heavy = 2 * all_slots * width < 4 * (heavy_mlp_in.size + heavy_mlp_out.size)
    here = lax.all_gather(ship, "seq", axis=1, tiled=True) if gather_heavy else ship
    part, feed_grads, mlp = feed(
        low_two, rows, slot, gate_two, out_grad, slots, light_in, light_feedforward_output_weight,
        heavy_in, heavy_mlp_out, light_cols,
    )
    beyond, mlp_other = other_core(part), other_core(mlp)
    bits = (seq_devices - 1).bit_length()
    blocks = 1 << (bits - 2)
    first_going = scatter_start(feed_grads[:2].reshape(-1, light_cols), 0)
    mixed, middle_grad, mix_grad, grad_pairs, out_grads, small, query_logit = middle_back(
        tokens, own, other, part, beyond, out_grad, gain_rows, router_rows, slots, gate, mlp,
        mlp_other, mix, heavy_mix, light_attention_output_weight, heavy_out, feed_grads[2], seq_devices,
    )
    pair_grad = exchange(grad_pairs)
    local, early, late = light_backward(place, query, window, lse, mix_grad)
    first_wave = scatter_end(first_going, local)
    lead, tail = to_neighbours(early, late)
    triple = heavy_backward(
        pair_query, pair_key, pair_value, kept, after(pair_grad, local, first_wave)
    )
    triple_pairs = exchange(triple)
    second_going = scatter_start(after(out_grads, triple), 1)
    light_sums, light_part = light_project(after(local, triple), low, light_weights)
    second_wave = scatter_end(second_going, light_part)
    heavy_grads, light_grads, low_part, logit = heavy_project(
        light_part, low, after(triple_pairs, second_wave), heavy_weights_qkv, slots, gate, raw,
        query_logit, lead, tail, light_weights, light_sums,
    )
    heavy_going = scatter_start(heavy_grads.reshape(-1, light_cols), 1)
    light_going = scatter_start(light_grads.reshape(-1, light_cols), 0)
    second_going = scatter_start(after(second_wave, low_part), 0)
    first_going = scatter_start(after(first_wave, low_part), 1)
    low_other, logit_other = other_core(low_part), other_core(logit)
    here = after(here, low_part)
    there = other_core(here).reshape(-1, width)
    here = here.reshape(-1, width)
    blocks_done = [0]
    heavy_sums = []

    def heavy_piece(count, *others):
        heavy_sums[:] = heavy_weights(
            core, after(here, *others), there, heavy_in, heavy_mlp_out, blocks_done[0], count, heavy_sums
        )
        blocks_done[0] += count
        return heavy_sums[1]

    input_grad, small = input_back(
        low_part, low_other, logit, logit_other, gate, slots, tokens, gain_rows,
        router_rows, middle_grad, small,
    )
    small_rows = small.astype(LOW).reshape(-1, light_cols)
    small_rows = jnp.pad(small_rows, ((0, 16 * blocks - small_rows.shape[0]), (0, 0)))
    small_got = lax.ppermute(small_rows, "seq", bit_pairs(1))
    second_wave = scatter_end(second_going, input_grad)
    first_wave = scatter_end(first_going, input_grad)
    early_sizes = [first_wave.shape[0], second_wave.shape[0]]
    wave = interleave([first_wave, second_wave], blocks)
    going = scatter_start(wave, 2)
    mark = heavy_piece(2, input_grad, wave)
    wave = scatter_end(going, mark)
    heavy_wave = scatter_end(heavy_going, mark)
    light_wave = scatter_end(light_going, mark)
    light_going = scatter_start(light_wave, 1)
    small_rows = scatter_end((small_rows, small_got), mark)
    for bit in range(3, bits - 1):
        wave = scatter_end(scatter_start(wave, bit))
    going = scatter_start(wave, bits - 1)
    heavy_going = scatter_start(heavy_wave, 0)
    small_got = lax.ppermute(small_rows, "seq", bit_pairs(0))
    mark = heavy_piece(1, wave, heavy_wave, light_wave, small_rows)
    wave = scatter_end(going, mark)
    heavy_wave = scatter_end(heavy_going, mark)
    light_wave = scatter_end(light_going, mark)
    small_rows = scatter_end((small_rows, small_got), mark)
    for bit in reversed(range(4, bits)):
        wave = gather_end(gather_start(wave, bit))
    going = gather_start(wave, 3)
    late_wave = [light_wave, heavy_wave, small_rows]
    late_sizes = [p.shape[0] for p in late_wave]
    late_wave = interleave(late_wave, blocks)
    late_going = scatter_start(late_wave, 2)
    mark = heavy_piece(1, late_wave, wave)
    wave = gather_end(going, mark)
    late_wave = scatter_end(late_going, mark)
    for bit in range(3, bits - 1):
        late_wave = scatter_end(scatter_start(late_wave, bit))
    going = gather_start(wave, 2)
    late_going = scatter_start(late_wave, bits - 1)
    mark = heavy_piece(1, late_wave, wave)
    wave = apart(gather_end(going, mark), blocks, early_sizes)
    going = [gather_start(p, bit) for p, bit in zip(wave, (1, 0))]
    late_wave = scatter_end(late_going, mark)
    for bit in reversed(range(4, bits)):
        late_wave = gather_end(gather_start(late_wave, bit))
    late_going = gather_start(late_wave, 3)
    mark = heavy_piece(1, late_wave, *wave)
    wave = [gather_end(p, mark) for p in going]
    early_halves = [(p, lax.ppermute(p, "seq", bit_pairs(bit))) for p, bit in zip(wave, (0, 1))]
    late_wave = gather_end(late_going, mark)
    late_going = gather_start(late_wave, 2)
    mark = heavy_piece(1, late_wave, *wave)
    late_wave = apart(gather_end(late_going, mark), blocks, late_sizes)
    small_sum = late_wave.pop().astype(WIDE)
    late_going = [gather_start(p, bit) for p, bit in zip(late_wave, (1, 0))]
    early_halves = [(after(p, *late_wave), after(got, mark)) for p, got in early_halves]
    hidden = light_feedforward_output_weight.shape[1]
    square, kinds = (width, light_cols), [(3 * width, light_cols)]
    (feed_in,) = finish_call(feed_in_kernel, 0, *early_halves[0], [(width, 2, hidden)], "feed_in")
    feed_out, light_out_sum, heavy_out_sum = finish_call(
        outs_kernel, 1, *early_halves[1], [(width, hidden), square, square], "outs"
    )
    late_wave = [gather_end(p, feed_in, feed_out) for p in late_going]
    late_halves = [
        (p, lax.ppermute(p, "seq", bit_pairs(bit))) for p, bit in zip(late_wave, (0, 1))
    ]
    mark = heavy_piece(1, *late_wave)
    late_halves = [(p, after(got, mark)) for p, got in late_halves]
    heavy_in_grad, heavy_out_grad = heavy_sums
    if not gather_heavy:
        sums = [heavy_in_grad[:, 0], heavy_in_grad[:, 1], heavy_out_grad]
        sums = [p.astype(LOW) for p in sums]
        for bit in range(bits):
            sums = [scatter_end(scatter_start(p, bit)) for p in sums]
        for bit in reversed(range(bits)):
            sums = [gather_end(gather_start(p, bit)) for p in sums]
        heavy_in_grad = jnp.stack(sums[:2], axis=1).astype(WIDE)
        heavy_out_grad = sums[2].astype(WIDE)
    (light_sum,) = finish_call(kinds_kernel, 0, *late_halves[0], kinds, "light_sum")
    (heavy_sum,) = finish_call(kinds_kernel, 1, *late_halves[1], kinds, "heavy_sum")
    small_sum = small_sum[: 8 * width // light_cols].reshape(8, width)
    return (
        mixed,
        input_grad,
        light_sum.reshape(3, width, light_cols).transpose(1, 0, 2),
        light_out_sum,
        heavy_sum.reshape(3, width, light_cols).transpose(1, 0, 2),
        heavy_out_sum,
        feed_in,
        feed_out,
        heavy_in_grad,
        heavy_out_grad,
        jnp.stack([small_sum[2], small_sum[0]], axis=1),
        jnp.stack([small_sum[3], small_sum[4], small_sum[1]], axis=1),
    )


def solution(mesh):
    rows = P(None, "seq", None)
    by_column = P(None, None, "mp")
    by_hidden = P(None, "mp")
    slots = P(None, "seq")
    weights = (by_column, by_hidden) * 4
    return jax.shard_map(
        shards,
        mesh=mesh,
        in_specs=(rows, rows, P(), P()) + weights + (slots, slots, slots, rows),
        out_specs=(rows, rows) + weights + (P(), P()),
        check_vma=False,
    )
```

profile of v0, /device:TPU:0, one launch (start us, length us, event | category | flops | bytes accessed | tf_op | source)
XLA Modules:
  0.0 415.6 jit_solution(4157285773463003599)
XLA Ops:
  9.5 5.5 %collective-permute-start = (bf16[128,768]{1,0:T(8,128)(2,1)S(1)}, bf16[128,768]{1,0:T(8,128)(2,1)S(1)}, u32[]{:S(2)}, u32[]{:S(2)}) collective-permute-start(bf16[128,768]{1,0:T(8,128)(2,1)S(1)} %get-tuple-element.229), channel_id=1, source_target_pairs={{0,2},{2,4},{4,6},{6,8},{8,10},{10,12},{12,14},{14,16},{16,18},{18... | collective-permute-start | bytes 589832 | tf_op jit(solution)/shard_map/ppermute | solution.py:1203
  17.4 5.5 %front.1 = (bf16[2,384,768]{2,1,0:T(8,128)(2,1)}, bf16[16,144,128]{2,1,0:T(8,128)(2,1)}, f32[2,96,384]{2,1,0:T(8,128)}, f32[2,96,128]{2,1,0:T(8,128)}) custom-call(bf16[2,384,768]{2,1,0:T(8,128)(2,1)} %tokens_ref.7, f32[2,768]{1,0:T(2,128)} %bitcast.222, f32[3,768]{1,0:T(4,128)} %bitcast.218, s32[2,96,6]{2,1,0:T(8,128)} %copy.48.slots_ref, ...), custom_call_target="tpu_custom_call" | custom-call | flops 160000000 | bytes 1024 | tf_op jit(solution)/shard_map/front/pallas_call | solution.py:237
  26.3 7.9 %all-to-all-start = ((bf16[16,144,128]{2,1,0:T(8,128)(2,1)}), bf16[16,144,128]{2,1,0:T(8,128)(2,1)S(1)}, u32[]{:S(2)}, u32[]{:S(2)}) async-start(bf16[16,144,128]{2,1,0:T(8,128)(2,1)} %get-tuple-element.124), calls=%async_computation | async-start | bytes 1179648 | tf_op jit(solution)/shard_map/all_to_all | solution.py:1207
  34.8 13.2 %light_forward.1 = (bf16[2,384,384]{2,1,0:T(8,128)(2,1)}, f32[2,384,768]{2,1,0:T(8,128)}, f32[2,384,128]{2,1,0:T(8,128)}, bf16[2,384,512]{2,1,0:T(8,128)(2,1)}, bf16[2,2,640,512]{3,2,1,0:T(8,128)(2,1)}) custom-call(s32[1,2]{1,0:T(1,128)} %add_bitcast_fusion.refs_0_, bf16[2,384,768]{2,1,0:T(8,128)(2,1)} %get-tuple-element.121.refs_1_.low_ref, ...), custom_call_target="tpu_custom_call" | custom-call | flops 300000000 | bytes 1024 | tf_op jit(solution)/shard_map/light_forward/pallas_call | solution.py:318
  48.0 2.7 all-to-all-done.refs_0_
  51.5 9.9 %heavy_forward.1 = (bf16[1536,128]{1,0:T(8,128)(2,1)}, bf16[1536,128]{1,0:T(8,128)(2,1)}, bf16[1536,128]{1,0:T(8,128)(2,1)}, f32[1536,128]{1,0:T(8,128)}, bf16[16,48,128]{2,1,0:T(8,128)(2,1)}) custom-call(bf16[16,144,128]{2,1,0:T(8,128)(2,1)} %copy-done.6), custom_call_target="tpu_custom_call" | custom-call | flops 140000000 | bytes 1024 | tf_op jit(solution)/shard_map/heavy_forward/pallas_call | solution.py:503
  61.5 4.2 %all-to-all-start.1 = ((bf16[16,48,128]{2,1,0:T(8,128)(2,1)}), bf16[16,48,128]{2,1,0:T(8,128)(2,1)S(1)}, u32[]{:S(2)}, u32[]{:S(2)}) async-start(bf16[16,48,128]{2,1,0:T(8,128)(2,1)} %get-tuple-element.127), calls=%async_computation.1 | async-start | bytes 393216 | tf_op jit(solution)/shard_map/all_to_all | solution.py:1207
  67.3 8.3 %copy.64 = bf16[768,2,2048]{2,0,1:T(8,128)(2,1)} copy(bf16[768,2,2048]{2,1,0:T(2,128)(2,1)} %param.26) | data formatting | bytes 12582912 | tf_op jit(solution)/shard_map/optimization_barrier | solution.py:1089
  76.3 4.0 combine.1
  80.3 3.0 collective-permute-done.4.other_ref
  84.3 4.8 %mlp_slots.1 = (bf16[2,384,768]{2,1,0:T(8,128)(2,1)}, bf16[2,96,768]{2,1,0:T(8,128)(2,1)}, bf16[2,96,768]{2,1,0:T(8,128)(2,1)}, bf16[2,96,768]{2,1,0:T(8,128)(2,1)}, f32[2,96,128]{2,1,0:T(8,128)}) custom-call(s32[1,1]{1,0:T(1,128)} %bitcast.18.core_ref.refs_0_, bf16[2,384,768]{2,1,0:T(8,128)(2,1)} %tokens_ref.7, ...), custom_call_target="tpu_custom_call" | custom-call | flops 100000000 | bytes 1024 | tf_op jit(solution)/shard_map/mlp_slots/pallas_call | solution.py:607
  89.1 20.6 %feed.1 = (bf16[2,2,384,768]{3,2,1,0:T(8,128)(2,1)}, bf16[3,1024,384]{2,1,0:T(8,128)(2,1)}, f32[2,96,128]{2,1,0:T(8,128)}) custom-call(bf16[2,384,768]{2,1,0:T(8,128)(2,1)} %get-tuple-element.134.low_ref, bf16[192,768]{1,0:T(8,128)(2,1)} %bitcast.211, bf16[192,768]{1,0:T(8,128)(2,1)} %bitcast.212, f32[2,96,128]{2,1,0:T(8,128)} %get-tuple-element.137.kept_ref, ...), custom_call_target="tpu_custom_call" | custom-call | flops 400000000 | bytes 1024 | tf_op jit(solution)/shard_map/feed/pallas_call | solution.py:715
  109.9 1.6 slice.64
  111.6 2.0 collective-permute-start.7
  113.7 2.1 slice_bitcast_fusion.down_ref
  116.5 12.3 %middle_back.1 = (bf16[2,384,768]{2,1,0:T(8,128)(2,1)}, f32[2,384,768]{2,1,0:T(8,128)}, bf16[2,384,384]{2,1,0:T(8,128)(2,1)}, bf16[16,48,128]{2,1,0:T(8,128)(2,1...) custom-call(bf16[2,384,768]{2,1,0:T(8,128)(2,1)} %tokens_ref.7, ...), custom_call_target="tpu_custom_call" | custom-call | flops 220000000 | bytes 1024 | tf_op jit(solution)/shard_map/middle_back/pallas_call | solution.py:820
  128.7 5.6 %all-to-all-start.2 = ((bf16[16,48,128]{2,1,0:T(8,128)(2,1)}), bf16[16,48,128]{2,1,0:T(8,128)(2,1)S(1)}, u32[]{:S(2)}, u32[]{:S(2)}) async-start(bf16[16,48,128]{2,1,0:T(8,128)(2,1)} %get-tuple-element.152), calls=%async_computation.2 | async-start | bytes 393216 | tf_op jit(solution)/shard_map/all_to_all | solution.py:1207
  134.3 10.2 %light_backward.1 = (bf16[2,3,384,384]{3,2,1,0:T(8,128)(2,1)}, bf16[2,2,128,384]{3,2,1,0:T(8,128)(2,1)}, bf16[2,2,128,384]{3,2,1,0:T(8,128)(2,1)}) custom-call(s32[1,2]{1,0:T(1,128)} %add_bitcast_fusion.refs_0_, bf16[2,384,512]{2,1,0:T(8,128)(2,1)} %get-tuple-element.144.refs_1_, bf16[2,2,640,512]{3,2,1,0:T(8,128)(2,1)} %get-tuple-element.145.refs_2_, ...), custom_call_target="tpu_custom_call" | custom-call | flops 280000000 | bytes 1024 | tf_op jit(solution)/shard_map/light_backward/pallas_call | solution.py:388
  146.3 9.5 %heavy_backward.1 = bf16[16,144,128]{2,1,0:T(8,128)(2,1)} custom-call(bf16[1536,128]{1,0:T(8,128)(2,1)} %get-tuple-element.149.refs_0_, bf16[1536,128]{1,0:T(8,128)(2,1)} %get-tuple-element.150.refs_1_, bf16[1536,128]{1,0:T(8,128)(2,1)} %get-tuple-element.151.refs_2_, f32[1536,128]{1,0:T(8,128)} %get-tuple-element.128.refs_3_, bf16[16,48,128]{2,1,0:T(8,128)(2,1)} %copy-done.17), custom_call_target="tpu_custom_call" | custom-call | flops 200000000 | bytes 1024 | tf_op jit(solution)/shard_map/heavy_backward/pallas_call | solution.py:524
  156.9 1.7 collective-permute-start.8
  158.6 4.9 %all-to-all-start.3 = ((bf16[16,144,128]{2,1,0:T(8,128)(2,1)}), bf16[16,144,128]{2,1,0:T(8,128)(2,1)S(1)}, u32[]{:S(2)}, u32[]{:S(2)}) async-start(bf16[16,144,128]{2,1,0:T(8,128)(2,1)} %heavy_backward.1), calls=%async_computation.3 | async-start | bytes 1179648 | tf_op jit(solution)/shard_map/all_to_all | solution.py:1207
  163.5 4.6 %collective-permute-start.9 = (bf16[2,2,128,384]{3,2,1,0:T(8,128)(2,1)}, bf16[2,2,128,384]{3,2,1,0:T(8,128)(2,1)}, u32[]{:S(2)}, u32[]{:S(2)}) collective-permute-start(bf16[2,2,128,384]{3,2,1,0:T(8,128)(2,1)} %get-tuple-element.163), channel_id=1, source_target_pairs={{0,2},{2,4},{4,6},{6,8},{8,10},{10,12},{12,14},{14,16},{16,18},{18... | collective-permute-start | bytes 1179656 | tf_op jit(solution)/shard_map/ppermute | solution.py:1203
  169.5 9.3 %light_project.1 = (f32[3,768,384]{2,1,0:T(8,128)}, f32[2,384,768]{2,1,0:T(8,128)}) custom-call(bf16[2,3,384,384]{3,2,1,0:T(8,128)(2,1)} %get-tuple-element.155.local_ref, bf16[2,384,768]{2,1,0:T(8,128)(2,1)} %get-tuple-element.121.refs_1_.low_ref, bf16[3,768,384]{2,1,0:T(8,128)(2,1)} %bitcast.166), custom_call_target="tpu_custom_call" | custom-call | flops 180000000 | bytes 1024 | tf_op jit(solution)/shard_map/light_project/pallas_call | solution.py:857
  178.7 25.0 %collective-permute-done.8 = bf16[1280,384]{1,0:T(8,128)(2,1)S(1)} collective-permute-done((bf16[1280,384]{1,0:T(8,128)(2,1)}, bf16[1280,384]{1,0:T(8,128)(2,1)S(1)}, u32[]{:S(2)}, u32[]{:S(2)}) %collective-permute-start.8) | collective-permute-done | bytes 983072 | tf_op jit(solution)/shard_map/ppermute | solution.py:1097
  204.9 13.6 %heavy_project.1 = (bf16[3,768,384]{2,1,0:T(8,128)(2,1)}, bf16[3,768,384]{2,1,0:T(8,128)(2,1)}, bf16[2,384,768]{2,1,0:T(8,128)(2,1)}, f32[2,96,128]{2,1,0:T(8,128)}) custom-call(f32[2,384,768]{2,1,0:T(8,128)} %get-tuple-element.156.light_part_ref, bf16[2,384,768]{2,1,0:T(8,128)(2,1)} %get-tuple-element.121.refs_1_.low_ref, bf16[16,144,128]{2,1,0:T(8,128)(2,1)} %copy-done.5, ...), custom_call_target="tpu_custom_call" | custom-call | flops 220000000 | bytes 1024 | tf_op jit(solution)/shard_map/heavy_project/pallas_call | solution.py:930
  220.0 3.5 collective-permute-start.17
  227.1 2.4 collective-permute-start.19
  229.5 6.3 %input_back.1 = (f32[2,384,768]{2,1,0:T(8,128)}, f32[8,768]{1,0:T(8,128)}) custom-call(bf16[2,384,768]{2,1,0:T(8,128)(2,1)} %get-tuple-element.166.part_ref, bf16[2,384,768]{2,1,0:T(8,128)(2,1)} %collective-permute-done.11.other_ref, f32[2,96,128]{2,1,0:T(8,128)} %get-tuple-element.167.logit_ref, f32[2,96,128]{2,1,0:T(8,128)} %copy-done.20, ...), custom_call_target="tpu_custom_call" | custom-call | flops 120000000 | bytes 1024 | tf_op jit(solution)/shard_map/input_back/pallas_call | solution.py:988
  239.2 2.0 collective-permute-start.18
  245.4 23.6 %heavy_weights.7 = (f32[768,2,2048]{2,1,0:T(2,128)}, f32[768,2048]{1,0:T(8,128)}) custom-call(s32[1,1]{1,0:T(1,128)} %bitcast.18.core_ref.refs_0_, bf16[3072,768]{1,0:T(8,128)(2,1)} %bitcast.158, bf16[3072,768]{1,0:T(8,128)(2,1)} %bitcast.32.refs_2_, bf16[2,768,2048]{2,1,0:T(8,128)(2,1)} %bitcast.151, bf16[768,2048]{1,0:T(8,128)(2,1)} %refs_4_.13), custom_call_target="tpu_custom_call" | custom-call | flops 440000000 | bytes 1024 | tf_op jit(solution)/shard_map/heavy_weights/pallas_call | solution.py:1057
  275.0 1.5 collective-permute-start.21
  277.2 2.2 collective-permute-start.24
  279.5 1.7 collective-permute-start.15
  281.2 14.1 %heavy_weights.8 = (f32[768,2,2048]{2,1,0:T(2,128)}, f32[768,2048]{1,0:T(8,128)}) custom-call(s32[1,1]{1,0:T(1,128)} %bitcast.18.core_ref.refs_0_, bf16[3072,768]{1,0:T(8,128)(2,1)} %bitcast.159, bf16[3072,768]{1,0:T(8,128)(2,1)} %bitcast.32.refs_2_, bf16[2,768,2048]{2,1,0:T(8,128)(2,1)} %bitcast.152, ...), custom_call_target="tpu_custom_call", output_to_operand_aliasing={{0}: (5, {}), {1}: (6, {})} | custom-call | flops 260000000 | bytes 1024 | tf_op jit(solution)/shard_map/heavy_weights/pallas_call | solution.py:1057
  298.8 14.2 %heavy_weights.9 = (f32[768,2,2048]{2,1,0:T(2,128)}, f32[768,2048]{1,0:T(8,128)}) custom-call(s32[1,1]{1,0:T(1,128)} %bitcast.18.core_ref.refs_0_, bf16[3072,768]{1,0:T(8,128)(2,1)} %bitcast.160, bf16[3072,768]{1,0:T(8,128)(2,1)} %bitcast.32.refs_2_, bf16[2,768,2048]{2,1,0:T(8,128)(2,1)} %bitcast.153, ...), custom_call_target="tpu_custom_call", output_to_operand_aliasing={{0}: (5, {}), {1}: (6, {})} | custom-call | flops 260000000 | bytes 1024 | tf_op jit(solution)/shard_map/heavy_weights/pallas_call | solution.py:1057
  314.9 2.5 collective-permute-start.25
  317.3 14.5 %heavy_weights.10 = (f32[768,2,2048]{2,1,0:T(2,128)}, f32[768,2048]{1,0:T(8,128)}) custom-call(s32[1,1]{1,0:T(1,128)} %bitcast.18.core_ref.refs_0_, bf16[3072,768]{1,0:T(8,128)(2,1)} %bitcast.161, bf16[3072,768]{1,0:T(8,128)(2,1)} %bitcast.32.refs_2_, bf16[2,768,2048]{2,1,0:T(8,128)(2,1)} %bitcast.154, ...), custom_call_target="tpu_custom_call", output_to_operand_aliasing={{0}: (5, {}), {1}: (6, {})} | custom-call | flops 260000000 | bytes 1024 | tf_op jit(solution)/shard_map/heavy_weights/pallas_call | solution.py:1057
  334.2 14.3 %heavy_weights.11 = (f32[768,2,2048]{2,1,0:T(2,128)}, f32[768,2048]{1,0:T(8,128)}) custom-call(s32[1,1]{1,0:T(1,128)} %bitcast.18.core_ref.refs_0_, bf16[3072,768]{1,0:T(8,128)(2,1)} %bitcast.162, bf16[3072,768]{1,0:T(8,128)(2,1)} %bitcast.32.refs_2_, bf16[2,768,2048]{2,1,0:T(8,128)(2,1)} %bitcast.155, ...), custom_call_target="tpu_custom_call", output_to_operand_aliasing={{0}: (5, {}), {1}: (6, {})} | custom-call | flops 260000000 | bytes 1024 | tf_op jit(solution)/shard_map/heavy_weights/pallas_call | solution.py:1057
  349.4 1.8 collective-permute-start.33
  351.5 1.6 collective-permute-start.34
  353.1 14.1 %heavy_weights.12 = (f32[768,2,2048]{2,1,0:T(2,128)}, f32[768,2048]{1,0:T(8,128)}) custom-call(s32[1,1]{1,0:T(1,128)} %bitcast.18.core_ref.refs_0_, bf16[3072,768]{1,0:T(8,128)(2,1)} %bitcast.163, bf16[3072,768]{1,0:T(8,128)(2,1)} %bitcast.32.refs_2_, bf16[2,768,2048]{2,1,0:T(8,128)(2,1)} %bitcast.156, ...), custom_call_target="tpu_custom_call", output_to_operand_aliasing={{0}: (5, {}), {1}: (6, {})} | custom-call | flops 260000000 | bytes 1024 | tf_op jit(solution)/shard_map/heavy_weights/pallas_call | solution.py:1057
  369.6 4.3 %feed_in.1 = f32[768,2,512]{2,1,0:T(2,128)} custom-call(s32[1,1]{1,0:T(1,128)} %bitcast.27.bit_ref, bf16[1024,384]{1,0:T(8,128)(2,1)} %copy-done.4, bf16[1024,384]{1,0:T(8,128)(2,1)} %collective-permute-done.33.got_ref), custom_call_target="tpu_custom_call" | custom-call | tf_op jit(solution)/shard_map/feed_in/pallas_call | solution.py:1140
  376.0 3.7 outs.1
  382.1 1.5 collective-permute-start.37
  384.9 14.1 %heavy_weights.13 = (f32[768,2,2048]{2,1,0:T(2,128)}, f32[768,2048]{1,0:T(8,128)}) custom-call(s32[1,1]{1,0:T(1,128)} %bitcast.18.core_ref.refs_0_, bf16[3072,768]{1,0:T(8,128)(2,1)} %bitcast.164, bf16[3072,768]{1,0:T(8,128)(2,1)} %bitcast.32.refs_2_, bf16[2,768,2048]{2,1,0:T(8,128)(2,1)} %bitcast.157, ...), custom_call_target="tpu_custom_call", output_to_operand_aliasing={{0}: (5, {}), {1}: (6, {})} | custom-call | flops 260000000 | bytes 1024 | tf_op jit(solution)/shard_map/heavy_weights/pallas_call | solution.py:1057
  399.1 1.6 collective-permute-done.37.got_ref
  401.6 3.5 heavy_sum.1
  405.0 3.5 light_sum.1
  (175 shorter events, 56.4 us)
Async XLA Ops:
  8.2 15.1 %collective-permute-start.2 = (bf16[128,768]{1,0:T(8,128)(2,1)S(1)}, bf16[128,768]{1,0:T(8,128)(2,1)S(1)}, u32[]{:S(2)}, u32[]{:S(2)}) collective-permute-start(bf16[128,768]{1,0:T(8,128)(2,1)S(1)} %get-tuple-element.228), channel_id=1, source_target_pairs={{2,0},{4,2},{6,4},{8,6},{10,8},{12,10},{14,12},{16,14},{18,16},{20... | collective-permute-start | bytes 589832 | tf_op jit(solution)/shard_map/ppermute | solution.py:1203
  9.5 13.8 %collective-permute-start = (bf16[128,768]{1,0:T(8,128)(2,1)S(1)}, bf16[128,768]{1,0:T(8,128)(2,1)S(1)}, u32[]{:S(2)}, u32[]{:S(2)}) collective-permute-start(bf16[128,768]{1,0:T(8,128)(2,1)S(1)} %get-tuple-element.229), channel_id=1, source_target_pairs={{0,2},{2,4},{4,6},{6,8},{8,10},{10,12},{12,14},{14,16},{16,18},{18... | collective-permute-start | bytes 589832 | tf_op jit(solution)/shard_map/ppermute | solution.py:1203
  23.3 1.4 collective-permute-start.1
  23.3 2.2 collective-permute-start.3
  26.3 24.4 %all-to-all-start = ((bf16[16,144,128]{2,1,0:T(8,128)(2,1)}), bf16[16,144,128]{2,1,0:T(8,128)(2,1)S(1)}, u32[]{:S(2)}, u32[]{:S(2)}) async-start(bf16[16,144,128]{2,1,0:T(8,128)(2,1)} %get-tuple-element.124), calls=%async_computation | async-start | bytes 1179648 | tf_op jit(solution)/shard_map/all_to_all | solution.py:1207
  34.8 31.1 %copy-start.12 = (bf16[768,2,512]{2,1,0:T(2,128)(2,1)S(1)}, bf16[768,2,512]{2,1,0:T(2,128)(2,1)}, u32[]{:S(2)}) copy-start(bf16[768,2,512]{2,1,0:T(2,128)(2,1)} %param.24) | copy-start | bytes 4718596
  61.5 14.1 %all-to-all-start.1 = ((bf16[16,48,128]{2,1,0:T(8,128)(2,1)}), bf16[16,48,128]{2,1,0:T(8,128)(2,1)S(1)}, u32[]{:S(2)}, u32[]{:S(2)}) async-start(bf16[16,48,128]{2,1,0:T(8,128)(2,1)} %get-tuple-element.127), calls=%async_computation.1 | async-start | bytes 393216 | tf_op jit(solution)/shard_map/all_to_all | solution.py:1207
  65.7 152.9 %all-gather.2.cloned.1.call-start = ((), (), s32[]{:S(2)}) async-start(), calls=%async_computation.4 | async-start | bytes 5013504 | tf_op jit(solution)/shard_map/all_gather | solution.py:1273
  80.3 3.1 collective-permute-start.4
  109.8 6.0 %collective-permute-start.5 = (bf16[2,2,384,768]{3,2,1,0:T(8,128)(2,1)}, bf16[2,2,384,768]{3,2,1,0:T(8,128)(2,1)}, u32[]{:S(2)}, u32[]{:S(2)}) collective-permute-start(bf16[2,2,384,768]{3,2,1,0:T(8,128)(2,1)} %get-tuple-element.138.part_ref), channel_id=1, source_target_pairs={{0,1},{1,0},{2,3},{3,2},{4,5},{5,4},{6,7},{7,6},{8,9},{9,8},{10,11... | collective-permute-start | bytes 7077896 | tf_op jit(solution)/shard_map/ppermute | solution.py:1196
  111.6 32.9 %collective-permute-start.7 = (bf16[1024,384]{1,0:T(8,128)(2,1)S(1)}, bf16[1024,384]{1,0:T(8,128)(2,1)S(1)}, u32[]{:S(2)}, u32[]{:S(2)}) collective-permute-start(bf16[1024,384]{1,0:T(8,128)(2,1)S(1)} %dynamic-slice_bitcast_fusion.3), channel_id=1, source_target_pairs={{0,2},{2,0},{4,6},{6,4},{8,10},{10,8},{12,14},{14,12},{16,18},{18,... | collective-permute-start | bytes 2359304 | tf_op jit(solution)/shard_map/ppermute | solution.py:1097
  113.6 2.2 collective-permute-start.6
  128.7 17.0 %all-to-all-start.2 = ((bf16[16,48,128]{2,1,0:T(8,128)(2,1)}), bf16[16,48,128]{2,1,0:T(8,128)(2,1)S(1)}, u32[]{:S(2)}, u32[]{:S(2)}) async-start(bf16[16,48,128]{2,1,0:T(8,128)(2,1)} %get-tuple-element.152), calls=%async_computation.2 | async-start | bytes 393216 | tf_op jit(solution)/shard_map/all_to_all | solution.py:1207
  156.9 46.8 %collective-permute-start.8 = (bf16[1280,384]{1,0:T(8,128)(2,1)}, bf16[1280,384]{1,0:T(8,128)(2,1)S(1)}, u32[]{:S(2)}, u32[]{:S(2)}) collective-permute-start(bf16[1280,384]{1,0:T(8,128)(2,1)} %dynamic-slice_bitcast_fusion), channel_id=1, source_target_pairs={{0,4},{2,6},{4,0},{6,2},{8,12},{10,14},{12,8},{14,10},{16,20},{18,... | collective-permute-start | bytes 2949128 | tf_op jit(solution)/shard_map/ppermute | solution.py:1097
  158.6 45.5 %all-to-all-start.3 = ((bf16[16,144,128]{2,1,0:T(8,128)(2,1)}), bf16[16,144,128]{2,1,0:T(8,128)(2,1)S(1)}, u32[]{:S(2)}, u32[]{:S(2)}) async-start(bf16[16,144,128]{2,1,0:T(8,128)(2,1)} %heavy_backward.1), calls=%async_computation.3 | async-start | bytes 1179648 | tf_op jit(solution)/shard_map/all_to_all | solution.py:1207
  163.5 40.7 %collective-permute-start.9 = (bf16[2,2,128,384]{3,2,1,0:T(8,128)(2,1)}, bf16[2,2,128,384]{3,2,1,0:T(8,128)(2,1)}, u32[]{:S(2)}, u32[]{:S(2)}) collective-permute-start(bf16[2,2,128,384]{3,2,1,0:T(8,128)(2,1)} %get-tuple-element.163), channel_id=1, source_target_pairs={{0,2},{2,4},{4,6},{6,8},{8,10},{10,12},{12,14},{14,16},{16,18},{18... | collective-permute-start | bytes 1179656 | tf_op jit(solution)/shard_map/ppermute | solution.py:1203
  168.1 35.7 %copy-start.8 = (bf16[2560,384]{1,0:T(8,128)(2,1)S(1)}, bf16[2560,384]{1,0:T(8,128)(2,1)}, u32[]{:S(2)}) copy-start(bf16[2560,384]{1,0:T(8,128)(2,1)} %get-tuple-element.158) | copy-start | bytes 5898244
  168.1 36.1 %collective-permute-start.10 = (bf16[2,2,128,384]{3,2,1,0:T(8,128)(2,1)}, bf16[2,2,128,384]{3,2,1,0:T(8,128)(2,1)}, u32[]{:S(2)}, u32[]{:S(2)}) collective-permute-start(bf16[2,2,128,384]{3,2,1,0:T(8,128)(2,1)} %get-tuple-element.164), channel_id=1, source_target_pairs={{2,0},{4,2},{6,4},{8,6},{10,8},{12,10},{14,12},{16,14},{18,16},{20... | collective-permute-start | bytes 1179656 | tf_op jit(solution)/shard_map/ppermute | solution.py:1203
  218.6 26.8 %collective-permute-start.14 = (bf16[2,1536,768]{2,1,0:T(8,128)(2,1)}, bf16[2,1536,768]{2,1,0:T(8,128)(2,1)}, u32[]{:S(2)}, u32[]{:S(2)}) collective-permute-start(bf16[2,1536,768]{2,1,0:T(8,128)(2,1)} %all-gather.2.cloned.1.call-done), channel_id=1, source_target_pairs={{0,1},{1,0},{2,3},{3,2},{4,5},{5,4},{6,7},{7,6},{8,9},{9,8},{10,11... | collective-permute-start | bytes 14155784 | tf_op jit(solution)/shard_map/ppermute | solution.py:1196
  218.7 10.8 %collective-permute-start.11 = (bf16[2,384,768]{2,1,0:T(8,128)(2,1)}, bf16[2,384,768]{2,1,0:T(8,128)(2,1)}, u32[]{:S(2)}, u32[]{:S(2)}) collective-permute-start(bf16[2,384,768]{2,1,0:T(8,128)(2,1)} %get-tuple-element.166.part_ref), channel_id=1, source_target_pairs={{0,1},{1,0},{2,3},{3,2},{4,5},{5,4},{6,7},{7,6},{8,9},{9,8},{10,11... | collective-permute-start | bytes 3538952 | tf_op jit(solution)/shard_map/ppermute | solution.py:1196
  220.0 15.7 %collective-permute-start.17 = (bf16[640,384]{1,0:T(8,128)(2,1)}, bf16[640,384]{1,0:T(8,128)(2,1)}, u32[]{:S(2)}, u32[]{:S(2)}) collective-permute-start(bf16[640,384]{1,0:T(8,128)(2,1)} %dynamic-slice_bitcast_fusion.4), channel_id=1, source_target_pairs={{0,2},{2,0},{4,6},{6,4},{8,10},{10,8},{12,14},{14,12},{16,18},{18,... | collective-permute-start | bytes 1474568 | tf_op jit(solution)/shard_map/ppermute | solution.py:1097
  224.3 12.3 %collective-permute-start.16 = (bf16[512,384]{1,0:T(8,128)(2,1)}, bf16[512,384]{1,0:T(8,128)(2,1)}, u32[]{:S(2)}, u32[]{:S(2)}) collective-permute-start(bf16[512,384]{1,0:T(8,128)(2,1)} %dynamic-slice_bitcast_fusion.9), channel_id=1, source_target_pairs={{0,4},{2,6},{4,0},{6,2},{8,12},{10,14},{12,8},{14,10},{16,20},{18,... | collective-permute-start | bytes 1179656 | tf_op jit(solution)/shard_map/ppermute | solution.py:1097
  224.9 2.2 collective-permute-start.12
  227.1 42.0 %collective-permute-start.19 = (bf16[1152,384]{1,0:T(8,128)(2,1)}, bf16[1152,384]{1,0:T(8,128)(2,1)S(1)}, u32[]{:S(2)}, u32[]{:S(2)}) collective-permute-start(bf16[1152,384]{1,0:T(8,128)(2,1)} %dynamic-slice_bitcast_fusion.1), channel_id=1, source_target_pairs={{0,4},{2,6},{4,0},{6,2},{8,12},{10,14},{12,8},{14,10},{16,20},{18,... | collective-permute-start | bytes 2654216 | tf_op jit(solution)/shard_map/ppermute | solution.py:1097
  239.2 29.8 %collective-permute-start.18 = (bf16[576,384]{1,0:T(8,128)(2,1)S(1)}, bf16[576,384]{1,0:T(8,128)(2,1)S(1)}, u32[]{:S(2)}, u32[]{:S(2)}) collective-permute-start(bf16[576,384]{1,0:T(8,128)(2,1)S(1)} %dynamic-slice_bitcast_fusion.7), channel_id=1, source_target_pairs={{0,8},{2,10},{4,12},{6,14},{8,0},{10,2},{12,4},{14,6},{16,24},{18,... | collective-permute-start | bytes 1327112 | tf_op jit(solution)/shard_map/ppermute | solution.py:1097
  241.3 31.3 %collective-permute-start.13 = (bf16[1152,384]{1,0:T(8,128)(2,1)S(1)}, bf16[1152,384]{1,0:T(8,128)(2,1)}, u32[]{:S(2)}, u32[]{:S(2)}) collective-permute-start(bf16[1152,384]{1,0:T(8,128)(2,1)S(1)} %dynamic-slice_bitcast_fusion.2), channel_id=1, source_target_pairs={{0,2},{2,0},{4,6},{6,4},{8,10},{10,8},{12,14},{14,12},{16,18},{18,... | collective-permute-start | bytes 2654216 | tf_op jit(solution)/shard_map/ppermute | solution.py:1097
  244.8 24.2 %collective-permute-start.20 = (bf16[64,384]{1,0:T(8,128)(2,1)}, bf16[64,384]{1,0:T(8,128)(2,1)}, u32[]{:S(2)}, u32[]{:S(2)}) collective-permute-start(bf16[64,384]{1,0:T(8,128)(2,1)} %pad.4), channel_id=1, source_target_pairs={{0,4},{2,6},{4,0},{6,2},{8,12},{10,14},{12,8},{14,10},{16,20},{18,... | collective-permute-start | bytes 147464 | tf_op jit(solution)/shard_map/ppermute | solution.py:1325
  274.2 21.1 %collective-permute-start.22 = (bf16[64,384]{1,0:T(8,128)(2,1)}, bf16[64,384]{1,0:T(8,128)(2,1)}, u32[]{:S(2)}, u32[]{:S(2)}) collective-permute-start(bf16[64,384]{1,0:T(8,128)(2,1)} %add_convert_fusion.1), channel_id=1, source_target_pairs={{0,2},{2,0},{4,6},{6,4},{8,10},{10,8},{12,14},{14,12},{16,18},{18,... | collective-permute-start | bytes 147464 | tf_op jit(solution)/shard_map/ppermute | solution.py:1341
  275.0 21.2 %collective-permute-start.21 = (bf16[576,384]{1,0:T(8,128)(2,1)S(1)}, bf16[576,384]{1,0:T(8,128)(2,1)S(1)}, u32[]{:S(2)}, u32[]{:S(2)}) collective-permute-start(bf16[576,384]{1,0:T(8,128)(2,1)S(1)} %dynamic-slice_bitcast_fusion.6), channel_id=1, source_target_pairs={{0,2},{2,0},{4,6},{6,4},{8,10},{10,8},{12,14},{14,12},{16,18},{18,... | collective-permute-start | bytes 1327112 | tf_op jit(solution)/shard_map/ppermute | solution.py:1097
  277.2 18.9 %collective-permute-start.24 = (bf16[288,384]{1,0:T(8,128)(2,1)}, bf16[288,384]{1,0:T(8,128)(2,1)}, u32[]{:S(2)}, u32[]{:S(2)}) collective-permute-start(bf16[288,384]{1,0:T(8,128)(2,1)} %dynamic-slice_bitcast_fusion.11), channel_id=1, source_target_pairs={{0,16},{2,18},{4,20},{6,22},{8,24},{10,26},{12,28},{14,30},{16,0},... | collective-permute-start | bytes 663560 | tf_op jit(solution)/shard_map/ppermute | solution.py:1097
  279.5 16.8 %collective-permute-start.15 = (bf16[576,384]{1,0:T(8,128)(2,1)S(1)}, bf16[576,384]{1,0:T(8,128)(2,1)S(1)}, u32[]{:S(2)}, u32[]{:S(2)}) collective-permute-start(bf16[576,384]{1,0:T(8,128)(2,1)S(1)} %dynamic-slice_bitcast_fusion.8), channel_id=1, source_target_pairs={{0,4},{2,6},{4,0},{6,2},{8,12},{10,14},{12,8},{14,10},{16,20},{18,... | collective-permute-start | bytes 1327112 | tf_op jit(solution)/shard_map/ppermute | solution.py:1097
  296.6 18.2 %collective-permute-start.23 = (bf16[608,384]{1,0:T(8,128)(2,1)S(1)}, bf16[608,384]{1,0:T(8,128)(2,1)S(1)}, u32[]{:S(2)}, u32[]{:S(2)}) collective-permute-start(bf16[608,384]{1,0:T(8,128)(2,1)S(1)} %dynamic-slice_bitcast_fusion.5), channel_id=1, source_target_pairs={{0,8},{2,10},{4,12},{6,14},{8,0},{10,2},{12,4},{14,6},{16,24},{18,... | collective-permute-start | bytes 1400840 | tf_op jit(solution)/shard_map/ppermute | solution.py:1097
  298.2 14.8 %collective-permute-start.26 = (bf16[288,384]{1,0:T(8,128)(2,1)S(1)}, bf16[288,384]{1,0:T(8,128)(2,1)S(1)}, u32[]{:S(2)}, u32[]{:S(2)}) collective-permute-start(bf16[288,384]{1,0:T(8,128)(2,1)S(1)} %fusion.11), channel_id=1, source_target_pairs={{0,16},{2,18},{4,20},{6,22},{8,24},{10,26},{12,28},{14,30},{16,0},... | collective-permute-start | bytes 663560 | tf_op jit(solution)/shard_map/ppermute | solution.py:1107
  313.2 18.7 %collective-permute-start.28 = (bf16[576,384]{1,0:T(8,128)(2,1)S(1)}, bf16[576,384]{1,0:T(8,128)(2,1)S(1)}, u32[]{:S(2)}, u32[]{:S(2)}) collective-permute-start(bf16[576,384]{1,0:T(8,128)(2,1)S(1)} %maximum_select_fusion.7), channel_id=1, source_target_pairs={{0,8},{2,10},{4,12},{6,14},{8,0},{10,2},{12,4},{14,6},{16,24},{18,... | collective-permute-start | bytes 1327112 | tf_op jit(solution)/shard_map/ppermute | solution.py:1107
  314.9 17.0 %collective-permute-start.25 = (bf16[304,384]{1,0:T(8,128)(2,1)S(1)}, bf16[304,384]{1,0:T(8,128)(2,1)S(1)}, u32[]{:S(2)}, u32[]{:S(2)}) collective-permute-start(bf16[304,384]{1,0:T(8,128)(2,1)S(1)} %dynamic-slice_bitcast_fusion.10), channel_id=1, source_target_pairs={{0,16},{2,18},{4,20},{6,22},{8,24},{10,26},{12,28},{14,30},{16,0},... | collective-permute-start | bytes 700424 | tf_op jit(solution)/shard_map/ppermute | solution.py:1097
  331.9 16.6 %collective-permute-start.27 = (bf16[304,384]{1,0:T(8,128)(2,1)S(1)}, bf16[304,384]{1,0:T(8,128)(2,1)S(1)}, u32[]{:S(2)}, u32[]{:S(2)}) collective-permute-start(bf16[304,384]{1,0:T(8,128)(2,1)S(1)} %fusion.10), channel_id=1, source_target_pairs={{0,16},{2,18},{4,20},{6,22},{8,24},{10,26},{12,28},{14,30},{16,0},... | collective-permute-start | bytes 700424 | tf_op jit(solution)/shard_map/ppermute | solution.py:1107
  332.9 16.1 %collective-permute-start.30 = (bf16[512,384]{1,0:T(8,128)(2,1)S(1)}, bf16[512,384]{1,0:T(8,128)(2,1)S(1)}, u32[]{:S(2)}, u32[]{:S(2)}) collective-permute-start(bf16[512,384]{1,0:T(8,128)(2,1)S(1)} %bitcast.209), channel_id=1, source_target_pairs={{0,4},{2,6},{4,0},{6,2},{8,12},{10,14},{12,8},{14,10},{16,20},{18,... | collective-permute-start | bytes 1179656 | tf_op jit(solution)/shard_map/ppermute | solution.py:1107
  333.6 17.5 %collective-permute-start.31 = (bf16[640,384]{1,0:T(8,128)(2,1)S(1)}, bf16[640,384]{1,0:T(8,128)(2,1)S(1)}, u32[]{:S(2)}, u32[]{:S(2)}) collective-permute-start(bf16[640,384]{1,0:T(8,128)(2,1)S(1)} %bitcast.191), channel_id=1, source_target_pairs={{0,2},{2,0},{4,6},{6,4},{8,10},{10,8},{12,14},{14,12},{16,18},{18,... | collective-permute-start | bytes 1474568 | tf_op jit(solution)/shard_map/ppermute | solution.py:1107
  348.7 18.5 %collective-permute-start.29 = (bf16[608,384]{1,0:T(8,128)(2,1)S(1)}, bf16[608,384]{1,0:T(8,128)(2,1)}, u32[]{:S(2)}, u32[]{:S(2)}) collective-permute-start(bf16[608,384]{1,0:T(8,128)(2,1)S(1)} %maximum_select_fusion.6), channel_id=1, source_target_pairs={{0,8},{2,10},{4,12},{6,14},{8,0},{10,2},{12,4},{14,6},{16,24},{18,... | collective-permute-start | bytes 1400840 | tf_op jit(solution)/shard_map/ppermute | solution.py:1107
  349.4 17.8 %copy-start.4 = (bf16[1024,384]{1,0:T(8,128)(2,1)}, bf16[1024,384]{1,0:T(8,128)(2,1)S(1)}, u32[]{:S(2)}) copy-start(bf16[1024,384]{1,0:T(8,128)(2,1)S(1)} %maximum_select_fusion.5.mine_ref) | copy-start | bytes 2359300
  349.4 20.2 %collective-permute-start.33 = (bf16[1024,384]{1,0:T(8,128)(2,1)S(1)}, bf16[1024,384]{1,0:T(8,128)(2,1)}, u32[]{:S(2)}, u32[]{:S(2)}) collective-permute-start(bf16[1024,384]{1,0:T(8,128)(2,1)S(1)} %maximum_select_fusion.5.mine_ref), channel_id=1, source_target_pairs={{0,2},{2,0},{4,6},{6,4},{8,10},{10,8},{12,14},{14,12},{16,18},{18,... | collective-permute-start | bytes 2359304 | tf_op jit(solution)/shard_map/ppermute | solution.py:1370
  351.5 23.5 %collective-permute-start.34 = (bf16[1280,384]{1,0:T(8,128)(2,1)S(1)}, bf16[1280,384]{1,0:T(8,128)(2,1)S(1)}, u32[]{:S(2)}, u32[]{:S(2)}) collective-permute-start(bf16[1280,384]{1,0:T(8,128)(2,1)S(1)} %maximum_select_fusion.mine_ref), channel_id=1, source_target_pairs={{0,4},{2,6},{4,0},{6,2},{8,12},{10,14},{12,8},{14,10},{16,20},{18,... | collective-permute-start | bytes 2949128 | tf_op jit(solution)/shard_map/ppermute | solution.py:1370
  368.7 11.0 %collective-permute-start.36 = (bf16[576,384]{1,0:T(8,128)(2,1)S(1)}, bf16[576,384]{1,0:T(8,128)(2,1)S(1)}, u32[]{:S(2)}, u32[]{:S(2)}) collective-permute-start(bf16[576,384]{1,0:T(8,128)(2,1)S(1)} %bitcast.200), channel_id=1, source_target_pairs={{0,2},{2,0},{4,6},{6,4},{8,10},{10,8},{12,14},{14,12},{16,18},{18,... | collective-permute-start | bytes 1327112 | tf_op jit(solution)/shard_map/ppermute | solution.py:1107
  368.9 11.6 %collective-permute-start.32 = (bf16[576,384]{1,0:T(8,128)(2,1)S(1)}, bf16[576,384]{1,0:T(8,128)(2,1)S(1)}, u32[]{:S(2)}, u32[]{:S(2)}) collective-permute-start(bf16[576,384]{1,0:T(8,128)(2,1)S(1)} %bitcast.202), channel_id=1, source_target_pairs={{0,4},{2,6},{4,0},{6,2},{8,12},{10,14},{12,8},{14,10},{16,20},{18,... | collective-permute-start | bytes 1327112 | tf_op jit(solution)/shard_map/ppermute | solution.py:1107
  380.8 18.2 %copy-start.2 = (bf16[1152,384]{1,0:T(8,128)(2,1)}, bf16[1152,384]{1,0:T(8,128)(2,1)S(1)}, u32[]{:S(2)}) copy-start(bf16[1152,384]{1,0:T(8,128)(2,1)S(1)} %maximum_select_fusion.3.mine_ref) | copy-start | bytes 2654212
  380.8 18.2 %collective-permute-start.35 = (bf16[1152,384]{1,0:T(8,128)(2,1)S(1)}, bf16[1152,384]{1,0:T(8,128)(2,1)S(1)}, u32[]{:S(2)}, u32[]{:S(2)}) collective-permute-start(bf16[1152,384]{1,0:T(8,128)(2,1)S(1)} %maximum_select_fusion.3.mine_ref), channel_id=1, source_target_pairs={{0,2},{2,0},{4,6},{6,4},{8,10},{10,8},{12,14},{14,12},{16,18},{18,... | collective-permute-start | bytes 2654216 | tf_op jit(solution)/shard_map/ppermute | solution.py:1386
  382.1 16.9 %copy-start.3 = (bf16[1152,384]{1,0:T(8,128)(2,1)}, bf16[1152,384]{1,0:T(8,128)(2,1)S(1)}, u32[]{:S(2)}) copy-start(bf16[1152,384]{1,0:T(8,128)(2,1)S(1)} %maximum_select_fusion.4.mine_ref) | copy-start | bytes 2654212
  382.1 18.6 %collective-permute-start.37 = (bf16[1152,384]{1,0:T(8,128)(2,1)S(1)}, bf16[1152,384]{1,0:T(8,128)(2,1)S(1)}, u32[]{:S(2)}, u32[]{:S(2)}) collective-permute-start(bf16[1152,384]{1,0:T(8,128)(2,1)S(1)} %maximum_select_fusion.4.mine_ref), channel_id=1, source_target_pairs={{0,4},{2,6},{4,0},{6,2},{8,12},{10,14},{12,8},{14,10},{16,20},{18,... | collective-permute-start | bytes 2654216 | tf_op jit(solution)/shard_map/ppermute | solution.py:1386
  (19 other events, 65.4 us)
Sparse Core Ops, SparseCore 0:
  89.3 117.8 all-gather.1
where the time goes:
time: 424 us; the launch traced here: 416 us
  Pallas kernels  243 us (57%)
  starting transfers between devices  71.2 us (17%)
  waiting for transfers between devices  39 us (9%)
  local copies, waits for them, and re-layouts  29.6 us (7%)
  other arithmetic  18 us (4%)
  between operations  15 us (4%)
    pallas_call x7, Pallas kernels, heavy_weights(): pl.pallas_call(lambda *refs: heavy_weights_kernel(tile, *refs), grid=(cou...  109 us
    ppermute x12, waiting for transfers between devices, scatter_start(): return (kept, lax.ppermute(sent, 'seq', bit_pairs(bit)))  25.9 us
    all_to_all x4, starting transfers between devices, exchange(): return lax.all_to_all(pairs, 'seq', split_axis=0, concat_axis=0, tiled=True)  22.5 us
    ppermute x12, starting transfers between devices, scatter_start(): return (kept, lax.ppermute(sent, 'seq', bit_pairs(bit)))  22.2 us
    pallas_call x1, Pallas kernels, feed(): pl.pallas_call(feed_kernel, grid=(heavy_out.shape[1] // cols,), in_specs=...  20.6 us
    pallas_call x4, Pallas kernels, finish_call(): pl.pallas_call(kernel, in_specs=[pl.BlockSpec(memory_space=pltpu.SMEM), p...  14.9 us
    pallas_call x1, Pallas kernels, heavy_project(): pl.pallas_call(heavy_project_kernel, grid=(low.shape[0],), in_specs=[each...  13.6 us
    pallas_call x1, Pallas kernels, light_forward(): pl.pallas_call(lambda *refs: light_forward_kernel(1.0 / math.sqrt(LHD), *...  13.2 us
  transfers between devices with their start and end apart: 43, of which 12 were waited for; matrix products, arithmetic and copies ran while one was open for 9% of the time, Pallas kernels for 52%

commit v1 on v0

--- a/solution.py
+++ b/solution.py
@@ -645,7 +645,7 @@
 
 def feed_kernel(
     low_ref, rows_ref, slot_ref, kept_ref, up_ref, slots_ref, in_ref, out_ref, heavy_in_ref,
-    heavy_out_ref, part_ref, weights_ref, gate_ref, heavy_acc, back_acc, hidden_ref, dgate_ref, dup_ref,
+    heavy_out_ref, part_ref, weights_ref, down_ref, gate_ref, heavy_acc, back_acc, hidden_ref, dgate_ref, dup_ref,
 ):
     step = pl.program_id(0)
     seqs, length, width = up_ref.shape
@@ -698,7 +698,7 @@
         up = up_ref[...].reshape(seqs * length, width)
         pack_wide(weights_ref.at[0], cols_dot(low, dgate_ref[...]))
         pack_wide(weights_ref.at[1], cols_dot(low, dup_ref[...]))
-        pack_wide(weights_ref.at[2], cols_dot(up, hidden_ref[...]))
+        pack_wide(down_ref, cols_dot(up, hidden_ref[...]))
 
 
 def feed(low, rows, slot, kept, up, slots, light_in, light_out, heavy_in, heavy_out, packed_cols):
@@ -709,7 +709,8 @@
     rows, slot = rows.reshape(-1, width), slot.reshape(-1, width)
     shapes = [
         like((2, seqs, length, width), LOW),
-        like((3, width * hidden // packed_cols, packed_cols), LOW),
+        like((2, width * hidden // packed_cols, packed_cols), LOW),
+        like((width * hidden // packed_cols, packed_cols), LOW),
         like((seqs, cap, LANES), WIDE),
     ]
     return pl.pallas_call(
@@ -868,15 +869,13 @@
 
 def heavy_project_kernel(
     light_part_ref, low_ref, pairs_ref, heavy_ref, slots_ref, gate_ref, raw_ref, logit_ref,
-    lead_ref, tail_ref, light_ref, light_sum_ref,
-    grad_ref, light_grad_ref, part_ref, both_logit_ref, grad_acc, light_acc,
+    grad_ref, part_ref, both_logit_ref, grad_acc,
 ):
     step = pl.program_id(0)
 
     @pl.when(step == 0)
     def _():
         grad_acc[...] = jnp.zeros_like(grad_acc)
-        light_acc[...] = light_sum_ref[1:]
 
     low = low_ref[0]
     length = low.shape[0]
@@ -901,59 +900,78 @@
     part = part + place_rows(
         hot_key, rows_dot(key_grad, heavy_ref[1]) + rows_dot(raw_grad, heavy_ref[2])
     )
-    edges = []
-    for ref, rows in ((lead_ref, slice(0, WIN)), (tail_ref, slice(length - WIN, length))):
-        for kind in range(2):
-            light_acc[kind] += cols_dot(low[rows], ref[0, kind])
-        edges.append(rows_dot(ref[0, 0], light_ref[1]) + rows_dot(ref[0, 1], light_ref[2]))
-    part_ref[0, :WIN] = (part[:WIN] + edges[0]).astype(LOW)
-    part_ref[0, WIN : length - WIN] = part[WIN : length - WIN].astype(LOW)
-    part_ref[0, length - WIN :] = (part[length - WIN :] + edges[1]).astype(LOW)
+    part_ref[0] = part
 
     @pl.when(step == pl.num_programs(0) - 1)
     def _():
         grad_ref[...] = grad_acc[...].astype(LOW)
-        light_grad_ref[0] = light_sum_ref[0].astype(LOW)
-        light_grad_ref[1:] = light_acc[...].astype(LOW)
-
-
-def heavy_project(
-    light_part, low, pairs, heavy, slots, gate, raw, logit, lead, tail, light, light_sum
-):
+
+
+def heavy_project(light_part, low, pairs, heavy, slots, gate, raw, logit):
     heads = heavy.shape[2] // HHD
-    shapes = [
-        like(heavy.shape, LOW),
-        like(light.shape, LOW),
-        like(low.shape, LOW),
-        like(logit.shape, WIDE),
-    ]
+    shapes = [like(heavy.shape, LOW), like(low.shape, WIDE), like(logit.shape, WIDE)]
     return pl.pallas_call(
         heavy_project_kernel,
         grid=(low.shape[0],),
         in_specs=[
             each(light_part), each(low), pair_spec(pairs, heads), whole(heavy), each(slots),
-            each(gate), each(raw), each(logit), each(lead), each(tail), whole(light),
-            whole(light_sum),
+            each(gate), each(raw), each(logit),
         ],
-        out_specs=[whole(shapes[0]), whole(shapes[1]), each(shapes[2]), each(shapes[3])],
+        out_specs=[whole(shapes[0]), each(shapes[1]), each(shapes[2])],
         out_shape=shapes,
-        scratch_shapes=[
-            pltpu.VMEM(heavy.shape, WIDE),
-            pltpu.VMEM((2,) + light.shape[1:], WIDE),
-        ],
+        scratch_shapes=[pltpu.VMEM(heavy.shape, WIDE)],
         compiler_params=params(),
-        cost_estimate=cost(11),
+        cost_estimate=cost(10),
         name="heavy_project",
-    )(light_part, low, pairs, heavy, slots, gate, raw, logit, lead, tail, light, light_sum)
+    )(light_part, low, pairs, heavy, slots, gate, raw, logit)
+
+
+def edge_project_kernel(
+    part_in_ref, low_ref, lead_ref, tail_ref, light_ref, sum_ref, grad_ref, part_ref, grad_acc
+):
+    step = pl.program_id(0)
+
+    @pl.when(step == 0)
+    def _():
+        grad_acc[...] = sum_ref[1:]
+
+    length = low_ref.shape[1]
+    part_ref[0, WIN : length - WIN, :] = part_in_ref[0, WIN : length - WIN, :].astype(LOW)
+    for ref, rows in ((lead_ref, slice(0, WIN)), (tail_ref, slice(length - WIN, length))):
+        for kind in range(2):
+            grad_acc[kind] += cols_dot(low_ref[0, rows, :], ref[0, kind])
+        more = rows_dot(ref[0, 0], light_ref[1]) + rows_dot(ref[0, 1], light_ref[2])
+        part_ref[0, rows, :] = (part_in_ref[0, rows, :] + more).astype(LOW)
+
+    @pl.when(step == pl.num_programs(0) - 1)
+    def _():
+        grad_ref[0] = sum_ref[0].astype(LOW)
+        grad_ref[1:] = grad_acc[...].astype(LOW)
+
+
+def edge_project(part, low, lead, tail, light, light_sum):
+    shapes = [like(light.shape, LOW), like(low.shape, LOW)]
+    return pl.pallas_call(
+        edge_project_kernel,
+        grid=(low.shape[0],),
+        in_specs=[each(part), each(low), each(lead), each(tail), whole(light), whole(light_sum)],
+        out_specs=[whole(shapes[0]), each(shapes[1])],
+        out_shape=shapes,
+        scratch_shapes=[pltpu.VMEM((2,) + light.shape[1:], WIDE)],
+        compiler_params=params(),
+        cost_estimate=cost(5),
+        name="edge_project",
+    )(part, low, lead, tail, light, light_sum)
 
 
 def input_kernel(
     part_ref, other_ref, logit_ref, logit_other_ref, gate_ref, slots_ref, tokens_ref, gains_ref,
-    routers_ref, middle_ref, small_in_ref, grad_ref, small_ref,
+    routers_ref, middle_ref, small_in_ref, grad_ref, rows_ref, small_ref,
 ):
     @pl.when(pl.program_id(0) == 0)
     def _():
         small_ref[...] = small_in_ref[...]
+        rows_ref[...] = jnp.zeros_like(rows_ref)
 
     slots = slots_ref[0]
     cap = slots.shape[0]
@@ -982,9 +1000,18 @@
     small_ref[4:5, :] += jnp.sum(key_token * normed, axis=0, keepdims=True)
     grad_ref[0] = middle_ref[0] + norm_back(inputs, factor, normed_grad * gains_ref[0:1, :])
 
-
-def input_back(part, other, logit, logit_other, gate, slots, tokens, gains, routers, middle, small):
-    shapes = [like(middle.shape, WIDE), like(small.shape, WIDE)]
+    @pl.when(pl.program_id(0) == pl.num_programs(0) - 1)
+    def _():
+        cols = rows_ref.shape[1]
+        sums = small_ref[...]
+        folded = jnp.concatenate([sums[:, :cols], sums[:, cols:]], axis=0)
+        rows_ref[: folded.shape[0], :] = folded.astype(LOW)
+
+
+def input_back(
+    part, other, logit, logit_other, gate, slots, tokens, gains, routers, middle, small, rows
+):
+    shapes = [like(middle.shape, WIDE), like((rows, small.shape[1] // 2), LOW)]
     return pl.pallas_call(
         input_kernel,
         grid=(tokens.shape[0],),
@@ -994,6 +1021,7 @@
         ],
         out_specs=[each(shapes[0]), whole(shapes[1])],
         out_shape=shapes,
+        scratch_shapes=[pltpu.VMEM(small.shape, WIDE)],
         compiler_params=params(),
         cost_estimate=cost(6),
         name="input_back",
@@ -1190,6 +1218,20 @@
         wide_ref[half:, :] = second_ref[...].astype(WIDE)
 
     in_order(bit_ref, mine_ref, got_ref, body)
+
+
+def widen(bit, mine, got, name):
+    rows, cols = mine.shape
+    half = pl.BlockSpec((rows, LANES), lambda i: (0, i))
+    return pl.pallas_call(
+        kinds_kernel,
+        grid=(cols // LANES,),
+        in_specs=[pl.BlockSpec(memory_space=pltpu.SMEM), half, half],
+        out_specs=pl.BlockSpec((2 * rows, LANES), lambda i: (0, i)),
+        out_shape=like((2 * rows, cols), WIDE),
+        compiler_params=params(24),
+        name=name,
+    )(bit_here(bit).astype(jnp.int32).reshape(1, 1), mine, got)
 
 
 def other_core(value):
@@ -1271,17 +1313,17 @@
     all_slots = seq_count * capacity * seq_devices
     gather_heavy = 2 * all_slots * width < 4 * (heavy_mlp_in.size + heavy_mlp_out.size)
     here = lax.all_gather(ship, "seq", axis=1, tiled=True) if gather_heavy else ship
-    part, feed_grads, mlp = feed(
+    part, feed_grads, down_grad, mlp = feed(
         low_two, rows, slot, gate_two, out_grad, slots, light_in, light_feedforward_output_weight,
         heavy_in, heavy_mlp_out, light_cols,
     )
     beyond, mlp_other = other_core(part), other_core(mlp)
     bits = (seq_devices - 1).bit_length()
     blocks = 1 << (bits - 2)
-    first_going = scatter_start(feed_grads[:2].reshape(-1, light_cols), 0)
+    first_going = scatter_start(feed_grads.reshape(-1, light_cols), 0)
     mixed, middle_grad, mix_grad, grad_pairs, out_grads, small, query_logit = middle_back(
         tokens, own, other, part, beyond, out_grad, gain_rows, router_rows, slots, gate, mlp,
-        mlp_other, mix, heavy_mix, light_attention_output_weight, heavy_out, feed_grads[2], seq_devices,
+        mlp_other, mix, heavy_mix, light_attention_output_weight, heavy_out, down_grad, seq_devices,
     )
     pair_grad = exchange(grad_pairs)
     local, early, late = light_backward(place, query, window, lse, mix_grad)
@@ -1293,10 +1335,12 @@
     triple_pairs = exchange(triple)
     second_going = scatter_start(after(out_grads, triple), 1)
     light_sums, light_part = light_project(after(local, triple), low, light_weights)
-    second_wave = scatter_end(second_going, light_part)
-    heavy_grads, light_grads, low_part, logit = heavy_project(
-        light_part, low, after(triple_pairs, second_wave), heavy_weights_qkv, slots, gate, raw,
-        query_logit, lead, tail, light_weights, light_sums,
+    heavy_grads, part_sum, logit = heavy_project(
+        light_part, low, triple_pairs, heavy_weights_qkv, slots, gate, raw, query_logit
+    )
+    second_wave = scatter_end(second_going, part_sum)
+    light_grads, low_part = edge_project(
+        after(part_sum, second_wave), low, lead, tail, light_weights, light_sums
     )
     heavy_going = scatter_start(heavy_grads.reshape(-1, light_cols), 1)
     light_going = scatter_start(light_grads.reshape(-1, light_cols), 0)
@@ -1316,12 +1360,10 @@
         blocks_done[0] += count
         return heavy_sums[1]
 
-    input_grad, small = input_back(
+    input_grad, small_rows = input_back(
         low_part, low_other, logit, logit_other, gate, slots, tokens, gain_rows,
-        router_rows, middle_grad, small,
-    )
-    small_rows = small.astype(LOW).reshape(-1, light_cols)
-    small_rows = jnp.pad(small_rows, ((0, 16 * blocks - small_rows.shape[0]), (0, 0)))
+        router_rows, middle_grad, small, 16 * blocks,
+    )
     small_got = lax.ppermute(small_rows, "seq", bit_pairs(1))
     second_wave = scatter_end(second_going, input_grad)
     first_wave = scatter_end(first_going, input_grad)
@@ -1376,7 +1418,7 @@
     late_going = [gather_start(p, bit) for p, bit in zip(late_wave, (1, 0))]
     early_halves = [(after(p, *late_wave), after(got, mark)) for p, got in early_halves]
     hidden = light_feedforward_output_weight.shape[1]
-    square, kinds = (width, light_cols), [(3 * width, light_cols)]
+    square = (width, light_cols)
     (feed_in,) = finish_call(feed_in_kernel, 0, *early_halves[0], [(width, 2, hidden)], "feed_in")
     feed_out, light_out_sum, heavy_out_sum = finish_call(
         outs_kernel, 1, *early_halves[1], [(width, hidden), square, square], "outs"
@@ -1397,9 +1439,9 @@
             sums = [gather_end(gather_start(p, bit)) for p in sums]
         heavy_in_grad = jnp.stack(sums[:2], axis=1).astype(WIDE)
         heavy_out_grad = sums[2].astype(WIDE)
-    (light_sum,) = finish_call(kinds_kernel, 0, *late_halves[0], kinds, "light_sum")
-    (heavy_sum,) = finish_call(kinds_kernel, 1, *late_halves[1], kinds, "heavy_sum")
-    small_sum = small_sum[: 8 * width // light_cols].reshape(8, width)
+    light_sum = widen(0, *late_halves[0], "light_sum")
+    heavy_sum = widen(1, *late_halves[1], "heavy_sum")
+    small_sum = jnp.concatenate([small_sum[:8], small_sum[8:16]], axis=1)
     return (
         mixed,
         input_grad,

time: 424 us -> 414 us (0.976)
  waiting for transfers between devices: 39 us -> 30.6 us
    ppermute x12, waiting for transfers between devices: 25.9 us -> 11.7 us  [scatter_start(): return (kept, lax.ppermute(sent, 'seq', bit_pairs(bit)))]
    pallas_call x0 -> x3, Pallas kernels: none -> 12.9 us  [the longest x1 8.01 us: edge_project(): pl.pallas_call(edge_project_kernel, grid=(low.shape[0],), in_specs=[each(...]
    pallas_call x4 -> x2, Pallas kernels: 14.9 us -> 7.96 us  [finish_call(): pl.pallas_call(kernel, in_specs=[pl.BlockSpec(memory_space=pltpu.SMEM), p...]
    pallas_call x1, Pallas kernels: 13.6 us -> 8.82 us  [heavy_project(): pl.pallas_call(heavy_project_kernel, grid=(low.shape[0],), in_specs=[each...]
    all_to_all x4, waiting for transfers between devices: 3.82 us -> 8.3 us  [exchange(): return lax.all_to_all(pairs, 'seq', split_axis=0, concat_axis=0, tiled=True)]
  transfers between devices with their start and end apart: 43 -> 43, of which waited for: 12 -> 14; matrix products, arithmetic and copies ran while one was open for 9% -> 8% of each run, Pallas kernels for 52% -> 54%
where the time goes in v1:
time: 414 us; the launch traced here: 406 us
  Pallas kernels  244 us (59%)
  starting transfers between devices  71.7 us (17%)
  waiting for transfers between devices  30.6 us (7%)
  local copies, waits for them, and re-layouts  27.3 us (7%)
  other arithmetic  17.4 us (4%)
  between operations  14.9 us (4%)
    pallas_call x7, Pallas kernels, heavy_weights(): pl.pallas_call(lambda *refs: heavy_weights_kernel(tile, *refs), grid=(cou...  109 us
    all_to_all x4, starting transfers between devices, exchange(): return lax.all_to_all(pairs, 'seq', split_axis=0, concat_axis=0, tiled=True)  24 us
    ppermute x12, starting transfers between devices, scatter_start(): return (kept, lax.ppermute(sent, 'seq', bit_pairs(bit)))  22.5 us
    pallas_call x1, Pallas kernels, feed(): pl.pallas_call(feed_kernel, grid=(heavy_out.shape[1] // cols,), in_specs=...  20.7 us
    pallas_call x1, Pallas kernels, light_forward(): pl.pallas_call(lambda *refs: light_forward_kernel(1.0 / math.sqrt(LHD), *...  13.2 us
    pallas_call x1, Pallas kernels, middle_back(): pl.pallas_call(middle_kernel, grid=(seqs,), in_specs=[each(tokens), each(...  12 us
    ppermute x12, waiting for transfers between devices, scatter_start(): return (kept, lax.ppermute(sent, 'seq', bit_pairs(bit)))  11.7 us
    ppermute x4, starting transfers between devices, to_neighbours(): return (lax.ppermute(last, 'seq', up), lax.ppermute(first, 'seq', down))  11.4 us
  transfers between devices with their start and end apart: 43, of which 14 were waited for; matrix products, arithmetic and copies ran while one was open for 8% of the time, Pallas kernels for 54%

profile of v1, /device:TPU:0, one launch (start us, length us, event | category | flops | bytes accessed | tf_op | source)
XLA Modules:
  0.0 406.1 jit_solution(12674359954420731828)
XLA Ops:
  9.5 5.5 %collective-permute-start = (bf16[128,768]{1,0:T(8,128)(2,1)S(1)}, bf16[128,768]{1,0:T(8,128)(2,1)S(1)}, u32[]{:S(2)}, u32[]{:S(2)}) collective-permute-start(bf16[128,768]{1,0:T(8,128)(2,1)S(1)} %get-tuple-element.233), channel_id=1, source_target_pairs={{0,2},{2,4},{4,6},{6,8},{8,10},{10,12},{12,14},{14,16},{16,18},{18... | collective-permute-start | bytes 589832 | tf_op jit(solution)/shard_map/ppermute | solution.py:1245
  17.4 5.5 %front.1 = (bf16[2,384,768]{2,1,0:T(8,128)(2,1)}, bf16[16,144,128]{2,1,0:T(8,128)(2,1)}, f32[2,96,384]{2,1,0:T(8,128)}, f32[2,96,128]{2,1,0:T(8,128)}) custom-call(bf16[2,384,768]{2,1,0:T(8,128)(2,1)} %tokens_ref.7, f32[2,768]{1,0:T(2,128)} %bitcast.205, f32[3,768]{1,0:T(4,128)} %bitcast.201, s32[2,96,6]{2,1,0:T(8,128)} %copy.48.slots_ref, ...), custom_call_target="tpu_custom_call" | custom-call | flops 160000000 | bytes 1024 | tf_op jit(solution)/shard_map/front/pallas_call | solution.py:237
  26.3 7.9 %all-to-all-start = ((bf16[16,144,128]{2,1,0:T(8,128)(2,1)}), bf16[16,144,128]{2,1,0:T(8,128)(2,1)S(1)}, u32[]{:S(2)}, u32[]{:S(2)}) async-start(bf16[16,144,128]{2,1,0:T(8,128)(2,1)} %get-tuple-element.126), calls=%async_computation | async-start | bytes 1179648 | tf_op jit(solution)/shard_map/all_to_all | solution.py:1249
  34.8 13.2 %light_forward.1 = (bf16[2,384,384]{2,1,0:T(8,128)(2,1)}, f32[2,384,768]{2,1,0:T(8,128)}, f32[2,384,128]{2,1,0:T(8,128)}, bf16[2,384,512]{2,1,0:T(8,128)(2,1)}, bf16[2,2,640,512]{3,2,1,0:T(8,128)(2,1)}) custom-call(s32[1,2]{1,0:T(1,128)} %add_bitcast_fusion.refs_0_, bf16[2,384,768]{2,1,0:T(8,128)(2,1)} %get-tuple-element.123.refs_1_.low_ref, ...), custom_call_target="tpu_custom_call" | custom-call | flops 300000000 | bytes 1024 | tf_op jit(solution)/shard_map/light_forward/pallas_call | solution.py:318
  48.0 2.8 all-to-all-done.refs_0_
  51.5 9.9 %heavy_forward.1 = (bf16[1536,128]{1,0:T(8,128)(2,1)}, bf16[1536,128]{1,0:T(8,128)(2,1)}, bf16[1536,128]{1,0:T(8,128)(2,1)}, f32[1536,128]{1,0:T(8,128)}, bf16[16,48,128]{2,1,0:T(8,128)(2,1)}) custom-call(bf16[16,144,128]{2,1,0:T(8,128)(2,1)} %copy-done.4), custom_call_target="tpu_custom_call" | custom-call | flops 140000000 | bytes 1024 | tf_op jit(solution)/shard_map/heavy_forward/pallas_call | solution.py:503
  61.5 4.2 %all-to-all-start.1 = ((bf16[16,48,128]{2,1,0:T(8,128)(2,1)}), bf16[16,48,128]{2,1,0:T(8,128)(2,1)S(1)}, u32[]{:S(2)}, u32[]{:S(2)}) async-start(bf16[16,48,128]{2,1,0:T(8,128)(2,1)} %get-tuple-element.129), calls=%async_computation.1 | async-start | bytes 393216 | tf_op jit(solution)/shard_map/all_to_all | solution.py:1249
  67.3 8.3 %copy.59 = bf16[768,2,2048]{2,0,1:T(8,128)(2,1)} copy(bf16[768,2,2048]{2,1,0:T(2,128)(2,1)} %param.26) | data formatting | bytes 12582912 | tf_op jit(solution)/shard_map/optimization_barrier | solution.py:1117
  76.3 4.0 combine.1
  80.3 3.0 collective-permute-done.4.other_ref
  84.3 4.8 %mlp_slots.1 = (bf16[2,384,768]{2,1,0:T(8,128)(2,1)}, bf16[2,96,768]{2,1,0:T(8,128)(2,1)}, bf16[2,96,768]{2,1,0:T(8,128)(2,1)}, bf16[2,96,768]{2,1,0:T(8,128)(2,1)}, f32[2,96,128]{2,1,0:T(8,128)}) custom-call(s32[1,1]{1,0:T(1,128)} %bitcast.18.core_ref.refs_0_, bf16[2,384,768]{2,1,0:T(8,128)(2,1)} %tokens_ref.7, ...), custom_call_target="tpu_custom_call" | custom-call | flops 100000000 | bytes 1024 | tf_op jit(solution)/shard_map/mlp_slots/pallas_call | solution.py:607
  89.1 20.7 %feed.1 = (bf16[2,2,384,768]{3,2,1,0:T(8,128)(2,1)}, bf16[2,1024,384]{2,1,0:T(8,128)(2,1)}, bf16[1024,384]{1,0:T(8,128)(2,1)}, f32[2,96,128]{2,1,0:T(8,128)}) custom-call(bf16[2,384,768]{2,1,0:T(8,128)(2,1)} %get-tuple-element.136.low_ref, bf16[192,768]{1,0:T(8,128)(2,1)} %bitcast.194, bf16[192,768]{1,0:T(8,128)(2,1)} %bitcast.195, ...), custom_call_target="tpu_custom_call" | custom-call | flops 400000000 | bytes 1024 | tf_op jit(solution)/shard_map/feed/pallas_call | solution.py:716
  109.9 2.1 dynamic-slice_bitcast_fusion.3
  112.0 2.0 collective-permute-start.7
  116.9 12.0 %middle_back.1 = (bf16[2,384,768]{2,1,0:T(8,128)(2,1)}, f32[2,384,768]{2,1,0:T(8,128)}, bf16[2,384,384]{2,1,0:T(8,128)(2,1)}, bf16[16,48,128]{2,1,0:T(8,128)(2,1...) custom-call(bf16[2,384,768]{2,1,0:T(8,128)(2,1)} %tokens_ref.7, ...), custom_call_target="tpu_custom_call" | custom-call | flops 220000000 | bytes 1024 | tf_op jit(solution)/shard_map/middle_back/pallas_call | solution.py:821
  129.0 6.3 %all-to-all-start.2 = ((bf16[16,48,128]{2,1,0:T(8,128)(2,1)}), bf16[16,48,128]{2,1,0:T(8,128)(2,1)S(1)}, u32[]{:S(2)}, u32[]{:S(2)}) async-start(bf16[16,48,128]{2,1,0:T(8,128)(2,1)} %get-tuple-element.154), calls=%async_computation.2 | async-start | bytes 393216 | tf_op jit(solution)/shard_map/all_to_all | solution.py:1249
  135.3 10.3 %light_backward.1 = (bf16[2,3,384,384]{3,2,1,0:T(8,128)(2,1)}, bf16[2,2,128,384]{3,2,1,0:T(8,128)(2,1)}, bf16[2,2,128,384]{3,2,1,0:T(8,128)(2,1)}) custom-call(s32[1,2]{1,0:T(1,128)} %add_bitcast_fusion.refs_0_, bf16[2,384,512]{2,1,0:T(8,128)(2,1)} %get-tuple-element.146.refs_1_, bf16[2,2,640,512]{3,2,1,0:T(8,128)(2,1)} %get-tuple-element.147.refs_2_, ...), custom_call_target="tpu_custom_call" | custom-call | flops 280000000 | bytes 1024 | tf_op jit(solution)/shard_map/light_backward/pallas_call | solution.py:388
  147.8 9.7 %heavy_backward.1 = bf16[16,144,128]{2,1,0:T(8,128)(2,1)} custom-call(bf16[1536,128]{1,0:T(8,128)(2,1)} %get-tuple-element.151.refs_0_, bf16[1536,128]{1,0:T(8,128)(2,1)} %get-tuple-element.152.refs_1_, bf16[1536,128]{1,0:T(8,128)(2,1)} %get-tuple-element.153.refs_2_, f32[1536,128]{1,0:T(8,128)} %get-tuple-element.130.refs_3_, bf16[16,48,128]{2,1,0:T(8,128)(2,1)} %copy-done.15), custom_call_target="tpu_custom_call" | custom-call | flops 200000000 | bytes 1024 | tf_op jit(solution)/shard_map/heavy_backward/pallas_call | solution.py:524
  157.5 5.7 %all-to-all-start.3 = ((bf16[16,144,128]{2,1,0:T(8,128)(2,1)}), bf16[16,144,128]{2,1,0:T(8,128)(2,1)S(1)}, u32[]{:S(2)}, u32[]{:S(2)}) async-start(bf16[16,144,128]{2,1,0:T(8,128)(2,1)} %heavy_backward.1), calls=%async_computation.3 | async-start | bytes 1179648 | tf_op jit(solution)/shard_map/all_to_all | solution.py:1249
  164.2 1.9 collective-permute-start.8
  166.2 3.4 collective-permute-start.9
  170.8 9.3 %light_project.1 = (f32[3,768,384]{2,1,0:T(8,128)}, f32[2,384,768]{2,1,0:T(8,128)}) custom-call(bf16[2,3,384,384]{3,2,1,0:T(8,128)(2,1)} %get-tuple-element.158.local_ref, bf16[2,384,768]{2,1,0:T(8,128)(2,1)} %get-tuple-element.123.refs_1_.low_ref, bf16[3,768,384]{2,1,0:T(8,128)(2,1)} %bitcast.149), custom_call_target="tpu_custom_call" | custom-call | flops 180000000 | bytes 1024 | tf_op jit(solution)/shard_map/light_project/pallas_call | solution.py:858
  180.1 4.2 %all-to-all-done.3.pairs_ref = bf16[16,144,128]{2,1,0:T(8,128)(2,1)S(1)} async-done(((bf16[16,144,128]{2,1,0:T(8,128)(2,1)}), bf16[16,144,128]{2,1,0:T(8,128)(2,1)S(1)}, u32[]{:S(2)}, u32[]{:S(2)}) %all-to-all-start.3) | async-done | bytes 589856 | tf_op jit(solution)/shard_map/all_to_all | solution.py:1249
  185.2 8.8 %heavy_project.1 = (bf16[3,768,384]{2,1,0:T(8,128)(2,1)}, f32[2,384,768]{2,1,0:T(8,128)}, f32[2,96,128]{2,1,0:T(8,128)}) custom-call(f32[2,384,768]{2,1,0:T(8,128)} %get-tuple-element.159.light_part_ref, bf16[2,384,768]{2,1,0:T(8,128)(2,1)} %get-tuple-element.123.refs_1_.low_ref, bf16[16,144,128]{2,1,0:T(8,128)(2,1)} %copy-done.3, ...), custom_call_target="tpu_custom_call" | custom-call | flops 200000000 | bytes 1024 | tf_op jit(solution)/shard_map/heavy_project/pallas_call | solution.py:913
  194.0 10.8 %collective-permute-done.8 = bf16[1280,384]{1,0:T(8,128)(2,1)S(1)} collective-permute-done((bf16[1280,384]{1,0:T(8,128)(2,1)}, bf16[1280,384]{1,0:T(8,128)(2,1)S(1)}, u32[]{:S(2)}, u32[]{:S(2)}) %collective-permute-start.8) | collective-permute-done | bytes 983072 | tf_op jit(solution)/shard_map/ppermute | solution.py:1125
  206.0 8.0 %edge_project.1 = (bf16[3,768,384]{2,1,0:T(8,128)(2,1)}, bf16[2,384,768]{2,1,0:T(8,128)(2,1)}) custom-call(f32[2,384,768]{2,1,0:T(8,128)} %get-tuple-element.166.part_in_ref, bf16[2,384,768]{2,1,0:T(8,128)(2,1)} %get-tuple-element.123.refs_1_.low_ref, bf16[2,2,128,384]{3,2,1,0:T(8,128)(2,1)} %copy-done.18, bf16[2,2,128,384]{3,2,1,0:T(8,128)(2,1)} %copy-done.19, ...), custom_call_target="tpu_custom_call" | custom-call | flops 100000000 | bytes 1024 | tf_op jit(solution)/shard_map/edge_project/pallas_call | solution.py:954
  215.4 3.5 collective-permute-start.17
  222.5 2.4 collective-permute-start.19
  224.9 6.3 %input_back.1 = (f32[2,384,768]{2,1,0:T(8,128)}, bf16[64,384]{1,0:T(8,128)(2,1)}) custom-call(bf16[2,384,768]{2,1,0:T(8,128)(2,1)} %get-tuple-element.170.part_ref, bf16[2,384,768]{2,1,0:T(8,128)(2,1)} %collective-permute-done.11.other_ref, f32[2,96,128]{2,1,0:T(8,128)} %get-tuple-element.171.logit_ref, f32[2,96,128]{2,1,0:T(8,128)} %copy-done.20, ...), custom_call_target="tpu_custom_call" | custom-call | flops 120000000 | bytes 1024 | tf_op jit(solution)/shard_map/input_back/pallas_call | solution.py:1015
  234.6 2.1 collective-permute-start.18
  238.9 23.6 %heavy_weights.7 = (f32[768,2,2048]{2,1,0:T(2,128)}, f32[768,2048]{1,0:T(8,128)}) custom-call(s32[1,1]{1,0:T(1,128)} %bitcast.18.core_ref.refs_0_, bf16[3072,768]{1,0:T(8,128)(2,1)} %bitcast.141, bf16[3072,768]{1,0:T(8,128)(2,1)} %bitcast.31.refs_2_, bf16[2,768,2048]{2,1,0:T(8,128)(2,1)} %bitcast.134, bf16[768,2048]{1,0:T(8,128)(2,1)} %refs_4_.13), custom_call_target="tpu_custom_call" | custom-call | flops 440000000 | bytes 1024 | tf_op jit(solution)/shard_map/heavy_weights/pallas_call | solution.py:1085
  270.7 2.2 collective-permute-start.24
  273.0 1.7 collective-permute-start.15
  274.7 14.1 %heavy_weights.8 = (f32[768,2,2048]{2,1,0:T(2,128)}, f32[768,2048]{1,0:T(8,128)}) custom-call(s32[1,1]{1,0:T(1,128)} %bitcast.18.core_ref.refs_0_, bf16[3072,768]{1,0:T(8,128)(2,1)} %bitcast.142, bf16[3072,768]{1,0:T(8,128)(2,1)} %bitcast.31.refs_2_, bf16[2,768,2048]{2,1,0:T(8,128)(2,1)} %bitcast.135, ...), custom_call_target="tpu_custom_call", output_to_operand_aliasing={{0}: (5, {}), {1}: (6, {})} | custom-call | flops 260000000 | bytes 1024 | tf_op jit(solution)/shard_map/heavy_weights/pallas_call | solution.py:1085
  292.3 14.2 %heavy_weights.9 = (f32[768,2,2048]{2,1,0:T(2,128)}, f32[768,2048]{1,0:T(8,128)}) custom-call(s32[1,1]{1,0:T(1,128)} %bitcast.18.core_ref.refs_0_, bf16[3072,768]{1,0:T(8,128)(2,1)} %bitcast.143, bf16[3072,768]{1,0:T(8,128)(2,1)} %bitcast.31.refs_2_, bf16[2,768,2048]{2,1,0:T(8,128)(2,1)} %bitcast.136, ...), custom_call_target="tpu_custom_call", output_to_operand_aliasing={{0}: (5, {}), {1}: (6, {})} | custom-call | flops 260000000 | bytes 1024 | tf_op jit(solution)/shard_map/heavy_weights/pallas_call | solution.py:1085
  306.7 1.6 collective-permute-start.28
  308.4 2.5 collective-permute-start.25
  310.9 14.5 %heavy_weights.10 = (f32[768,2,2048]{2,1,0:T(2,128)}, f32[768,2048]{1,0:T(8,128)}) custom-call(s32[1,1]{1,0:T(1,128)} %bitcast.18.core_ref.refs_0_, bf16[3072,768]{1,0:T(8,128)(2,1)} %bitcast.144, bf16[3072,768]{1,0:T(8,128)(2,1)} %bitcast.31.refs_2_, bf16[2,768,2048]{2,1,0:T(8,128)(2,1)} %bitcast.137, ...), custom_call_target="tpu_custom_call", output_to_operand_aliasing={{0}: (5, {}), {1}: (6, {})} | custom-call | flops 260000000 | bytes 1024 | tf_op jit(solution)/shard_map/heavy_weights/pallas_call | solution.py:1085
  327.8 14.2 %heavy_weights.11 = (f32[768,2,2048]{2,1,0:T(2,128)}, f32[768,2048]{1,0:T(8,128)}) custom-call(s32[1,1]{1,0:T(1,128)} %bitcast.18.core_ref.refs_0_, bf16[3072,768]{1,0:T(8,128)(2,1)} %bitcast.145, bf16[3072,768]{1,0:T(8,128)(2,1)} %bitcast.31.refs_2_, bf16[2,768,2048]{2,1,0:T(8,128)(2,1)} %bitcast.138, ...), custom_call_target="tpu_custom_call", output_to_operand_aliasing={{0}: (5, {}), {1}: (6, {})} | custom-call | flops 260000000 | bytes 1024 | tf_op jit(solution)/shard_map/heavy_weights/pallas_call | solution.py:1085
  342.9 1.8 collective-permute-start.33
  346.6 14.1 %heavy_weights.12 = (f32[768,2,2048]{2,1,0:T(2,128)}, f32[768,2048]{1,0:T(8,128)}) custom-call(s32[1,1]{1,0:T(1,128)} %bitcast.18.core_ref.refs_0_, bf16[3072,768]{1,0:T(8,128)(2,1)} %bitcast.146, bf16[3072,768]{1,0:T(8,128)(2,1)} %bitcast.31.refs_2_, bf16[2,768,2048]{2,1,0:T(8,128)(2,1)} %bitcast.139, ...), custom_call_target="tpu_custom_call", output_to_operand_aliasing={{0}: (5, {}), {1}: (6, {})} | custom-call | flops 260000000 | bytes 1024 | tf_op jit(solution)/shard_map/heavy_weights/pallas_call | solution.py:1085
  363.1 4.3 %feed_in.1 = f32[768,2,512]{2,1,0:T(2,128)} custom-call(s32[1,1]{1,0:T(1,128)} %bitcast.26.bit_ref, bf16[1024,384]{1,0:T(8,128)(2,1)} %copy-done.2, bf16[1024,384]{1,0:T(8,128)(2,1)} %collective-permute-done.33.got_ref), custom_call_target="tpu_custom_call" | custom-call | tf_op jit(solution)/shard_map/feed_in/pallas_call | solution.py:1168
  369.4 3.7 outs.1
  375.6 1.6 collective-permute-start.37
  378.5 14.1 %heavy_weights.13 = (f32[768,2,2048]{2,1,0:T(2,128)}, f32[768,2048]{1,0:T(8,128)}) custom-call(s32[1,1]{1,0:T(1,128)} %bitcast.18.core_ref.refs_0_, bf16[3072,768]{1,0:T(8,128)(2,1)} %bitcast.147, bf16[3072,768]{1,0:T(8,128)(2,1)} %bitcast.31.refs_2_, bf16[2,768,2048]{2,1,0:T(8,128)(2,1)} %bitcast.140, ...), custom_call_target="tpu_custom_call", output_to_operand_aliasing={{0}: (5, {}), {1}: (6, {})} | custom-call | flops 260000000 | bytes 1024 | tf_op jit(solution)/shard_map/heavy_weights/pallas_call | solution.py:1085
  392.6 1.6 collective-permute-done.37.got_ref
  394.1 2.4 heavy_sum.1
  396.6 2.4 light_sum.1
  (163 shorter events, 58.1 us)
Async XLA Ops:
  8.2 15.1 %collective-permute-start.2 = (bf16[128,768]{1,0:T(8,128)(2,1)S(1)}, bf16[128,768]{1,0:T(8,128)(2,1)S(1)}, u32[]{:S(2)}, u32[]{:S(2)}) collective-permute-start(bf16[128,768]{1,0:T(8,128)(2,1)S(1)} %get-tuple-element.232), channel_id=1, source_target_pairs={{2,0},{4,2},{6,4},{8,6},{10,8},{12,10},{14,12},{16,14},{18,16},{20... | collective-permute-start | bytes 589832 | tf_op jit(solution)/shard_map/ppermute | solution.py:1245
  9.5 13.8 %collective-permute-start = (bf16[128,768]{1,0:T(8,128)(2,1)S(1)}, bf16[128,768]{1,0:T(8,128)(2,1)S(1)}, u32[]{:S(2)}, u32[]{:S(2)}) collective-permute-start(bf16[128,768]{1,0:T(8,128)(2,1)S(1)} %get-tuple-element.233), channel_id=1, source_target_pairs={{0,2},{2,4},{4,6},{6,8},{8,10},{10,12},{12,14},{14,16},{16,18},{18... | collective-permute-start | bytes 589832 | tf_op jit(solution)/shard_map/ppermute | solution.py:1245
  23.3 1.4 collective-permute-start.1
  23.3 2.2 collective-permute-start.3
  26.3 24.4 %all-to-all-start = ((bf16[16,144,128]{2,1,0:T(8,128)(2,1)}), bf16[16,144,128]{2,1,0:T(8,128)(2,1)S(1)}, u32[]{:S(2)}, u32[]{:S(2)}) async-start(bf16[16,144,128]{2,1,0:T(8,128)(2,1)} %get-tuple-element.126), calls=%async_computation | async-start | bytes 1179648 | tf_op jit(solution)/shard_map/all_to_all | solution.py:1249
  34.8 31.1 %copy-start.11 = (bf16[768,2,512]{2,1,0:T(2,128)(2,1)S(1)}, bf16[768,2,512]{2,1,0:T(2,128)(2,1)}, u32[]{:S(2)}) copy-start(bf16[768,2,512]{2,1,0:T(2,128)(2,1)} %param.24) | copy-start | bytes 4718596
  61.5 14.1 %all-to-all-start.1 = ((bf16[16,48,128]{2,1,0:T(8,128)(2,1)}), bf16[16,48,128]{2,1,0:T(8,128)(2,1)S(1)}, u32[]{:S(2)}, u32[]{:S(2)}) async-start(bf16[16,48,128]{2,1,0:T(8,128)(2,1)} %get-tuple-element.129), calls=%async_computation.1 | async-start | bytes 393216 | tf_op jit(solution)/shard_map/all_to_all | solution.py:1249
  65.7 148.3 %all-gather.2.cloned.1.call-start = ((), (), s32[]{:S(2)}) async-start(), calls=%async_computation.4 | async-start | bytes 5013504 | tf_op jit(solution)/shard_map/all_gather | solution.py:1315
  80.3 3.1 collective-permute-start.4
  109.8 5.7 %collective-permute-start.5 = (bf16[2,2,384,768]{3,2,1,0:T(8,128)(2,1)}, bf16[2,2,384,768]{3,2,1,0:T(8,128)(2,1)S(1)}, u32[]{:S(2)}, u32[]{:S(2)}) collective-permute-start(bf16[2,2,384,768]{3,2,1,0:T(8,128)(2,1)} %get-tuple-element.140.part_ref), channel_id=1, source_target_pairs={{0,1},{1,0},{2,3},{3,2},{4,5},{5,4},{6,7},{7,6},{8,9},{9,8},{10,11... | collective-permute-start | bytes 7077896 | tf_op jit(solution)/shard_map/ppermute | solution.py:1238
  112.0 33.6 %collective-permute-start.7 = (bf16[1024,384]{1,0:T(8,128)(2,1)}, bf16[1024,384]{1,0:T(8,128)(2,1)S(1)}, u32[]{:S(2)}, u32[]{:S(2)}) collective-permute-start(bf16[1024,384]{1,0:T(8,128)(2,1)} %dynamic-slice_bitcast_fusion.3), channel_id=1, source_target_pairs={{0,2},{2,0},{4,6},{6,4},{8,10},{10,8},{12,14},{14,12},{16,18},{18,... | collective-permute-start | bytes 2359304 | tf_op jit(solution)/shard_map/ppermute | solution.py:1125
  114.0 1.5 collective-permute-start.6
  129.0 18.2 %all-to-all-start.2 = ((bf16[16,48,128]{2,1,0:T(8,128)(2,1)}), bf16[16,48,128]{2,1,0:T(8,128)(2,1)S(1)}, u32[]{:S(2)}, u32[]{:S(2)}) async-start(bf16[16,48,128]{2,1,0:T(8,128)(2,1)} %get-tuple-element.154), calls=%async_computation.2 | async-start | bytes 393216 | tf_op jit(solution)/shard_map/all_to_all | solution.py:1249
  147.8 15.3 %copy-start.6 = (bf16[2560,384]{1,0:T(8,128)(2,1)S(1)}, bf16[2560,384]{1,0:T(8,128)(2,1)}, u32[]{:S(2)}) copy-start(bf16[2560,384]{1,0:T(8,128)(2,1)} %get-tuple-element.164) | copy-start | bytes 5898244
  157.5 26.9 %all-to-all-start.3 = ((bf16[16,144,128]{2,1,0:T(8,128)(2,1)}), bf16[16,144,128]{2,1,0:T(8,128)(2,1)S(1)}, u32[]{:S(2)}, u32[]{:S(2)}) async-start(bf16[16,144,128]{2,1,0:T(8,128)(2,1)} %heavy_backward.1), calls=%async_computation.3 | async-start | bytes 1179648 | tf_op jit(solution)/shard_map/all_to_all | solution.py:1249
  164.2 40.6 %collective-permute-start.8 = (bf16[1280,384]{1,0:T(8,128)(2,1)}, bf16[1280,384]{1,0:T(8,128)(2,1)S(1)}, u32[]{:S(2)}, u32[]{:S(2)}) collective-permute-start(bf16[1280,384]{1,0:T(8,128)(2,1)} %dynamic-slice_bitcast_fusion), channel_id=1, source_target_pairs={{0,4},{2,6},{4,0},{6,2},{8,12},{10,14},{12,8},{14,10},{16,20},{18,... | collective-permute-start | bytes 2949128 | tf_op jit(solution)/shard_map/ppermute | solution.py:1125
  166.2 38.9 %collective-permute-start.9 = (bf16[2,2,128,384]{3,2,1,0:T(8,128)(2,1)}, bf16[2,2,128,384]{3,2,1,0:T(8,128)(2,1)S(1)}, u32[]{:S(2)}, u32[]{:S(2)}) collective-permute-start(bf16[2,2,128,384]{3,2,1,0:T(8,128)(2,1)} %get-tuple-element.167), channel_id=1, source_target_pairs={{0,2},{2,4},{4,6},{6,8},{8,10},{10,12},{12,14},{14,16},{16,18},{18... | collective-permute-start | bytes 1179656 | tf_op jit(solution)/shard_map/ppermute | solution.py:1245
  169.5 35.6 %collective-permute-start.10 = (bf16[2,2,128,384]{3,2,1,0:T(8,128)(2,1)}, bf16[2,2,128,384]{3,2,1,0:T(8,128)(2,1)S(1)}, u32[]{:S(2)}, u32[]{:S(2)}) collective-permute-start(bf16[2,2,128,384]{3,2,1,0:T(8,128)(2,1)} %get-tuple-element.168), channel_id=1, source_target_pairs={{2,0},{4,2},{6,4},{8,6},{10,8},{12,10},{14,12},{16,14},{18,16},{20... | collective-permute-start | bytes 1179656 | tf_op jit(solution)/shard_map/ppermute | solution.py:1245
  185.2 19.7 %copy-start.7 = (bf16[2560,384]{1,0:T(8,128)(2,1)S(1)}, bf16[2560,384]{1,0:T(8,128)(2,1)}, u32[]{:S(2)}) copy-start(bf16[2560,384]{1,0:T(8,128)(2,1)} %get-tuple-element.164) | copy-start | bytes 5898244
  214.0 24.9 %collective-permute-start.14 = (bf16[2,1536,768]{2,1,0:T(8,128)(2,1)}, bf16[2,1536,768]{2,1,0:T(8,128)(2,1)}, u32[]{:S(2)}, u32[]{:S(2)}) collective-permute-start(bf16[2,1536,768]{2,1,0:T(8,128)(2,1)} %all-gather.2.cloned.1.call-done), channel_id=1, source_target_pairs={{0,1},{1,0},{2,3},{3,2},{4,5},{5,4},{6,7},{7,6},{8,9},{9,8},{10,11... | collective-permute-start | bytes 14155784 | tf_op jit(solution)/shard_map/ppermute | solution.py:1238
  214.1 10.8 %collective-permute-start.11 = (bf16[2,384,768]{2,1,0:T(8,128)(2,1)}, bf16[2,384,768]{2,1,0:T(8,128)(2,1)}, u32[]{:S(2)}, u32[]{:S(2)}) collective-permute-start(bf16[2,384,768]{2,1,0:T(8,128)(2,1)} %get-tuple-element.170.part_ref), channel_id=1, source_target_pairs={{0,1},{1,0},{2,3},{3,2},{4,5},{5,4},{6,7},{7,6},{8,9},{9,8},{10,11... | collective-permute-start | bytes 3538952 | tf_op jit(solution)/shard_map/ppermute | solution.py:1238
  215.4 15.8 %collective-permute-start.17 = (bf16[640,384]{1,0:T(8,128)(2,1)}, bf16[640,384]{1,0:T(8,128)(2,1)}, u32[]{:S(2)}, u32[]{:S(2)}) collective-permute-start(bf16[640,384]{1,0:T(8,128)(2,1)} %dynamic-slice_bitcast_fusion.4), channel_id=1, source_target_pairs={{0,2},{2,0},{4,6},{6,4},{8,10},{10,8},{12,14},{14,12},{16,18},{18,... | collective-permute-start | bytes 1474568 | tf_op jit(solution)/shard_map/ppermute | solution.py:1125
  219.7 12.3 %collective-permute-start.16 = (bf16[512,384]{1,0:T(8,128)(2,1)}, bf16[512,384]{1,0:T(8,128)(2,1)}, u32[]{:S(2)}, u32[]{:S(2)}) collective-permute-start(bf16[512,384]{1,0:T(8,128)(2,1)} %dynamic-slice_bitcast_fusion.9), channel_id=1, source_target_pairs={{0,4},{2,6},{4,0},{6,2},{8,12},{10,14},{12,8},{14,10},{16,20},{18,... | collective-permute-start | bytes 1179656 | tf_op jit(solution)/shard_map/ppermute | solution.py:1125
  220.3 2.2 collective-permute-start.12
  222.5 40.1 %collective-permute-start.19 = (bf16[1152,384]{1,0:T(8,128)(2,1)}, bf16[1152,384]{1,0:T(8,128)(2,1)S(1)}, u32[]{:S(2)}, u32[]{:S(2)}) collective-permute-start(bf16[1152,384]{1,0:T(8,128)(2,1)} %dynamic-slice_bitcast_fusion.1), channel_id=1, source_target_pairs={{0,4},{2,6},{4,0},{6,2},{8,12},{10,14},{12,8},{14,10},{16,20},{18,... | collective-permute-start | bytes 2654216 | tf_op jit(solution)/shard_map/ppermute | solution.py:1125
  234.6 27.9 %collective-permute-start.18 = (bf16[576,384]{1,0:T(8,128)(2,1)S(1)}, bf16[576,384]{1,0:T(8,128)(2,1)S(1)}, u32[]{:S(2)}, u32[]{:S(2)}) collective-permute-start(bf16[576,384]{1,0:T(8,128)(2,1)S(1)} %dynamic-slice_bitcast_fusion.7), channel_id=1, source_target_pairs={{0,8},{2,10},{4,12},{6,14},{8,0},{10,2},{12,4},{14,6},{16,24},{18,... | collective-permute-start | bytes 1327112 | tf_op jit(solution)/shard_map/ppermute | solution.py:1125
  236.8 29.4 %collective-permute-start.13 = (bf16[1152,384]{1,0:T(8,128)(2,1)S(1)}, bf16[1152,384]{1,0:T(8,128)(2,1)}, u32[]{:S(2)}, u32[]{:S(2)}) collective-permute-start(bf16[1152,384]{1,0:T(8,128)(2,1)S(1)} %dynamic-slice_bitcast_fusion.2), channel_id=1, source_target_pairs={{0,2},{2,0},{4,6},{6,4},{8,10},{10,8},{12,14},{14,12},{16,18},{18,... | collective-permute-start | bytes 2654216 | tf_op jit(solution)/shard_map/ppermute | solution.py:1125
  238.3 24.2 %collective-permute-start.20 = (bf16[64,384]{1,0:T(8,128)(2,1)}, bf16[64,384]{1,0:T(8,128)(2,1)}, u32[]{:S(2)}, u32[]{:S(2)}) collective-permute-start(bf16[64,384]{1,0:T(8,128)(2,1)} %get-tuple-element.188), channel_id=1, source_target_pairs={{0,4},{2,6},{4,0},{6,2},{8,12},{10,14},{12,8},{14,10},{16,20},{18,... | collective-permute-start | bytes 147464 | tf_op jit(solution)/shard_map/ppermute | solution.py:1367
  267.7 21.1 %collective-permute-start.22 = (bf16[64,384]{1,0:T(8,128)(2,1)}, bf16[64,384]{1,0:T(8,128)(2,1)}, u32[]{:S(2)}, u32[]{:S(2)}) collective-permute-start(bf16[64,384]{1,0:T(8,128)(2,1)} %add_convert_fusion.1), channel_id=1, source_target_pairs={{0,2},{2,0},{4,6},{6,4},{8,10},{10,8},{12,14},{14,12},{16,18},{18,... | collective-permute-start | bytes 147464 | tf_op jit(solution)/shard_map/ppermute | solution.py:1383
  268.5 21.2 %collective-permute-start.21 = (bf16[576,384]{1,0:T(8,128)(2,1)S(1)}, bf16[576,384]{1,0:T(8,128)(2,1)S(1)}, u32[]{:S(2)}, u32[]{:S(2)}) collective-permute-start(bf16[576,384]{1,0:T(8,128)(2,1)S(1)} %dynamic-slice_bitcast_fusion.6), channel_id=1, source_target_pairs={{0,2},{2,0},{4,6},{6,4},{8,10},{10,8},{12,14},{14,12},{16,18},{18,... | collective-permute-start | bytes 1327112 | tf_op jit(solution)/shard_map/ppermute | solution.py:1125
  270.7 18.9 %collective-permute-start.24 = (bf16[288,384]{1,0:T(8,128)(2,1)}, bf16[288,384]{1,0:T(8,128)(2,1)}, u32[]{:S(2)}, u32[]{:S(2)}) collective-permute-start(bf16[288,384]{1,0:T(8,128)(2,1)} %dynamic-slice_bitcast_fusion.11), channel_id=1, source_target_pairs={{0,16},{2,18},{4,20},{6,22},{8,24},{10,26},{12,28},{14,30},{16,0},... | collective-permute-start | bytes 663560 | tf_op jit(solution)/shard_map/ppermute | solution.py:1125
  273.0 16.8 %collective-permute-start.15 = (bf16[576,384]{1,0:T(8,128)(2,1)S(1)}, bf16[576,384]{1,0:T(8,128)(2,1)S(1)}, u32[]{:S(2)}, u32[]{:S(2)}) collective-permute-start(bf16[576,384]{1,0:T(8,128)(2,1)S(1)} %dynamic-slice_bitcast_fusion.8), channel_id=1, source_target_pairs={{0,4},{2,6},{4,0},{6,2},{8,12},{10,14},{12,8},{14,10},{16,20},{18,... | collective-permute-start | bytes 1327112 | tf_op jit(solution)/shard_map/ppermute | solution.py:1125
  290.1 18.1 %collective-permute-start.23 = (bf16[608,384]{1,0:T(8,128)(2,1)S(1)}, bf16[608,384]{1,0:T(8,128)(2,1)S(1)}, u32[]{:S(2)}, u32[]{:S(2)}) collective-permute-start(bf16[608,384]{1,0:T(8,128)(2,1)S(1)} %dynamic-slice_bitcast_fusion.5), channel_id=1, source_target_pairs={{0,8},{2,10},{4,12},{6,14},{8,0},{10,2},{12,4},{14,6},{16,24},{18,... | collective-permute-start | bytes 1400840 | tf_op jit(solution)/shard_map/ppermute | solution.py:1125
  291.7 14.8 %collective-permute-start.26 = (bf16[288,384]{1,0:T(8,128)(2,1)S(1)}, bf16[288,384]{1,0:T(8,128)(2,1)S(1)}, u32[]{:S(2)}, u32[]{:S(2)}) collective-permute-start(bf16[288,384]{1,0:T(8,128)(2,1)S(1)} %fusion.11), channel_id=1, source_target_pairs={{0,16},{2,18},{4,20},{6,22},{8,24},{10,26},{12,28},{14,30},{16,0},... | collective-permute-start | bytes 663560 | tf_op jit(solution)/shard_map/ppermute | solution.py:1135
  306.7 18.7 %collective-permute-start.28 = (bf16[576,384]{1,0:T(8,128)(2,1)S(1)}, bf16[576,384]{1,0:T(8,128)(2,1)S(1)}, u32[]{:S(2)}, u32[]{:S(2)}) collective-permute-start(bf16[576,384]{1,0:T(8,128)(2,1)S(1)} %maximum_select_fusion.7), channel_id=1, source_target_pairs={{0,8},{2,10},{4,12},{6,14},{8,0},{10,2},{12,4},{14,6},{16,24},{18,... | collective-permute-start | bytes 1327112 | tf_op jit(solution)/shard_map/ppermute | solution.py:1135
  308.4 17.0 %collective-permute-start.25 = (bf16[304,384]{1,0:T(8,128)(2,1)S(1)}, bf16[304,384]{1,0:T(8,128)(2,1)S(1)}, u32[]{:S(2)}, u32[]{:S(2)}) collective-permute-start(bf16[304,384]{1,0:T(8,128)(2,1)S(1)} %dynamic-slice_bitcast_fusion.10), channel_id=1, source_target_pairs={{0,16},{2,18},{4,20},{6,22},{8,24},{10,26},{12,28},{14,30},{16,0},... | collective-permute-start | bytes 700424 | tf_op jit(solution)/shard_map/ppermute | solution.py:1125
  325.5 16.5 %collective-permute-start.27 = (bf16[304,384]{1,0:T(8,128)(2,1)S(1)}, bf16[304,384]{1,0:T(8,128)(2,1)S(1)}, u32[]{:S(2)}, u32[]{:S(2)}) collective-permute-start(bf16[304,384]{1,0:T(8,128)(2,1)S(1)} %fusion.10), channel_id=1, source_target_pairs={{0,16},{2,18},{4,20},{6,22},{8,24},{10,26},{12,28},{14,30},{16,0},... | collective-permute-start | bytes 700424 | tf_op jit(solution)/shard_map/ppermute | solution.py:1135
  326.5 16.1 %collective-permute-start.30 = (bf16[512,384]{1,0:T(8,128)(2,1)S(1)}, bf16[512,384]{1,0:T(8,128)(2,1)S(1)}, u32[]{:S(2)}, u32[]{:S(2)}) collective-permute-start(bf16[512,384]{1,0:T(8,128)(2,1)S(1)} %bitcast.192), channel_id=1, source_target_pairs={{0,4},{2,6},{4,0},{6,2},{8,12},{10,14},{12,8},{14,10},{16,20},{18,... | collective-permute-start | bytes 1179656 | tf_op jit(solution)/shard_map/ppermute | solution.py:1135
  327.1 17.5 %collective-permute-start.31 = (bf16[640,384]{1,0:T(8,128)(2,1)S(1)}, bf16[640,384]{1,0:T(8,128)(2,1)S(1)}, u32[]{:S(2)}, u32[]{:S(2)}) collective-permute-start(bf16[640,384]{1,0:T(8,128)(2,1)S(1)} %bitcast.174), channel_id=1, source_target_pairs={{0,2},{2,0},{4,6},{6,4},{8,10},{10,8},{12,14},{14,12},{16,18},{18,... | collective-permute-start | bytes 1474568 | tf_op jit(solution)/shard_map/ppermute | solution.py:1135
  342.2 18.5 %collective-permute-start.29 = (bf16[608,384]{1,0:T(8,128)(2,1)S(1)}, bf16[608,384]{1,0:T(8,128)(2,1)}, u32[]{:S(2)}, u32[]{:S(2)}) collective-permute-start(bf16[608,384]{1,0:T(8,128)(2,1)S(1)} %maximum_select_fusion.6), channel_id=1, source_target_pairs={{0,8},{2,10},{4,12},{6,14},{8,0},{10,2},{12,4},{14,6},{16,24},{18,... | collective-permute-start | bytes 1400840 | tf_op jit(solution)/shard_map/ppermute | solution.py:1135
  342.9 17.8 %copy-start.2 = (bf16[1024,384]{1,0:T(8,128)(2,1)}, bf16[1024,384]{1,0:T(8,128)(2,1)S(1)}, u32[]{:S(2)}) copy-start(bf16[1024,384]{1,0:T(8,128)(2,1)S(1)} %maximum_select_fusion.5.mine_ref) | copy-start | bytes 2359300
  342.9 20.2 %collective-permute-start.33 = (bf16[1024,384]{1,0:T(8,128)(2,1)S(1)}, bf16[1024,384]{1,0:T(8,128)(2,1)}, u32[]{:S(2)}, u32[]{:S(2)}) collective-permute-start(bf16[1024,384]{1,0:T(8,128)(2,1)S(1)} %maximum_select_fusion.5.mine_ref), channel_id=1, source_target_pairs={{0,2},{2,0},{4,6},{6,4},{8,10},{10,8},{12,14},{14,12},{16,18},{18,... | collective-permute-start | bytes 2359304 | tf_op jit(solution)/shard_map/ppermute | solution.py:1412
  345.0 15.6 %copy-start.1 = (bf16[1280,384]{1,0:T(8,128)(2,1)}, bf16[1280,384]{1,0:T(8,128)(2,1)S(1)}, u32[]{:S(2)}) copy-start(bf16[1280,384]{1,0:T(8,128)(2,1)S(1)} %maximum_select_fusion.mine_ref) | copy-start | bytes 2949124
  345.0 23.5 %collective-permute-start.34 = (bf16[1280,384]{1,0:T(8,128)(2,1)S(1)}, bf16[1280,384]{1,0:T(8,128)(2,1)S(1)}, u32[]{:S(2)}, u32[]{:S(2)}) collective-permute-start(bf16[1280,384]{1,0:T(8,128)(2,1)S(1)} %maximum_select_fusion.mine_ref), channel_id=1, source_target_pairs={{0,4},{2,6},{4,0},{6,2},{8,12},{10,14},{12,8},{14,10},{16,20},{18,... | collective-permute-start | bytes 2949128 | tf_op jit(solution)/shard_map/ppermute | solution.py:1412
  362.2 10.9 %collective-permute-start.36 = (bf16[576,384]{1,0:T(8,128)(2,1)S(1)}, bf16[576,384]{1,0:T(8,128)(2,1)S(1)}, u32[]{:S(2)}, u32[]{:S(2)}) collective-permute-start(bf16[576,384]{1,0:T(8,128)(2,1)S(1)} %bitcast.183), channel_id=1, source_target_pairs={{0,2},{2,0},{4,6},{6,4},{8,10},{10,8},{12,14},{14,12},{16,18},{18,... | collective-permute-start | bytes 1327112 | tf_op jit(solution)/shard_map/ppermute | solution.py:1135
  362.4 11.6 %collective-permute-start.32 = (bf16[576,384]{1,0:T(8,128)(2,1)S(1)}, bf16[576,384]{1,0:T(8,128)(2,1)S(1)}, u32[]{:S(2)}, u32[]{:S(2)}) collective-permute-start(bf16[576,384]{1,0:T(8,128)(2,1)S(1)} %bitcast.185), channel_id=1, source_target_pairs={{0,4},{2,6},{4,0},{6,2},{8,12},{10,14},{12,8},{14,10},{16,20},{18,... | collective-permute-start | bytes 1327112 | tf_op jit(solution)/shard_map/ppermute | solution.py:1135
  374.4 18.2 %collective-permute-start.35 = (bf16[1152,384]{1,0:T(8,128)(2,1)S(1)}, bf16[1152,384]{1,0:T(8,128)(2,1)S(1)}, u32[]{:S(2)}, u32[]{:S(2)}) collective-permute-start(bf16[1152,384]{1,0:T(8,128)(2,1)S(1)} %maximum_select_fusion.3.mine_ref), channel_id=1, source_target_pairs={{0,2},{2,0},{4,6},{6,4},{8,10},{10,8},{12,14},{14,12},{16,18},{18,... | collective-permute-start | bytes 2654216 | tf_op jit(solution)/shard_map/ppermute | solution.py:1428
  375.6 18.5 %collective-permute-start.37 = (bf16[1152,384]{1,0:T(8,128)(2,1)S(1)}, bf16[1152,384]{1,0:T(8,128)(2,1)S(1)}, u32[]{:S(2)}, u32[]{:S(2)}) collective-permute-start(bf16[1152,384]{1,0:T(8,128)(2,1)S(1)} %maximum_select_fusion.4.mine_ref), channel_id=1, source_target_pairs={{0,4},{2,6},{4,0},{6,2},{8,12},{10,14},{12,8},{14,10},{16,20},{18,... | collective-permute-start | bytes 2654216 | tf_op jit(solution)/shard_map/ppermute | solution.py:1428
  (17 other events, 37.6 us)
Sparse Core Ops, SparseCore 0:
  89.3 108.7 all-gather.1

commit v2 on v1

--- a/solution.py
+++ b/solution.py
@@ -838,29 +838,42 @@
     )
 
 
-def light_project_kernel(local_ref, low_ref, light_ref, grad_ref, part_ref):
+def light_project_kernel(local_ref, low_ref, light_ref, first_ref, grad_ref, part_ref, first_acc):
     @pl.when(pl.program_id(0) == 0)
     def _():
+        first_acc[...] = jnp.zeros_like(first_acc)
         grad_ref[...] = jnp.zeros_like(grad_ref)
 
     low = low_ref[0]
     part = None
     for kind in range(3):
         rows = local_ref[0, kind]
-        grad_ref[kind] += cols_dot(low, rows)
+        if kind == 0:
+            first_acc[...] += cols_dot(low, rows)
+        else:
+            grad_ref[kind - 1] += cols_dot(low, rows)
         more = rows_dot(rows, light_ref[kind])
         part = more if part is None else part + more
     part_ref[0] = part
 
+    @pl.when(pl.program_id(0) == pl.num_programs(0) - 1)
+    def _():
+        first_ref[...] = first_acc[...].astype(LOW)
+
 
 def light_project(local, low, light):
-    shapes = [like(light.shape, WIDE), like(low.shape, WIDE)]
+    shapes = [
+        like(light.shape[1:], LOW),
+        like((2,) + light.shape[1:], WIDE),
+        like(low.shape, WIDE),
+    ]
     return pl.pallas_call(
         light_project_kernel,
         grid=(low.shape[0],),
         in_specs=[each(local), each(low), whole(light)],
-        out_specs=[whole(shapes[0]), each(shapes[1])],
+        out_specs=[whole(shapes[0]), whole(shapes[1]), each(shapes[2])],
         out_shape=shapes,
+        scratch_shapes=[pltpu.VMEM(light.shape[1:], WIDE)],
         compiler_params=params(),
         cost_estimate=cost(9),
         name="light_project",
@@ -927,41 +940,50 @@
 
 
 def edge_project_kernel(
-    part_in_ref, low_ref, lead_ref, tail_ref, light_ref, sum_ref, grad_ref, part_ref, grad_acc
+    part_in_ref, low_ref, lead_ref, tail_ref, key_ref, value_ref, first_ref, sum_ref,
+    grad_ref, part_ref, grad_acc,
 ):
     step = pl.program_id(0)
 
     @pl.when(step == 0)
     def _():
-        grad_acc[...] = sum_ref[1:]
+        grad_acc[...] = sum_ref[...]
 
     length = low_ref.shape[1]
     part_ref[0, WIN : length - WIN, :] = part_in_ref[0, WIN : length - WIN, :].astype(LOW)
     for ref, rows in ((lead_ref, slice(0, WIN)), (tail_ref, slice(length - WIN, length))):
         for kind in range(2):
             grad_acc[kind] += cols_dot(low_ref[0, rows, :], ref[0, kind])
-        more = rows_dot(ref[0, 0], light_ref[1]) + rows_dot(ref[0, 1], light_ref[2])
+        more = rows_dot(ref[0, 0], key_ref[0]) + rows_dot(ref[0, 1], value_ref[0])
         part_ref[0, rows, :] = (part_in_ref[0, rows, :] + more).astype(LOW)
 
     @pl.when(step == pl.num_programs(0) - 1)
     def _():
-        grad_ref[0] = sum_ref[0].astype(LOW)
+        grad_ref[0] = first_ref[...]
         grad_ref[1:] = grad_acc[...].astype(LOW)
 
 
-def edge_project(part, low, lead, tail, light, light_sum):
+def edge_project(part, low, lead, tail, light, first, light_sum):
     shapes = [like(light.shape, LOW), like(low.shape, LOW)]
+    kinds = [
+        pl.BlockSpec(
+            (1,) + light.shape[1:], lambda s, kind=kind: (kind, 0, 0), pipeline_mode=pl.Buffered(1)
+        )
+        for kind in (1, 2)
+    ]
     return pl.pallas_call(
         edge_project_kernel,
         grid=(low.shape[0],),
-        in_specs=[each(part), each(low), each(lead), each(tail), whole(light), whole(light_sum)],
+        in_specs=[each(part), each(low), each(lead), each(tail)]
+        + kinds
+        + [whole(first), whole(light_sum)],
         out_specs=[whole(shapes[0]), each(shapes[1])],
         out_shape=shapes,
         scratch_shapes=[pltpu.VMEM((2,) + light.shape[1:], WIDE)],
         compiler_params=params(),
         cost_estimate=cost(5),
         name="edge_project",
-    )(part, low, lead, tail, light, light_sum)
+    )(part, low, lead, tail, light, light, first, light_sum)
 
 
 def input_kernel(
@@ -1334,13 +1356,13 @@
     )
     triple_pairs = exchange(triple)
     second_going = scatter_start(after(out_grads, triple), 1)
-    light_sums, light_part = light_project(after(local, triple), low, light_weights)
+    light_first, light_sums, light_part = light_project(after(local, triple), low, light_weights)
     heavy_grads, part_sum, logit = heavy_project(
         light_part, low, triple_pairs, heavy_weights_qkv, slots, gate, raw, query_logit
     )
     second_wave = scatter_end(second_going, part_sum)
     light_grads, low_part = edge_project(
-        after(part_sum, second_wave), low, lead, tail, light_weights, light_sums
+        after(part_sum, second_wave), low, lead, tail, light_weights, light_first, light_sums
     )
     heavy_going = scatter_start(heavy_grads.reshape(-1, light_cols), 1)
     light_going = scatter_start(light_grads.reshape(-1, light_cols), 0)

time: 414 us -> 414 us (level)
  transfers between devices with their start and end apart: 43 -> 43, of which waited for: 14 -> 13; matrix products, arithmetic and copies ran while one was open for 8% -> 8% of each run, Pallas kernels for 54% -> 54%
where the time goes in v2:
time: 414 us; the launch traced here: 406 us
  Pallas kernels  244 us (59%)
  starting transfers between devices  71.6 us (17%)
  waiting for transfers between devices  30.7 us (7%)
  local copies, waits for them, and re-layouts  27.4 us (7%)
  other arithmetic  17.4 us (4%)
  between operations  14.9 us (4%)
    pallas_call x7, Pallas kernels, heavy_weights(): pl.pallas_call(lambda *refs: heavy_weights_kernel(tile, *refs), grid=(cou...  109 us
    all_to_all x4, starting transfers between devices, exchange(): return lax.all_to_all(pairs, 'seq', split_axis=0, concat_axis=0, tiled=True)  24 us
    ppermute x12, starting transfers between devices, scatter_start(): return (kept, lax.ppermute(sent, 'seq', bit_pairs(bit)))  22.4 us
    pallas_call x1, Pallas kernels, feed(): pl.pallas_call(feed_kernel, grid=(heavy_out.shape[1] // cols,), in_specs=...  20.7 us
    pallas_call x1, Pallas kernels, light_forward(): pl.pallas_call(lambda *refs: light_forward_kernel(1.0 / math.sqrt(LHD), *...  13.2 us
    ppermute x12, waiting for transfers between devices, scatter_start(): return (kept, lax.ppermute(sent, 'seq', bit_pairs(bit)))  12.2 us
    pallas_call x1, Pallas kernels, middle_back(): pl.pallas_call(middle_kernel, grid=(seqs,), in_specs=[each(tokens), each(...  12 us
    ppermute x4, starting transfers between devices, to_neighbours(): return (lax.ppermute(last, 'seq', up), lax.ppermute(first, 'seq', down))  11.4 us
  transfers between devices with their start and end apart: 43, of which 13 were waited for; matrix products, arithmetic and copies ran while one was open for 8% of the time, Pallas kernels for 54%

profile of v2, /device:TPU:0, one launch (start us, length us, event | category | flops | bytes accessed | tf_op | source)
XLA Modules:
  0.0 405.8 jit_solution(7164773797973420377)
XLA Ops:
  9.5 5.5 %collective-permute-start = (bf16[128,768]{1,0:T(8,128)(2,1)S(1)}, bf16[128,768]{1,0:T(8,128)(2,1)S(1)}, u32[]{:S(2)}, u32[]{:S(2)}) collective-permute-start(bf16[128,768]{1,0:T(8,128)(2,1)S(1)} %get-tuple-element.235), channel_id=1, source_target_pairs={{0,2},{2,4},{4,6},{6,8},{8,10},{10,12},{12,14},{14,16},{16,18},{18... | collective-permute-start | bytes 589832 | tf_op jit(solution)/shard_map/ppermute | solution.py:1267
  17.4 5.5 %front.1 = (bf16[2,384,768]{2,1,0:T(8,128)(2,1)}, bf16[16,144,128]{2,1,0:T(8,128)(2,1)}, f32[2,96,384]{2,1,0:T(8,128)}, f32[2,96,128]{2,1,0:T(8,128)}) custom-call(bf16[2,384,768]{2,1,0:T(8,128)(2,1)} %tokens_ref.7, f32[2,768]{1,0:T(2,128)} %bitcast.206, f32[3,768]{1,0:T(4,128)} %bitcast.202, s32[2,96,6]{2,1,0:T(8,128)} %copy.48.slots_ref, ...), custom_call_target="tpu_custom_call" | custom-call | flops 160000000 | bytes 1024 | tf_op jit(solution)/shard_map/front/pallas_call | solution.py:237
  26.3 7.9 %all-to-all-start = ((bf16[16,144,128]{2,1,0:T(8,128)(2,1)}), bf16[16,144,128]{2,1,0:T(8,128)(2,1)S(1)}, u32[]{:S(2)}, u32[]{:S(2)}) async-start(bf16[16,144,128]{2,1,0:T(8,128)(2,1)} %get-tuple-element.127), calls=%async_computation | async-start | bytes 1179648 | tf_op jit(solution)/shard_map/all_to_all | solution.py:1271
  34.8 13.2 %light_forward.1 = (bf16[2,384,384]{2,1,0:T(8,128)(2,1)}, f32[2,384,768]{2,1,0:T(8,128)}, f32[2,384,128]{2,1,0:T(8,128)}, bf16[2,384,512]{2,1,0:T(8,128)(2,1)}, bf16[2,2,640,512]{3,2,1,0:T(8,128)(2,1)}) custom-call(s32[1,2]{1,0:T(1,128)} %add_bitcast_fusion.refs_0_, bf16[2,384,768]{2,1,0:T(8,128)(2,1)} %get-tuple-element.124.refs_1_.low_ref, ...), custom_call_target="tpu_custom_call" | custom-call | flops 300000000 | bytes 1024 | tf_op jit(solution)/shard_map/light_forward/pallas_call | solution.py:318
  48.0 2.7 all-to-all-done.refs_0_
  51.5 9.9 %heavy_forward.1 = (bf16[1536,128]{1,0:T(8,128)(2,1)}, bf16[1536,128]{1,0:T(8,128)(2,1)}, bf16[1536,128]{1,0:T(8,128)(2,1)}, f32[1536,128]{1,0:T(8,128)}, bf16[16,48,128]{2,1,0:T(8,128)(2,1)}) custom-call(bf16[16,144,128]{2,1,0:T(8,128)(2,1)} %copy-done.4), custom_call_target="tpu_custom_call" | custom-call | flops 140000000 | bytes 1024 | tf_op jit(solution)/shard_map/heavy_forward/pallas_call | solution.py:503
  61.5 4.2 %all-to-all-start.1 = ((bf16[16,48,128]{2,1,0:T(8,128)(2,1)}), bf16[16,48,128]{2,1,0:T(8,128)(2,1)S(1)}, u32[]{:S(2)}, u32[]{:S(2)}) async-start(bf16[16,48,128]{2,1,0:T(8,128)(2,1)} %get-tuple-element.130), calls=%async_computation.1 | async-start | bytes 393216 | tf_op jit(solution)/shard_map/all_to_all | solution.py:1271
  67.3 8.3 %copy.59 = bf16[768,2,2048]{2,0,1:T(8,128)(2,1)} copy(bf16[768,2,2048]{2,1,0:T(2,128)(2,1)} %param.26) | data formatting | bytes 12582912 | tf_op jit(solution)/shard_map/optimization_barrier | solution.py:1139
  76.3 4.0 combine.1
  80.3 3.0 collective-permute-done.4.other_ref
  84.4 4.8 %mlp_slots.1 = (bf16[2,384,768]{2,1,0:T(8,128)(2,1)}, bf16[2,96,768]{2,1,0:T(8,128)(2,1)}, bf16[2,96,768]{2,1,0:T(8,128)(2,1)}, bf16[2,96,768]{2,1,0:T(8,128)(2,1)}, f32[2,96,128]{2,1,0:T(8,128)}) custom-call(s32[1,1]{1,0:T(1,128)} %bitcast.18.core_ref.refs_0_, bf16[2,384,768]{2,1,0:T(8,128)(2,1)} %tokens_ref.7, ...), custom_call_target="tpu_custom_call" | custom-call | flops 100000000 | bytes 1024 | tf_op jit(solution)/shard_map/mlp_slots/pallas_call | solution.py:607
  89.2 20.7 %feed.1 = (bf16[2,2,384,768]{3,2,1,0:T(8,128)(2,1)}, bf16[2,1024,384]{2,1,0:T(8,128)(2,1)}, bf16[1024,384]{1,0:T(8,128)(2,1)}, f32[2,96,128]{2,1,0:T(8,128)}) custom-call(bf16[2,384,768]{2,1,0:T(8,128)(2,1)} %get-tuple-element.137.low_ref, bf16[192,768]{1,0:T(8,128)(2,1)} %bitcast.195, bf16[192,768]{1,0:T(8,128)(2,1)} %bitcast.196, ...), custom_call_target="tpu_custom_call" | custom-call | flops 400000000 | bytes 1024 | tf_op jit(solution)/shard_map/feed/pallas_call | solution.py:716
  110.0 2.1 dynamic-slice_bitcast_fusion.3
  112.1 2.0 collective-permute-start.7
  117.0 12.0 %middle_back.1 = (bf16[2,384,768]{2,1,0:T(8,128)(2,1)}, f32[2,384,768]{2,1,0:T(8,128)}, bf16[2,384,384]{2,1,0:T(8,128)(2,1)}, bf16[16,48,128]{2,1,0:T(8,128)(2,1...) custom-call(bf16[2,384,768]{2,1,0:T(8,128)(2,1)} %tokens_ref.7, ...), custom_call_target="tpu_custom_call" | custom-call | flops 220000000 | bytes 1024 | tf_op jit(solution)/shard_map/middle_back/pallas_call | solution.py:821
  129.1 6.3 %all-to-all-start.2 = ((bf16[16,48,128]{2,1,0:T(8,128)(2,1)}), bf16[16,48,128]{2,1,0:T(8,128)(2,1)S(1)}, u32[]{:S(2)}, u32[]{:S(2)}) async-start(bf16[16,48,128]{2,1,0:T(8,128)(2,1)} %get-tuple-element.155), calls=%async_computation.2 | async-start | bytes 393216 | tf_op jit(solution)/shard_map/all_to_all | solution.py:1271
  135.4 10.3 %light_backward.1 = (bf16[2,3,384,384]{3,2,1,0:T(8,128)(2,1)}, bf16[2,2,128,384]{3,2,1,0:T(8,128)(2,1)}, bf16[2,2,128,384]{3,2,1,0:T(8,128)(2,1)}) custom-call(s32[1,2]{1,0:T(1,128)} %add_bitcast_fusion.refs_0_, bf16[2,384,512]{2,1,0:T(8,128)(2,1)} %get-tuple-element.147.refs_1_, bf16[2,2,640,512]{3,2,1,0:T(8,128)(2,1)} %get-tuple-element.148.refs_2_, ...), custom_call_target="tpu_custom_call" | custom-call | flops 280000000 | bytes 1024 | tf_op jit(solution)/shard_map/light_backward/pallas_call | solution.py:388
  147.9 9.7 %heavy_backward.1 = bf16[16,144,128]{2,1,0:T(8,128)(2,1)} custom-call(bf16[1536,128]{1,0:T(8,128)(2,1)} %get-tuple-element.152.refs_0_, bf16[1536,128]{1,0:T(8,128)(2,1)} %get-tuple-element.153.refs_1_, bf16[1536,128]{1,0:T(8,128)(2,1)} %get-tuple-element.154.refs_2_, f32[1536,128]{1,0:T(8,128)} %get-tuple-element.131.refs_3_, bf16[16,48,128]{2,1,0:T(8,128)(2,1)} %copy-done.15), custom_call_target="tpu_custom_call" | custom-call | flops 200000000 | bytes 1024 | tf_op jit(solution)/shard_map/heavy_backward/pallas_call | solution.py:524
  157.6 5.6 %all-to-all-start.3 = ((bf16[16,144,128]{2,1,0:T(8,128)(2,1)}), bf16[16,144,128]{2,1,0:T(8,128)(2,1)S(1)}, u32[]{:S(2)}, u32[]{:S(2)}) async-start(bf16[16,144,128]{2,1,0:T(8,128)(2,1)} %heavy_backward.1), calls=%async_computation.3 | async-start | bytes 1179648 | tf_op jit(solution)/shard_map/all_to_all | solution.py:1271
  164.3 1.9 collective-permute-start.8
  166.2 3.4 collective-permute-start.9
  170.9 9.4 %light_project.1 = (bf16[768,384]{1,0:T(8,128)(2,1)}, f32[2,768,384]{2,1,0:T(8,128)}, f32[2,384,768]{2,1,0:T(8,128)}) custom-call(bf16[2,3,384,384]{3,2,1,0:T(8,128)(2,1)} %get-tuple-element.159.local_ref, bf16[2,384,768]{2,1,0:T(8,128)(2,1)} %get-tuple-element.124.refs_1_.low_ref, bf16[3,768,384]{2,1,0:T(8,128)(2,1)} %bitcast.149), custom_call_target="tpu_custom_call" | custom-call | flops 180000000 | bytes 1024 | tf_op jit(solution)/shard_map/light_project/pallas_call | solution.py:870
  180.3 3.8 all-to-all-done.3.pairs_ref
  184.9 8.8 %heavy_project.1 = (bf16[3,768,384]{2,1,0:T(8,128)(2,1)}, f32[2,384,768]{2,1,0:T(8,128)}, f32[2,96,128]{2,1,0:T(8,128)}) custom-call(f32[2,384,768]{2,1,0:T(8,128)} %get-tuple-element.160.light_part_ref, bf16[2,384,768]{2,1,0:T(8,128)(2,1)} %get-tuple-element.124.refs_1_.low_ref, bf16[16,144,128]{2,1,0:T(8,128)(2,1)} %copy-done.3, ...), custom_call_target="tpu_custom_call" | custom-call | flops 200000000 | bytes 1024 | tf_op jit(solution)/shard_map/heavy_project/pallas_call | solution.py:926
  193.8 11.2 %collective-permute-done.8 = bf16[1280,384]{1,0:T(8,128)(2,1)S(1)} collective-permute-done((bf16[1280,384]{1,0:T(8,128)(2,1)}, bf16[1280,384]{1,0:T(8,128)(2,1)S(1)}, u32[]{:S(2)}, u32[]{:S(2)}) %collective-permute-start.8) | collective-permute-done | bytes 983072 | tf_op jit(solution)/shard_map/ppermute | solution.py:1147
  206.1 7.7 %edge_project.1 = (bf16[3,768,384]{2,1,0:T(8,128)(2,1)}, bf16[2,384,768]{2,1,0:T(8,128)(2,1)}) custom-call(f32[2,384,768]{2,1,0:T(8,128)} %get-tuple-element.167.part_in_ref, bf16[2,384,768]{2,1,0:T(8,128)(2,1)} %get-tuple-element.124.refs_1_.low_ref, bf16[2,2,128,384]{3,2,1,0:T(8,128)(2,1)} %copy-done.18, bf16[2,2,128,384]{3,2,1,0:T(8,128)(2,1)} %copy-done.19, ...), custom_call_target="tpu_custom_call" | custom-call | flops 100000000 | bytes 1024 | tf_op jit(solution)/shard_map/edge_project/pallas_call | solution.py:974
  215.2 3.5 collective-permute-start.17
  222.3 2.4 collective-permute-start.19
  224.6 6.3 %input_back.1 = (f32[2,384,768]{2,1,0:T(8,128)}, bf16[64,384]{1,0:T(8,128)(2,1)}) custom-call(bf16[2,384,768]{2,1,0:T(8,128)(2,1)} %get-tuple-element.172.part_ref, bf16[2,384,768]{2,1,0:T(8,128)(2,1)} %collective-permute-done.11.other_ref, f32[2,96,128]{2,1,0:T(8,128)} %get-tuple-element.173.logit_ref, f32[2,96,128]{2,1,0:T(8,128)} %copy-done.20, ...), custom_call_target="tpu_custom_call" | custom-call | flops 120000000 | bytes 1024 | tf_op jit(solution)/shard_map/input_back/pallas_call | solution.py:1037
  234.4 2.0 collective-permute-start.18
  238.6 23.6 %heavy_weights.7 = (f32[768,2,2048]{2,1,0:T(2,128)}, f32[768,2048]{1,0:T(8,128)}) custom-call(s32[1,1]{1,0:T(1,128)} %bitcast.18.core_ref.refs_0_, bf16[3072,768]{1,0:T(8,128)(2,1)} %bitcast.141, bf16[3072,768]{1,0:T(8,128)(2,1)} %bitcast.31.refs_2_, bf16[2,768,2048]{2,1,0:T(8,128)(2,1)} %bitcast.134, bf16[768,2048]{1,0:T(8,128)(2,1)} %refs_4_.13), custom_call_target="tpu_custom_call" | custom-call | flops 440000000 | bytes 1024 | tf_op jit(solution)/shard_map/heavy_weights/pallas_call | solution.py:1107
  270.4 2.2 collective-permute-start.24
  272.7 1.7 collective-permute-start.15
  274.4 14.1 %heavy_weights.8 = (f32[768,2,2048]{2,1,0:T(2,128)}, f32[768,2048]{1,0:T(8,128)}) custom-call(s32[1,1]{1,0:T(1,128)} %bitcast.18.core_ref.refs_0_, bf16[3072,768]{1,0:T(8,128)(2,1)} %bitcast.142, bf16[3072,768]{1,0:T(8,128)(2,1)} %bitcast.31.refs_2_, bf16[2,768,2048]{2,1,0:T(8,128)(2,1)} %bitcast.135, ...), custom_call_target="tpu_custom_call", output_to_operand_aliasing={{0}: (5, {}), {1}: (6, {})} | custom-call | flops 260000000 | bytes 1024 | tf_op jit(solution)/shard_map/heavy_weights/pallas_call | solution.py:1107
  292.0 14.2 %heavy_weights.9 = (f32[768,2,2048]{2,1,0:T(2,128)}, f32[768,2048]{1,0:T(8,128)}) custom-call(s32[1,1]{1,0:T(1,128)} %bitcast.18.core_ref.refs_0_, bf16[3072,768]{1,0:T(8,128)(2,1)} %bitcast.143, bf16[3072,768]{1,0:T(8,128)(2,1)} %bitcast.31.refs_2_, bf16[2,768,2048]{2,1,0:T(8,128)(2,1)} %bitcast.136, ...), custom_call_target="tpu_custom_call", output_to_operand_aliasing={{0}: (5, {}), {1}: (6, {})} | custom-call | flops 260000000 | bytes 1024 | tf_op jit(solution)/shard_map/heavy_weights/pallas_call | solution.py:1107
  308.1 2.5 collective-permute-start.25
  310.6 14.5 %heavy_weights.10 = (f32[768,2,2048]{2,1,0:T(2,128)}, f32[768,2048]{1,0:T(8,128)}) custom-call(s32[1,1]{1,0:T(1,128)} %bitcast.18.core_ref.refs_0_, bf16[3072,768]{1,0:T(8,128)(2,1)} %bitcast.144, bf16[3072,768]{1,0:T(8,128)(2,1)} %bitcast.31.refs_2_, bf16[2,768,2048]{2,1,0:T(8,128)(2,1)} %bitcast.137, ...), custom_call_target="tpu_custom_call", output_to_operand_aliasing={{0}: (5, {}), {1}: (6, {})} | custom-call | flops 260000000 | bytes 1024 | tf_op jit(solution)/shard_map/heavy_weights/pallas_call | solution.py:1107
  327.5 14.2 %heavy_weights.11 = (f32[768,2,2048]{2,1,0:T(2,128)}, f32[768,2048]{1,0:T(8,128)}) custom-call(s32[1,1]{1,0:T(1,128)} %bitcast.18.core_ref.refs_0_, bf16[3072,768]{1,0:T(8,128)(2,1)} %bitcast.145, bf16[3072,768]{1,0:T(8,128)(2,1)} %bitcast.31.refs_2_, bf16[2,768,2048]{2,1,0:T(8,128)(2,1)} %bitcast.138, ...), custom_call_target="tpu_custom_call", output_to_operand_aliasing={{0}: (5, {}), {1}: (6, {})} | custom-call | flops 260000000 | bytes 1024 | tf_op jit(solution)/shard_map/heavy_weights/pallas_call | solution.py:1107
  342.6 1.8 collective-permute-start.33
  344.7 1.6 collective-permute-start.34
  346.3 14.1 %heavy_weights.12 = (f32[768,2,2048]{2,1,0:T(2,128)}, f32[768,2048]{1,0:T(8,128)}) custom-call(s32[1,1]{1,0:T(1,128)} %bitcast.18.core_ref.refs_0_, bf16[3072,768]{1,0:T(8,128)(2,1)} %bitcast.146, bf16[3072,768]{1,0:T(8,128)(2,1)} %bitcast.31.refs_2_, bf16[2,768,2048]{2,1,0:T(8,128)(2,1)} %bitcast.139, ...), custom_call_target="tpu_custom_call", output_to_operand_aliasing={{0}: (5, {}), {1}: (6, {})} | custom-call | flops 260000000 | bytes 1024 | tf_op jit(solution)/shard_map/heavy_weights/pallas_call | solution.py:1107
  362.8 4.3 %feed_in.1 = f32[768,2,512]{2,1,0:T(2,128)} custom-call(s32[1,1]{1,0:T(1,128)} %bitcast.26.bit_ref, bf16[1024,384]{1,0:T(8,128)(2,1)} %copy-done.2, bf16[1024,384]{1,0:T(8,128)(2,1)} %collective-permute-done.33.got_ref), custom_call_target="tpu_custom_call" | custom-call | tf_op jit(solution)/shard_map/feed_in/pallas_call | solution.py:1190
  369.2 3.7 outs.1
  375.4 1.6 collective-permute-start.37
  378.2 14.1 %heavy_weights.13 = (f32[768,2,2048]{2,1,0:T(2,128)}, f32[768,2048]{1,0:T(8,128)}) custom-call(s32[1,1]{1,0:T(1,128)} %bitcast.18.core_ref.refs_0_, bf16[3072,768]{1,0:T(8,128)(2,1)} %bitcast.147, bf16[3072,768]{1,0:T(8,128)(2,1)} %bitcast.31.refs_2_, bf16[2,768,2048]{2,1,0:T(8,128)(2,1)} %bitcast.140, ...), custom_call_target="tpu_custom_call", output_to_operand_aliasing={{0}: (5, {}), {1}: (6, {})} | custom-call | flops 260000000 | bytes 1024 | tf_op jit(solution)/shard_map/heavy_weights/pallas_call | solution.py:1107
  392.3 1.6 collective-permute-done.37.got_ref
  393.9 2.4 heavy_sum.1
  396.3 2.4 light_sum.1
  (163 shorter events, 58.3 us)
Async XLA Ops:
  8.2 15.1 %collective-permute-start.2 = (bf16[128,768]{1,0:T(8,128)(2,1)S(1)}, bf16[128,768]{1,0:T(8,128)(2,1)S(1)}, u32[]{:S(2)}, u32[]{:S(2)}) collective-permute-start(bf16[128,768]{1,0:T(8,128)(2,1)S(1)} %get-tuple-element.234), channel_id=1, source_target_pairs={{2,0},{4,2},{6,4},{8,6},{10,8},{12,10},{14,12},{16,14},{18,16},{20... | collective-permute-start | bytes 589832 | tf_op jit(solution)/shard_map/ppermute | solution.py:1267
  9.5 13.8 %collective-permute-start = (bf16[128,768]{1,0:T(8,128)(2,1)S(1)}, bf16[128,768]{1,0:T(8,128)(2,1)S(1)}, u32[]{:S(2)}, u32[]{:S(2)}) collective-permute-start(bf16[128,768]{1,0:T(8,128)(2,1)S(1)} %get-tuple-element.235), channel_id=1, source_target_pairs={{0,2},{2,4},{4,6},{6,8},{8,10},{10,12},{12,14},{14,16},{16,18},{18... | collective-permute-start | bytes 589832 | tf_op jit(solution)/shard_map/ppermute | solution.py:1267
  23.3 1.4 collective-permute-start.1
  23.3 2.2 collective-permute-start.3
  26.3 24.4 %all-to-all-start = ((bf16[16,144,128]{2,1,0:T(8,128)(2,1)}), bf16[16,144,128]{2,1,0:T(8,128)(2,1)S(1)}, u32[]{:S(2)}, u32[]{:S(2)}) async-start(bf16[16,144,128]{2,1,0:T(8,128)(2,1)} %get-tuple-element.127), calls=%async_computation | async-start | bytes 1179648 | tf_op jit(solution)/shard_map/all_to_all | solution.py:1271
  34.8 31.1 %copy-start.11 = (bf16[768,2,512]{2,1,0:T(2,128)(2,1)S(1)}, bf16[768,2,512]{2,1,0:T(2,128)(2,1)}, u32[]{:S(2)}) copy-start(bf16[768,2,512]{2,1,0:T(2,128)(2,1)} %param.24) | copy-start | bytes 4718596
  61.5 14.1 %all-to-all-start.1 = ((bf16[16,48,128]{2,1,0:T(8,128)(2,1)}), bf16[16,48,128]{2,1,0:T(8,128)(2,1)S(1)}, u32[]{:S(2)}, u32[]{:S(2)}) async-start(bf16[16,48,128]{2,1,0:T(8,128)(2,1)} %get-tuple-element.130), calls=%async_computation.1 | async-start | bytes 393216 | tf_op jit(solution)/shard_map/all_to_all | solution.py:1271
  65.7 148.1 %all-gather.2.cloned.1.call-start = ((), (), s32[]{:S(2)}) async-start(), calls=%async_computation.4 | async-start | bytes 5013504 | tf_op jit(solution)/shard_map/all_gather | solution.py:1337
  80.3 3.1 collective-permute-start.4
  109.9 5.7 %collective-permute-start.5 = (bf16[2,2,384,768]{3,2,1,0:T(8,128)(2,1)}, bf16[2,2,384,768]{3,2,1,0:T(8,128)(2,1)S(1)}, u32[]{:S(2)}, u32[]{:S(2)}) collective-permute-start(bf16[2,2,384,768]{3,2,1,0:T(8,128)(2,1)} %get-tuple-element.141.part_ref), channel_id=1, source_target_pairs={{0,1},{1,0},{2,3},{3,2},{4,5},{5,4},{6,7},{7,6},{8,9},{9,8},{10,11... | collective-permute-start | bytes 7077896 | tf_op jit(solution)/shard_map/ppermute | solution.py:1260
  112.1 33.6 %collective-permute-start.7 = (bf16[1024,384]{1,0:T(8,128)(2,1)}, bf16[1024,384]{1,0:T(8,128)(2,1)S(1)}, u32[]{:S(2)}, u32[]{:S(2)}) collective-permute-start(bf16[1024,384]{1,0:T(8,128)(2,1)} %dynamic-slice_bitcast_fusion.3), channel_id=1, source_target_pairs={{0,2},{2,0},{4,6},{6,4},{8,10},{10,8},{12,14},{14,12},{16,18},{18,... | collective-permute-start | bytes 2359304 | tf_op jit(solution)/shard_map/ppermute | solution.py:1147
  114.1 1.5 collective-permute-start.6
  129.1 18.2 %all-to-all-start.2 = ((bf16[16,48,128]{2,1,0:T(8,128)(2,1)}), bf16[16,48,128]{2,1,0:T(8,128)(2,1)S(1)}, u32[]{:S(2)}, u32[]{:S(2)}) async-start(bf16[16,48,128]{2,1,0:T(8,128)(2,1)} %get-tuple-element.155), calls=%async_computation.2 | async-start | bytes 393216 | tf_op jit(solution)/shard_map/all_to_all | solution.py:1271
  147.9 15.3 %copy-start.6 = (bf16[2560,384]{1,0:T(8,128)(2,1)S(1)}, bf16[2560,384]{1,0:T(8,128)(2,1)}, u32[]{:S(2)}) copy-start(bf16[2560,384]{1,0:T(8,128)(2,1)} %get-tuple-element.165) | copy-start | bytes 5898244
  157.6 26.5 %all-to-all-start.3 = ((bf16[16,144,128]{2,1,0:T(8,128)(2,1)}), bf16[16,144,128]{2,1,0:T(8,128)(2,1)S(1)}, u32[]{:S(2)}, u32[]{:S(2)}) async-start(bf16[16,144,128]{2,1,0:T(8,128)(2,1)} %heavy_backward.1), calls=%async_computation.3 | async-start | bytes 1179648 | tf_op jit(solution)/shard_map/all_to_all | solution.py:1271
  164.3 40.6 %collective-permute-start.8 = (bf16[1280,384]{1,0:T(8,128)(2,1)}, bf16[1280,384]{1,0:T(8,128)(2,1)S(1)}, u32[]{:S(2)}, u32[]{:S(2)}) collective-permute-start(bf16[1280,384]{1,0:T(8,128)(2,1)} %dynamic-slice_bitcast_fusion), channel_id=1, source_target_pairs={{0,4},{2,6},{4,0},{6,2},{8,12},{10,14},{12,8},{14,10},{16,20},{18,... | collective-permute-start | bytes 2949128 | tf_op jit(solution)/shard_map/ppermute | solution.py:1147
  166.2 39.0 %collective-permute-start.9 = (bf16[2,2,128,384]{3,2,1,0:T(8,128)(2,1)}, bf16[2,2,128,384]{3,2,1,0:T(8,128)(2,1)S(1)}, u32[]{:S(2)}, u32[]{:S(2)}) collective-permute-start(bf16[2,2,128,384]{3,2,1,0:T(8,128)(2,1)} %get-tuple-element.168), channel_id=1, source_target_pairs={{0,2},{2,4},{4,6},{6,8},{8,10},{10,12},{12,14},{14,16},{16,18},{18... | collective-permute-start | bytes 1179656 | tf_op jit(solution)/shard_map/ppermute | solution.py:1267
  169.6 35.6 %collective-permute-start.10 = (bf16[2,2,128,384]{3,2,1,0:T(8,128)(2,1)}, bf16[2,2,128,384]{3,2,1,0:T(8,128)(2,1)S(1)}, u32[]{:S(2)}, u32[]{:S(2)}) collective-permute-start(bf16[2,2,128,384]{3,2,1,0:T(8,128)(2,1)} %get-tuple-element.169), channel_id=1, source_target_pairs={{2,0},{4,2},{6,4},{8,6},{10,8},{12,10},{14,12},{16,14},{18,16},{20... | collective-permute-start | bytes 1179656 | tf_op jit(solution)/shard_map/ppermute | solution.py:1267
  184.9 20.0 %copy-start.7 = (bf16[2560,384]{1,0:T(8,128)(2,1)S(1)}, bf16[2560,384]{1,0:T(8,128)(2,1)}, u32[]{:S(2)}) copy-start(bf16[2560,384]{1,0:T(8,128)(2,1)} %get-tuple-element.165) | copy-start | bytes 5898244
  213.8 24.8 %collective-permute-start.14 = (bf16[2,1536,768]{2,1,0:T(8,128)(2,1)}, bf16[2,1536,768]{2,1,0:T(8,128)(2,1)}, u32[]{:S(2)}, u32[]{:S(2)}) collective-permute-start(bf16[2,1536,768]{2,1,0:T(8,128)(2,1)} %all-gather.2.cloned.1.call-done), channel_id=1, source_target_pairs={{0,1},{1,0},{2,3},{3,2},{4,5},{5,4},{6,7},{7,6},{8,9},{9,8},{10,11... | collective-permute-start | bytes 14155784 | tf_op jit(solution)/shard_map/ppermute | solution.py:1260
  213.9 10.8 %collective-permute-start.11 = (bf16[2,384,768]{2,1,0:T(8,128)(2,1)}, bf16[2,384,768]{2,1,0:T(8,128)(2,1)}, u32[]{:S(2)}, u32[]{:S(2)}) collective-permute-start(bf16[2,384,768]{2,1,0:T(8,128)(2,1)} %get-tuple-element.172.part_ref), channel_id=1, source_target_pairs={{0,1},{1,0},{2,3},{3,2},{4,5},{5,4},{6,7},{7,6},{8,9},{9,8},{10,11... | collective-permute-start | bytes 3538952 | tf_op jit(solution)/shard_map/ppermute | solution.py:1260
  215.2 15.7 %collective-permute-start.17 = (bf16[640,384]{1,0:T(8,128)(2,1)}, bf16[640,384]{1,0:T(8,128)(2,1)}, u32[]{:S(2)}, u32[]{:S(2)}) collective-permute-start(bf16[640,384]{1,0:T(8,128)(2,1)} %dynamic-slice_bitcast_fusion.4), channel_id=1, source_target_pairs={{0,2},{2,0},{4,6},{6,4},{8,10},{10,8},{12,14},{14,12},{16,18},{18,... | collective-permute-start | bytes 1474568 | tf_op jit(solution)/shard_map/ppermute | solution.py:1147
  219.5 12.3 %collective-permute-start.16 = (bf16[512,384]{1,0:T(8,128)(2,1)}, bf16[512,384]{1,0:T(8,128)(2,1)}, u32[]{:S(2)}, u32[]{:S(2)}) collective-permute-start(bf16[512,384]{1,0:T(8,128)(2,1)} %dynamic-slice_bitcast_fusion.9), channel_id=1, source_target_pairs={{0,4},{2,6},{4,0},{6,2},{8,12},{10,14},{12,8},{14,10},{16,20},{18,... | collective-permute-start | bytes 1179656 | tf_op jit(solution)/shard_map/ppermute | solution.py:1147
  220.1 2.2 collective-permute-start.12
  222.3 40.0 %collective-permute-start.19 = (bf16[1152,384]{1,0:T(8,128)(2,1)}, bf16[1152,384]{1,0:T(8,128)(2,1)S(1)}, u32[]{:S(2)}, u32[]{:S(2)}) collective-permute-start(bf16[1152,384]{1,0:T(8,128)(2,1)} %dynamic-slice_bitcast_fusion.1), channel_id=1, source_target_pairs={{0,4},{2,6},{4,0},{6,2},{8,12},{10,14},{12,8},{14,10},{16,20},{18,... | collective-permute-start | bytes 2654216 | tf_op jit(solution)/shard_map/ppermute | solution.py:1147
  234.4 27.9 %collective-permute-start.18 = (bf16[576,384]{1,0:T(8,128)(2,1)S(1)}, bf16[576,384]{1,0:T(8,128)(2,1)S(1)}, u32[]{:S(2)}, u32[]{:S(2)}) collective-permute-start(bf16[576,384]{1,0:T(8,128)(2,1)S(1)} %dynamic-slice_bitcast_fusion.7), channel_id=1, source_target_pairs={{0,8},{2,10},{4,12},{6,14},{8,0},{10,2},{12,4},{14,6},{16,24},{18,... | collective-permute-start | bytes 1327112 | tf_op jit(solution)/shard_map/ppermute | solution.py:1147
  236.5 29.4 %collective-permute-start.13 = (bf16[1152,384]{1,0:T(8,128)(2,1)S(1)}, bf16[1152,384]{1,0:T(8,128)(2,1)}, u32[]{:S(2)}, u32[]{:S(2)}) collective-permute-start(bf16[1152,384]{1,0:T(8,128)(2,1)S(1)} %dynamic-slice_bitcast_fusion.2), channel_id=1, source_target_pairs={{0,2},{2,0},{4,6},{6,4},{8,10},{10,8},{12,14},{14,12},{16,18},{18,... | collective-permute-start | bytes 2654216 | tf_op jit(solution)/shard_map/ppermute | solution.py:1147
  238.0 24.2 %collective-permute-start.20 = (bf16[64,384]{1,0:T(8,128)(2,1)}, bf16[64,384]{1,0:T(8,128)(2,1)}, u32[]{:S(2)}, u32[]{:S(2)}) collective-permute-start(bf16[64,384]{1,0:T(8,128)(2,1)} %get-tuple-element.190), channel_id=1, source_target_pairs={{0,4},{2,6},{4,0},{6,2},{8,12},{10,14},{12,8},{14,10},{16,20},{18,... | collective-permute-start | bytes 147464 | tf_op jit(solution)/shard_map/ppermute | solution.py:1389
  267.4 21.1 %collective-permute-start.22 = (bf16[64,384]{1,0:T(8,128)(2,1)}, bf16[64,384]{1,0:T(8,128)(2,1)}, u32[]{:S(2)}, u32[]{:S(2)}) collective-permute-start(bf16[64,384]{1,0:T(8,128)(2,1)} %add_convert_fusion.1), channel_id=1, source_target_pairs={{0,2},{2,0},{4,6},{6,4},{8,10},{10,8},{12,14},{14,12},{16,18},{18,... | collective-permute-start | bytes 147464 | tf_op jit(solution)/shard_map/ppermute | solution.py:1405
  268.2 21.2 %collective-permute-start.21 = (bf16[576,384]{1,0:T(8,128)(2,1)S(1)}, bf16[576,384]{1,0:T(8,128)(2,1)S(1)}, u32[]{:S(2)}, u32[]{:S(2)}) collective-permute-start(bf16[576,384]{1,0:T(8,128)(2,1)S(1)} %dynamic-slice_bitcast_fusion.6), channel_id=1, source_target_pairs={{0,2},{2,0},{4,6},{6,4},{8,10},{10,8},{12,14},{14,12},{16,18},{18,... | collective-permute-start | bytes 1327112 | tf_op jit(solution)/shard_map/ppermute | solution.py:1147
  270.4 18.9 %collective-permute-start.24 = (bf16[288,384]{1,0:T(8,128)(2,1)}, bf16[288,384]{1,0:T(8,128)(2,1)}, u32[]{:S(2)}, u32[]{:S(2)}) collective-permute-start(bf16[288,384]{1,0:T(8,128)(2,1)} %dynamic-slice_bitcast_fusion.11), channel_id=1, source_target_pairs={{0,16},{2,18},{4,20},{6,22},{8,24},{10,26},{12,28},{14,30},{16,0},... | collective-permute-start | bytes 663560 | tf_op jit(solution)/shard_map/ppermute | solution.py:1147
  272.7 16.8 %collective-permute-start.15 = (bf16[576,384]{1,0:T(8,128)(2,1)S(1)}, bf16[576,384]{1,0:T(8,128)(2,1)S(1)}, u32[]{:S(2)}, u32[]{:S(2)}) collective-permute-start(bf16[576,384]{1,0:T(8,128)(2,1)S(1)} %dynamic-slice_bitcast_fusion.8), channel_id=1, source_target_pairs={{0,4},{2,6},{4,0},{6,2},{8,12},{10,14},{12,8},{14,10},{16,20},{18,... | collective-permute-start | bytes 1327112 | tf_op jit(solution)/shard_map/ppermute | solution.py:1147
  289.8 18.2 %collective-permute-start.23 = (bf16[608,384]{1,0:T(8,128)(2,1)S(1)}, bf16[608,384]{1,0:T(8,128)(2,1)S(1)}, u32[]{:S(2)}, u32[]{:S(2)}) collective-permute-start(bf16[608,384]{1,0:T(8,128)(2,1)S(1)} %dynamic-slice_bitcast_fusion.5), channel_id=1, source_target_pairs={{0,8},{2,10},{4,12},{6,14},{8,0},{10,2},{12,4},{14,6},{16,24},{18,... | collective-permute-start | bytes 1400840 | tf_op jit(solution)/shard_map/ppermute | solution.py:1147
  291.4 14.8 %collective-permute-start.26 = (bf16[288,384]{1,0:T(8,128)(2,1)S(1)}, bf16[288,384]{1,0:T(8,128)(2,1)S(1)}, u32[]{:S(2)}, u32[]{:S(2)}) collective-permute-start(bf16[288,384]{1,0:T(8,128)(2,1)S(1)} %fusion.11), channel_id=1, source_target_pairs={{0,16},{2,18},{4,20},{6,22},{8,24},{10,26},{12,28},{14,30},{16,0},... | collective-permute-start | bytes 663560 | tf_op jit(solution)/shard_map/ppermute | solution.py:1157
  306.4 18.7 %collective-permute-start.28 = (bf16[576,384]{1,0:T(8,128)(2,1)S(1)}, bf16[576,384]{1,0:T(8,128)(2,1)S(1)}, u32[]{:S(2)}, u32[]{:S(2)}) collective-permute-start(bf16[576,384]{1,0:T(8,128)(2,1)S(1)} %maximum_select_fusion.7), channel_id=1, source_target_pairs={{0,8},{2,10},{4,12},{6,14},{8,0},{10,2},{12,4},{14,6},{16,24},{18,... | collective-permute-start | bytes 1327112 | tf_op jit(solution)/shard_map/ppermute | solution.py:1157
  308.1 17.0 %collective-permute-start.25 = (bf16[304,384]{1,0:T(8,128)(2,1)S(1)}, bf16[304,384]{1,0:T(8,128)(2,1)S(1)}, u32[]{:S(2)}, u32[]{:S(2)}) collective-permute-start(bf16[304,384]{1,0:T(8,128)(2,1)S(1)} %dynamic-slice_bitcast_fusion.10), channel_id=1, source_target_pairs={{0,16},{2,18},{4,20},{6,22},{8,24},{10,26},{12,28},{14,30},{16,0},... | collective-permute-start | bytes 700424 | tf_op jit(solution)/shard_map/ppermute | solution.py:1147
  325.2 16.5 %collective-permute-start.27 = (bf16[304,384]{1,0:T(8,128)(2,1)S(1)}, bf16[304,384]{1,0:T(8,128)(2,1)S(1)}, u32[]{:S(2)}, u32[]{:S(2)}) collective-permute-start(bf16[304,384]{1,0:T(8,128)(2,1)S(1)} %fusion.10), channel_id=1, source_target_pairs={{0,16},{2,18},{4,20},{6,22},{8,24},{10,26},{12,28},{14,30},{16,0},... | collective-permute-start | bytes 700424 | tf_op jit(solution)/shard_map/ppermute | solution.py:1157
  326.2 16.1 %collective-permute-start.30 = (bf16[512,384]{1,0:T(8,128)(2,1)S(1)}, bf16[512,384]{1,0:T(8,128)(2,1)S(1)}, u32[]{:S(2)}, u32[]{:S(2)}) collective-permute-start(bf16[512,384]{1,0:T(8,128)(2,1)S(1)} %bitcast.193), channel_id=1, source_target_pairs={{0,4},{2,6},{4,0},{6,2},{8,12},{10,14},{12,8},{14,10},{16,20},{18,... | collective-permute-start | bytes 1179656 | tf_op jit(solution)/shard_map/ppermute | solution.py:1157
  326.8 17.5 %collective-permute-start.31 = (bf16[640,384]{1,0:T(8,128)(2,1)S(1)}, bf16[640,384]{1,0:T(8,128)(2,1)S(1)}, u32[]{:S(2)}, u32[]{:S(2)}) collective-permute-start(bf16[640,384]{1,0:T(8,128)(2,1)S(1)} %bitcast.175), channel_id=1, source_target_pairs={{0,2},{2,0},{4,6},{6,4},{8,10},{10,8},{12,14},{14,12},{16,18},{18,... | collective-permute-start | bytes 1474568 | tf_op jit(solution)/shard_map/ppermute | solution.py:1157
  341.9 18.5 %collective-permute-start.29 = (bf16[608,384]{1,0:T(8,128)(2,1)S(1)}, bf16[608,384]{1,0:T(8,128)(2,1)}, u32[]{:S(2)}, u32[]{:S(2)}) collective-permute-start(bf16[608,384]{1,0:T(8,128)(2,1)S(1)} %maximum_select_fusion.6), channel_id=1, source_target_pairs={{0,8},{2,10},{4,12},{6,14},{8,0},{10,2},{12,4},{14,6},{16,24},{18,... | collective-permute-start | bytes 1400840 | tf_op jit(solution)/shard_map/ppermute | solution.py:1157
  342.6 17.8 %copy-start.2 = (bf16[1024,384]{1,0:T(8,128)(2,1)}, bf16[1024,384]{1,0:T(8,128)(2,1)S(1)}, u32[]{:S(2)}) copy-start(bf16[1024,384]{1,0:T(8,128)(2,1)S(1)} %maximum_select_fusion.5.mine_ref) | copy-start | bytes 2359300
  342.6 20.2 %collective-permute-start.33 = (bf16[1024,384]{1,0:T(8,128)(2,1)S(1)}, bf16[1024,384]{1,0:T(8,128)(2,1)}, u32[]{:S(2)}, u32[]{:S(2)}) collective-permute-start(bf16[1024,384]{1,0:T(8,128)(2,1)S(1)} %maximum_select_fusion.5.mine_ref), channel_id=1, source_target_pairs={{0,2},{2,0},{4,6},{6,4},{8,10},{10,8},{12,14},{14,12},{16,18},{18,... | collective-permute-start | bytes 2359304 | tf_op jit(solution)/shard_map/ppermute | solution.py:1434
  344.7 15.7 %copy-start.1 = (bf16[1280,384]{1,0:T(8,128)(2,1)}, bf16[1280,384]{1,0:T(8,128)(2,1)S(1)}, u32[]{:S(2)}) copy-start(bf16[1280,384]{1,0:T(8,128)(2,1)S(1)} %maximum_select_fusion.mine_ref) | copy-start | bytes 2949124
  344.7 23.5 %collective-permute-start.34 = (bf16[1280,384]{1,0:T(8,128)(2,1)S(1)}, bf16[1280,384]{1,0:T(8,128)(2,1)S(1)}, u32[]{:S(2)}, u32[]{:S(2)}) collective-permute-start(bf16[1280,384]{1,0:T(8,128)(2,1)S(1)} %maximum_select_fusion.mine_ref), channel_id=1, source_target_pairs={{0,4},{2,6},{4,0},{6,2},{8,12},{10,14},{12,8},{14,10},{16,20},{18,... | collective-permute-start | bytes 2949128 | tf_op jit(solution)/shard_map/ppermute | solution.py:1434
  361.9 10.9 %collective-permute-start.36 = (bf16[576,384]{1,0:T(8,128)(2,1)S(1)}, bf16[576,384]{1,0:T(8,128)(2,1)S(1)}, u32[]{:S(2)}, u32[]{:S(2)}) collective-permute-start(bf16[576,384]{1,0:T(8,128)(2,1)S(1)} %bitcast.184), channel_id=1, source_target_pairs={{0,2},{2,0},{4,6},{6,4},{8,10},{10,8},{12,14},{14,12},{16,18},{18,... | collective-permute-start | bytes 1327112 | tf_op jit(solution)/shard_map/ppermute | solution.py:1157
  362.2 11.6 %collective-permute-start.32 = (bf16[576,384]{1,0:T(8,128)(2,1)S(1)}, bf16[576,384]{1,0:T(8,128)(2,1)S(1)}, u32[]{:S(2)}, u32[]{:S(2)}) collective-permute-start(bf16[576,384]{1,0:T(8,128)(2,1)S(1)} %bitcast.186), channel_id=1, source_target_pairs={{0,4},{2,6},{4,0},{6,2},{8,12},{10,14},{12,8},{14,10},{16,20},{18,... | collective-permute-start | bytes 1327112 | tf_op jit(solution)/shard_map/ppermute | solution.py:1157
  374.1 18.2 %collective-permute-start.35 = (bf16[1152,384]{1,0:T(8,128)(2,1)S(1)}, bf16[1152,384]{1,0:T(8,128)(2,1)S(1)}, u32[]{:S(2)}, u32[]{:S(2)}) collective-permute-start(bf16[1152,384]{1,0:T(8,128)(2,1)S(1)} %maximum_select_fusion.3.mine_ref), channel_id=1, source_target_pairs={{0,2},{2,0},{4,6},{6,4},{8,10},{10,8},{12,14},{14,12},{16,18},{18,... | collective-permute-start | bytes 2654216 | tf_op jit(solution)/shard_map/ppermute | solution.py:1450
  375.4 18.5 %collective-permute-start.37 = (bf16[1152,384]{1,0:T(8,128)(2,1)S(1)}, bf16[1152,384]{1,0:T(8,128)(2,1)S(1)}, u32[]{:S(2)}, u32[]{:S(2)}) collective-permute-start(bf16[1152,384]{1,0:T(8,128)(2,1)S(1)} %maximum_select_fusion.4.mine_ref), channel_id=1, source_target_pairs={{0,4},{2,6},{4,0},{6,2},{8,12},{10,14},{12,8},{14,10},{16,20},{18,... | collective-permute-start | bytes 2654216 | tf_op jit(solution)/shard_map/ppermute | solution.py:1450
  (17 other events, 37.7 us)
Sparse Core Ops, SparseCore 0:
  89.4 108.7 all-gather.1
